TPU v7x, 768 devices: a whole 4x8x12 slice. The times are simulated.
768 devices in a mesh: pair: 64 (over x, y, core), virt: 12 (over z).
Axes of the slice: x: 4, y: 8, z: 12, core: 2. Of those that a mesh axis runs over, the one named last changes fastest.
Arguments:
- amplitudes: float32 [64, 12288, 256], P('pair', 'virt'), may hold values from -4 to 4
- source: float32 [64, 12288, 256], P('pair', 'virt'), may hold values from -12 to 12
- diag_block: float32 [12288, 1024], P('virt'), may hold values from -0.1875 to 0.1875
- edge_low: float32 [3072, 256], P('virt'), may hold values from -0.375 to 0.375
- edge_high: float32 [3072, 256], P('virt'), may hold values from -0.375 to 0.375
- hole_coupling: float32 [64, 64], replicated, may hold values from -0.75 to 0.75
- pair_energy: float32 [64], replicated, may hold values from -3 to -1
- virt_energy: float32 [12288], replicated, may hold values from 1 to 4
- column_tiles: int32 [2], replicated, may hold values from 0 to 95, as said below
Outputs:
- updated: float32 [64, 12288, 256], P('pair', 'virt')
Inputs may be any that keep to these rules, and one draw needn't show every extreme that they name: `column_tiles`: 2 distinct tile numbers; the last entry is always the highest tile, 95.
All inputs are finite; a program needn't handle non-finite values.
Results may differ from a plain program's by a relative error of at most 0.0003.
Values sent between devices are 32-bit elements; how exact they have to be, the bound alone decides.
No kernel may reach another device: no remote copies, remote signals or barrier semaphores. Data moves between devices by JAX's collectives and lax.ppermute only.
A program may use at most 64 MiB of HBM per device.

v0:
```python
import jax
import jax.numpy as jnp
from jax import lax
from jax.sharding import PartitionSpec as P

TW = 128
ITERS = 2


def with_halo(x, sides, width):
    for axis, dim in sides:
        count, length = (lax.axis_size(axis), x.shape[dim])
        up = [(i, (i + 1) % count) for i in range(count - 1)]
        down = [(j, i) for i, j in up]
        last = lax.slice_in_dim(x, length - width, length, axis=dim)
        first = lax.slice_in_dim(x, 0, width, axis=dim)
        before = lax.ppermute(last, axis, up)
        after = lax.ppermute(first, axis, down)
        x = jnp.concatenate([before, x, after], axis=dim)
    return x


def couple_rows(diag_block, edge_low, edge_high, field, padded):
    exact = lax.Precision.HIGHEST
    rows = field.shape[1]
    width = edge_low.shape[0]
    out = jnp.einsum("rc,pcn->prn", diag_block, field, precision=exact)
    lower = jnp.einsum("rc,pcn->prn", edge_low, padded[:, :width], precision=exact)
    upper = jnp.einsum("rc,pcn->prn", edge_high, padded[:, rows + width :], precision=exact)
    out = out.at[:, :width].add(lower)
    return out.at[:, rows - width :].add(upper)


def column_energy(virt_energy, column_tiles):
    index = (column_tiles[:, None] * TW + jnp.arange(TW, dtype=jnp.int32)[None, :]).reshape(-1)
    return virt_energy[index]


def local(
    amplitudes,
    source,
    diag_block,
    edge_low,
    edge_high,
    hole_coupling,
    pair_energy,
    virt_energy,
    column_tiles,
):
    exact = lax.Precision.HIGHEST
    rows = amplitudes.shape[1]
    width = edge_low.shape[0]
    row_energy = lax.dynamic_slice_in_dim(virt_energy, lax.axis_index("virt") * rows, rows)
    kept_energy = column_energy(virt_energy, column_tiles)
    count = amplitudes.shape[0]
    own_energy = lax.dynamic_slice_in_dim(pair_energy, lax.axis_index("pair") * count, count)
    denom = row_energy[None, :, None] + kept_energy[None, None, :] - own_energy[:, None, None]
    field = amplitudes
    for step in range(ITERS):
        padded = with_halo(field, (("virt", 1),), width)
        banded = couple_rows(diag_block, edge_low, edge_high, field, padded)
        mixed = jnp.einsum(
            "pq,qrn->prn",
            hole_coupling,
            lax.all_to_all(field, "pair", split_axis=1, concat_axis=0, tiled=True),
            precision=exact,
        )
        hole = lax.all_to_all(mixed, "pair", split_axis=0, concat_axis=1, tiled=True)
        field = (source + banded + hole) / denom
    return field


def solution(mesh):
    in_specs = (
        P("pair", "virt", None),
        P("pair", "virt", None),
        P("virt", None),
        P("virt", None),
        P("virt", None),
        P(),
        P(),
        P(),
        P(),
    )
    out_specs = P("pair", "virt", None)
    return jax.shard_map(local, mesh=mesh, in_specs=in_specs, out_specs=out_specs, check_vma=False)
```

profile of v0, /device:TPU:1, one launch (start us, length us, event | category | flops | bytes accessed | tf_op | source)
XLA Modules:
  0.0 165.7 jit_solution(5110479764321195598)
XLA Ops:
  0.0 0.0 copy-start
  0.0 2.4 %copy.27 = f32[1,1024,256]{2,0,1:T(1,128)S(1)} copy(f32[1,1024,256]{2,1,0:T(8,128)} %param.17) | data formatting | bytes 2097152 | tf_op args[0]
  2.4 42.3 %all_to_all.48 = f32[1,1024,256]{2,0,1:T(1,128)S(1)} all-to-all(f32[1,1024,256]{2,0,1:T(1,128)S(1)} %copy.27), channel_id=1, replica_groups=mesh['pair'=64,'virt'=12] {'pair'}, dimensions={1} | all-to-all | bytes 2097152 | tf_op jit(solution)/shard_map/all_to_all | solution.py:65
  44.7 0.1 copy.37
  44.8 0.0 copy-start.5
  44.8 0.0 copy-done.4
  44.8 1.6 fusion.9
  46.4 1.6 copy.29
  48.0 6.5 %all-to-all-start.1 = ((f32[64,16,256]{2,1,0:T(8,128)}), f32[64,16,256]{2,1,0:T(8,128)}, u32[]{:S(2)}, u32[]{:S(2)}) async-start(f32[64,16,256]{2,1,0:T(8,128)} %copy.29), calls=%async_computation.1 | async-start | bytes 2097152 | tf_op jit(solution)/shard_map/all_to_all | solution.py:68
  54.5 0.0 copy-done.2
  54.5 0.0 copy-start.1
  54.5 0.9 fusion.25
  55.3 1.3 collective-permute-start.1
  56.6 4.7 %collective-permute-start = (f32[1,256,256]{2,1,0:T(8,128)}, f32[1,256,256]{2,1,0:T(8,128)}, u32[]{:S(2)}, u32[]{:S(2)}) collective-permute-start(f32[1,256,256]{2,1,0:T(8,128)} %get-tuple-element.56), channel_id=1, source_target_pairs={{0,1},{1,2},{2,3},{3,4},{4,5},{5,6},{6,7},{7,8},{8,9},{9,10},{10,1... | collective-permute-start | bytes 786440 | tf_op jit(solution)/shard_map/ppermute | solution.py:17
  61.4 0.0 copy-done.5
  61.4 0.1 iota_add_fusion
  61.5 8.7 %fusion.6 = f32[256,1024]{1,0:T(8,128)S(1)} fusion(f32[1024,1024]{1,0:T(8,128)} %param.19, f32[1,1024,256]{2,1,0:T(8,128)S(1)} %copy-done.2), kind=kOutput, calls=%fused_computation.12 | convolution fusion | flops 3221225472 | bytes 6291456 | tf_op jit(solution)/shard_map/rc,pcn->prn/dot_general | solution.py:27
  70.2 0.0 copy-start.6
  70.2 1.7 %gather_fusion = f32[256]{0:T(256)S(1)} fusion(f32[12288]{0:T(1024)S(1)} %copy-done.1, s32[1024]{0:T(1024)S(1)} %pad_clamp_fusion), kind=kCustom, calls=%fused_computation | custom fusion | bytes 3072 | tf_op jit(solution)/shard_map/gather | solution.py:36
  72.0 1.6 copy.31
  73.6 0.1 copy.43
  73.7 0.6 dynamic_slice.7
  74.3 0.0 collective-permute-done
  74.3 1.5 fusion.3
  75.8 0.0 collective-permute-done.1
  75.8 1.6 fusion.13
  77.5 5.5 %all-to-all-done.1 = f32[64,16,256]{2,1,0:T(8,128)} async-done(((f32[64,16,256]{2,1,0:T(8,128)}), f32[64,16,256]{2,1,0:T(8,128)}, u32[]{:S(2)}, u32[]{:S(2)}) %all-to-all-start.1) | async-done | bytes 1048608 | tf_op jit(solution)/shard_map/all_to_all | solution.py:68
  82.9 2.5 %copy.30 = f32[1,1024,256]{1,2,0:T(8,128)} copy(f32[1,1024,256]{2,1,0:T(8,128)} %bitcast.10) | data formatting | bytes 2097152 | tf_op jit(solution)/shard_map/all_to_all | solution.py:68
  85.5 2.1 %fusion.11 = f32[1,1024,256]{1,2,0:T(8,128)S(1)} fusion(f32[1,1024,256]{1,2,0:T(8,128)} %copy.30, f32[1,1024,256]{1,2,0:T(8,128)S(1)} %copy.31, f32[1,1024,256]{1,2,0:T(8,128)S(1)} %fusion.13, f32[]{:T(128)} %bitcast.13, f32[256]{0:T(256)S(1)} %gather_fusion, f32[1024]{0:T(1024)S(1)} %dynamic_slice.6), kind=kLoop, calls=%fused_computation.19 | loop fusion | flops 1310720 | bytes 4199428 | tf_op jit(solution)/shard_map/div | solution.py:69
  87.6 0.8 copy.32
  88.4 34.5 %all_to_all.49 = f32[1,1024,256]{2,0,1:T(1,128)S(1)} all-to-all(f32[1,1024,256]{2,0,1:T(1,128)S(1)} %copy.32), channel_id=1, replica_groups=mesh['pair'=64,'virt'=12] {'pair'}, dimensions={1} | all-to-all | bytes 2097152 | tf_op jit(solution)/shard_map/all_to_all | solution.py:65
  122.9 0.1 copy.38
  123.0 1.7 %convolution_bitcast_fusion = f32[64,16,256]{2,0,1:T(8,128)S(1)} fusion(f32[64,16,256]{2,1,0:T(8,128)S(1)} %bitcast.76, f32[64,64]{1,0:T(8,128)S(1)} %copy-done.4), kind=kOutput, calls=%fused_computation.1 | convolution fusion | flops 201326592 | bytes 2113536 | tf_op jit(solution)/shard_map/pq,qrn->prn/dot_general | solution.py:62
  124.7 1.6 copy.34
  126.3 6.2 %all-to-all-start.3 = ((f32[64,16,256]{2,1,0:T(8,128)}), f32[64,16,256]{2,1,0:T(8,128)S(1)}, u32[]{:S(2)}, u32[]{:S(2)}) async-start(f32[64,16,256]{2,1,0:T(8,128)} %copy.34), calls=%async_computation.3 | async-start | bytes 2097152 | tf_op jit(solution)/shard_map/all_to_all | solution.py:68
  132.5 1.3 collective-permute-start.3
  133.8 0.0 copy-start.3
  133.8 4.4 %collective-permute-start.2 = (f32[1,256,256]{1,2,0:T(8,128)S(1)}, f32[1,256,256]{1,2,0:T(8,128)S(1)}, u32[]{:S(2)}, u32[]{:S(2)}) collective-permute-start(f32[1,256,256]{1,2,0:T(8,128)S(1)} %get-tuple-element.54), channel_id=1, source_target_pairs={{0,1},{1,2},{2,3},{3,4},{4,5},{5,6},{6,7},{7,8},{8,9},{9,10},{10,1... | collective-permute-start | bytes 786440 | tf_op jit(solution)/shard_map/ppermute | solution.py:17
  138.2 5.7 %fusion.4 = f32[256,1024]{1,0:T(8,128)S(1)} fusion(f32[1024,1024]{1,0:T(8,128)} %param.19, f32[1,1024,256]{1,2,0:T(8,128)S(1)} %fusion.11), kind=kOutput, calls=%fused_computation.10 | convolution fusion | flops 3221225472 | bytes 6291456 | tf_op jit(solution)/shard_map/rc,pcn->prn/dot_general | solution.py:27
  143.9 0.1 copy.45
  144.0 0.0 collective-permute-done.2
  144.0 0.4 fusion.1
  144.4 0.0 collective-permute-done.3
  144.4 0.5 fusion.12
  144.9 16.1 %all-to-all-done.3 = f32[64,16,256]{2,1,0:T(8,128)S(1)} async-done(((f32[64,16,256]{2,1,0:T(8,128)}), f32[64,16,256]{2,1,0:T(8,128)S(1)}, u32[]{:S(2)}, u32[]{:S(2)}) %all-to-all-start.3) | async-done | bytes 1048608 | tf_op jit(solution)/shard_map/all_to_all | solution.py:68
  161.0 1.3 copy.35
  162.3 2.1 %add_divide_fusion = f32[1,1024,256]{1,2,0:T(8,128)S(1)} fusion(f32[1,1024,256]{1,2,0:T(8,128)} %copy.35, f32[1,1024,256]{1,2,0:T(8,128)S(1)} %copy.31, f32[1,1024,256]{1,2,0:T(8,128)S(1)} %fusion.12, f32[]{:T(128)} %bitcast.13, f32[256]{0:T(256)S(1)} %gather_fusion, f32[1024]{0:T(1024)S(1)} %dynamic_slice.6), kind=kLoop, calls=%fused_computation.17 | loop fusion | flops 1310720 | bytes 4199428 | tf_op jit(solution)/shard_map/div | solution.py:69
  164.4 1.3 copy.36
  (11 shorter events, 0.1 us)
Async XLA Ops:
  0.0 74.3 %copy-start = (f32[256,256]{1,0:T(8,128)S(1)}, f32[256,256]{1,0:T(8,128)}, u32[]{:S(2)}) copy-start(f32[256,256]{1,0:T(8,128)} %param.20) | copy-start | bytes 786436
  0.0 44.8 %copy-start.4 = (f32[64,64]{1,0:T(8,128)S(1)}, f32[64,64]{1,0:T(8,128)}, u32[]{:S(2)}) copy-start(f32[64,64]{1,0:T(8,128)} %param.22) | copy-start | bytes 49156
  44.7 9.8 %copy-start.2 = (f32[1,1024,256]{2,1,0:T(8,128)S(1)}, f32[1,1024,256]{2,1,0:T(8,128)}, u32[]{:S(2)}) copy-start(f32[1,1024,256]{2,1,0:T(8,128)} %param.17) | copy-start | bytes 3145732
  44.8 16.6 %copy-start.5 = (s32[2]{0:T(128)S(1)}, s32[2]{0:T(128)}, u32[]{:S(2)}) copy-start(s32[2]{0:T(128)} %param.25) | copy-start | bytes 28
  48.0 34.9 %all-to-all-start.1 = ((f32[64,16,256]{2,1,0:T(8,128)}), f32[64,16,256]{2,1,0:T(8,128)}, u32[]{:S(2)}, u32[]{:S(2)}) async-start(f32[64,16,256]{2,1,0:T(8,128)} %copy.29), calls=%async_computation.1 | async-start | bytes 2097152 | tf_op jit(solution)/shard_map/all_to_all | solution.py:68
  54.5 15.8 %copy-start.1 = (f32[12288]{0:T(1024)S(1)}, f32[12288]{0:T(1024)}, u32[]{:S(2)}) copy-start(f32[12288]{0:T(1024)} %param.24) | copy-start | bytes 147460
  55.3 20.5 %collective-permute-start.1 = (f32[1,256,256]{2,1,0:T(8,128)}, f32[1,256,256]{2,1,0:T(8,128)}, u32[]{:S(2)}, u32[]{:S(2)}) collective-permute-start(f32[1,256,256]{2,1,0:T(8,128)} %get-tuple-element.55), channel_id=1, source_target_pairs={{1,0},{2,1},{3,2},{4,3},{5,4},{6,5},{7,6},{8,7},{9,8},{10,9},{11,1... | collective-permute-start | bytes 786440 | tf_op jit(solution)/shard_map/ppermute | solution.py:18
  56.6 17.6 %collective-permute-start = (f32[1,256,256]{2,1,0:T(8,128)}, f32[1,256,256]{2,1,0:T(8,128)}, u32[]{:S(2)}, u32[]{:S(2)}) collective-permute-start(f32[1,256,256]{2,1,0:T(8,128)} %get-tuple-element.56), channel_id=1, source_target_pairs={{0,1},{1,2},{2,3},{3,4},{4,5},{5,6},{6,7},{7,8},{8,9},{9,10},{10,1... | collective-permute-start | bytes 786440 | tf_op jit(solution)/shard_map/ppermute | solution.py:17
  70.2 3.5 %copy-start.6 = (f32[64]{0:T(128)S(1)}, f32[64]{0:T(128)}, u32[]{:S(2)}) copy-start(f32[64]{0:T(128)} %param.23) | copy-start | bytes 772
  126.3 34.8 %all-to-all-start.3 = ((f32[64,16,256]{2,1,0:T(8,128)}), f32[64,16,256]{2,1,0:T(8,128)S(1)}, u32[]{:S(2)}, u32[]{:S(2)}) async-start(f32[64,16,256]{2,1,0:T(8,128)} %copy.34), calls=%async_computation.3 | async-start | bytes 2097152 | tf_op jit(solution)/shard_map/all_to_all | solution.py:68
  132.5 11.9 %collective-permute-start.3 = (f32[1,256,256]{1,2,0:T(8,128)S(1)}, f32[1,256,256]{1,2,0:T(8,128)S(1)}, u32[]{:S(2)}, u32[]{:S(2)}) collective-permute-start(f32[1,256,256]{1,2,0:T(8,128)S(1)} %get-tuple-element.53), channel_id=1, source_target_pairs={{1,0},{2,1},{3,2},{4,3},{5,4},{6,5},{7,6},{8,7},{9,8},{10,9},{11,1... | collective-permute-start | bytes 786440 | tf_op jit(solution)/shard_map/ppermute | solution.py:18
  133.8 10.6 %copy-start.3 = (f32[256,256]{1,0:T(8,128)S(1)}, f32[256,256]{1,0:T(8,128)}, u32[]{:S(2)}) copy-start(f32[256,256]{1,0:T(8,128)} %param.21) | copy-start | bytes 786436
  133.8 10.2 %collective-permute-start.2 = (f32[1,256,256]{1,2,0:T(8,128)S(1)}, f32[1,256,256]{1,2,0:T(8,128)S(1)}, u32[]{:S(2)}, u32[]{:S(2)}) collective-permute-start(f32[1,256,256]{1,2,0:T(8,128)S(1)} %get-tuple-element.54), channel_id=1, source_target_pairs={{0,1},{1,2},{2,3},{3,4},{4,5},{5,6},{6,7},{7,8},{8,9},{9,10},{10,1... | collective-permute-start | bytes 786440 | tf_op jit(solution)/shard_map/ppermute | solution.py:17
where the time goes:
time: 166 us
  blocking collectives  76.9 us (46%)
  starting transfers between devices  24.3 us (15%)
  matrix products  21.8 us (13%)
  waiting for transfers between devices  21.6 us (13%)
  local copies, waits for them, and re-layouts  16.6 us (10%)
  other arithmetic  4.27 us (3%)
    all_to_all x2, blocking collectives, local(): lax.all_to_all(field, 'pair', split_axis=1, concat_axis=0, tiled=True)  76.9 us
    all_to_all x2, waiting for transfers between devices, local(): lax.all_to_all(mixed, 'pair', split_axis=0, concat_axis=1, tiled=True)  21.5 us
    dot_general x2, matrix products, couple_rows(): out = jnp.einsum('rc,pcn->prn', diag_block, field, precision=exact)  14.4 us
    all_to_all x2, starting transfers between devices, local(): lax.all_to_all(mixed, 'pair', split_axis=0, concat_axis=1, tiled=True)  12.7 us
    ppermute x2, starting transfers between devices, with_halo(): before = lax.ppermute(last, axis, up)  9.09 us
    unnamed x20, local copies, waits for them, and re-layouts  4.26 us
    div x2, other arithmetic, local(): field = (source + banded + hole) / denom  4.19 us
    all_to_all x2, local copies, waits for them, and re-layouts, local(): lax.all_to_all(mixed, 'pair', split_axis=0, concat_axis=1, tiled=True)  3.84 us
  transfers between devices with their start and end apart: 6, of which 2 were waited for; matrix products, arithmetic and copies ran while one was open for 14% of the time, Pallas kernels for 0%

commit v1 on v0

v1 whole, which is shorter than its diff:
```python
import functools

import jax
import jax.numpy as jnp
from jax import lax
from jax.experimental import pallas as pl
from jax.experimental.pallas import tpu as pltpu
from jax.sharding import PartitionSpec as P

TW = 128
ITERS = 2
BF = jnp.bfloat16
F32 = jnp.float32
VMEM = pl.BlockSpec(memory_space=pltpu.VMEM)
LIMIT = 40 * 1024 * 1024


def split(x):
    hi = x.astype(BF)
    return hi, (x - hi.astype(F32)).astype(BF)


def dot_nt(x, w):
    return lax.dot_general(x, w, (((1,), (1,)), ((), ())), preferred_element_type=F32)


def dot_nn(x, w):
    return jnp.dot(x, w, preferred_element_type=F32)


def three(dot, xh, xl, wh, wl):
    return dot(xh, wh) + (dot(xl, wh) + dot(xh, wl))


def pack_kernel(a_ref, s_ref, o_ref):
    k = pl.program_id(0)
    nk = pl.num_programs(0)
    for t in range(a_ref.shape[1] // TW):
        cols = slice(t * TW, (t + 1) * TW)
        base = t * TW * 2 * nk
        o_ref[pl.ds(base + k, TW, stride=2 * nk), :] = a_ref[:, cols].T
        o_ref[pl.ds(base + nk + k, TW, stride=2 * nk), :] = s_ref[:, cols].T


def pack(a, s):
    rows, cols = a.shape
    nk = rows // TW
    return pl.pallas_call(
        pack_kernel,
        grid=(nk,),
        in_specs=[pl.BlockSpec((TW, cols), lambda k: (k, 0))] * 2,
        out_specs=pl.BlockSpec((cols * 2 * nk, TW), lambda k: (0, 0)),
        out_shape=jax.ShapeDtypeStruct((cols * 2 * nk, TW), F32),
        compiler_params=pltpu.CompilerParams(vmem_limit_bytes=LIMIT),
        name="pack",
    )(a, s)


def unpack_kernel(u_ref, o_ref):
    k = pl.program_id(0)
    nk = pl.num_programs(0)
    for t in range(o_ref.shape[1] // TW):
        base = t * TW * nk
        o_ref[:, t * TW : (t + 1) * TW] = u_ref[pl.ds(base + k, TW, stride=nk), :].T


def unpack(u, rows, cols):
    nk = rows // TW
    return pl.pallas_call(
        unpack_kernel,
        grid=(nk,),
        in_specs=[pl.BlockSpec((cols * nk, TW), lambda k: (0, 0))],
        out_specs=pl.BlockSpec((TW, cols), lambda k: (k, 0)),
        out_shape=jax.ShapeDtypeStruct((rows, cols), F32),
        compiler_params=pltpu.CompilerParams(vmem_limit_bytes=LIMIT),
        name="unpack",
    )(u)


def prep_kernel(share, d_ref, l_ref, dh_ref, dl_ref, kh_ref, kl_ref):
    dh_ref[...], dl_ref[...] = split(d_ref[...])
    pairs = l_ref.shape[0]
    size = pairs * share
    spread = (
        lax.broadcasted_iota(jnp.int32, (size, pairs), 0) // share
        == lax.broadcasted_iota(jnp.int32, (size, pairs), 1)
    ).astype(F32).astype(BF)
    same = (
        lax.broadcasted_iota(jnp.int32, (size, size), 0) % share
        == lax.broadcasted_iota(jnp.int32, (size, size), 1) % share
    )
    for part, ref in zip(split(l_ref[...]), (kh_ref, kl_ref)):
        tall = dot_nn(spread, part).astype(BF)
        wide = dot_nt(tall, spread)
        ref[...] = jnp.where(same, wide, 0.0).astype(BF)


def prep(d, l, share):
    rows = d.shape[0]
    size = l.shape[0] * share
    return pl.pallas_call(
        functools.partial(prep_kernel, share),
        in_specs=[VMEM] * 2,
        out_specs=[VMEM] * 4,
        out_shape=[jax.ShapeDtypeStruct((rows, rows), BF)] * 2
        + [jax.ShapeDtypeStruct((size, size), BF)] * 2,
        compiler_params=pltpu.CompilerParams(vmem_limit_bytes=LIMIT),
        cost_estimate=pl.CostEstimate(
            flops=8 * rows * rows, bytes_accessed=8 * rows * rows, transcendentals=0
        ),
        name="prep",
    )(d, l)


def edges_kernel(nk, p_ref, first_ref, last_ref):
    lines = first_ref.shape[0]
    tiles = first_ref.shape[1] // TW
    for j in range(tiles):
        cols = slice(j * TW, (j + 1) * TW)
        first_ref[:, cols] = p_ref[pl.ds(j, lines, stride=2 * nk), :]
        last_ref[:, cols] = p_ref[pl.ds(nk - tiles + j, lines, stride=2 * nk), :]


def edges(p, nk, width):
    lines = p.shape[0] // (2 * nk)
    return pl.pallas_call(
        functools.partial(edges_kernel, nk),
        in_specs=[VMEM],
        out_specs=[VMEM] * 2,
        out_shape=[jax.ShapeDtypeStruct((lines, width), F32)] * 2,
        compiler_params=pltpu.CompilerParams(vmem_limit_bytes=LIMIT),
        name="edges",
    )(p)


def inner_kernel(nk, packed, *refs):
    if packed:
        p_ref, dh_ref, dl_ref, kh_ref, kl_ref, o_ref, xh_ref, xl_ref = refs
    else:
        f_ref, p_ref, dh_ref, dl_ref, kh_ref, kl_ref, o_ref, xh_ref, xl_ref = refs
    lines = o_ref.shape[0]
    for k in range(nk):
        cols = slice(k * TW, (k + 1) * TW)
        part = p_ref[pl.ds(k, lines, stride=2 * nk), :] if packed else f_ref[:, cols]
        xh_ref[:, cols], xl_ref[:, cols] = split(part)
    kh = kh_ref[...]
    kl = kl_ref[...]
    wide = 2 * TW
    for c in range(nk // 2):
        cols = slice(c * wide, (c + 1) * wide)
        out = three(dot_nt, xh_ref[...], xl_ref[...], dh_ref[cols, :], dl_ref[cols, :])
        out += three(dot_nn, kh, kl, xh_ref[:, cols], xl_ref[:, cols])
        for j in range(2):
            k = 2 * c + j
            o_ref[:, k * TW : (k + 1) * TW] = (
                out[:, j * TW : (j + 1) * TW] + p_ref[pl.ds(nk + k, lines, stride=2 * nk), :]
            )


def inner(field, p, parts, nk):
    lines = p.shape[0] // (2 * nk)
    rows = nk * TW
    packed = field is None
    args = ([] if packed else [field]) + [p, *parts]
    return pl.pallas_call(
        functools.partial(inner_kernel, nk, packed),
        in_specs=[VMEM] * len(args),
        out_specs=VMEM,
        out_shape=jax.ShapeDtypeStruct((lines, rows), F32),
        scratch_shapes=[pltpu.VMEM((lines, rows), BF)] * 2,
        compiler_params=pltpu.CompilerParams(vmem_limit_bytes=LIMIT),
        cost_estimate=pl.CostEstimate(
            flops=6 * lines * rows * (rows + lines),
            bytes_accessed=4 * rows * rows + 16 * lines * rows,
            transcendentals=0,
        ),
        name="inner",
    )(*args)


def finish_kernel(nk, last_step, sum_ref, before_ref, after_ref, low_ref, high_ref, row_ref, col_ref, pair_ref, *outs):
    lines, rows = sum_ref.shape
    width = low_ref.shape[0]
    low = three(dot_nt, *split(before_ref[...]), *split(low_ref[...]))
    high = three(dot_nt, *split(after_ref[...]), *split(high_ref[...]))
    col = col_ref[...]
    pair = pair_ref[...]
    for k in range(nk):
        cols = slice(k * TW, (k + 1) * TW)
        x = sum_ref[:, cols]
        at = k * TW
        if at < width:
            x += low[:, at : at + TW]
        at -= rows - width
        if at >= 0:
            x += high[:, at : at + TW]
        x = x / (row_ref[:, cols] + col - pair)
        if last_step:
            outs[0][pl.ds(k, lines, stride=nk), :] = x
        else:
            outs[0][:, cols] = x
            if k * TW < width:
                outs[1][:, cols] = x
            if at >= 0:
                outs[2][:, at : at + TW] = x


def finish(total, before, after, low, high, energies, nk, last_step):
    lines, rows = total.shape
    width = low.shape[0]
    edge = jax.ShapeDtypeStruct((lines, width), F32)
    if last_step:
        shapes = [jax.ShapeDtypeStruct((lines * nk, TW), F32)]
    else:
        shapes = [jax.ShapeDtypeStruct((lines, rows), F32), edge, edge]
    args = [total, before, after, low, high, *energies]
    return pl.pallas_call(
        functools.partial(finish_kernel, nk, last_step),
        in_specs=[VMEM] * len(args),
        out_specs=[VMEM] * len(shapes),
        out_shape=shapes,
        compiler_params=pltpu.CompilerParams(vmem_limit_bytes=LIMIT),
        name="finish",
    )(*args)


def exchange(first, last):
    count = lax.axis_size("virt")
    up = [(i, i + 1) for i in range(count - 1)]
    down = [(j, i) for i, j in up]
    before = lax.ppermute(last, "virt", up)
    after = lax.ppermute(first, "virt", down)
    return before, after


def local(
    amplitudes,
    source,
    diag_block,
    edge_low,
    edge_high,
    hole_coupling,
    pair_energy,
    virt_energy,
    column_tiles,
):
    rows, cols = amplitudes.shape[1:]
    width = edge_low.shape[0]
    pairs = pair_energy.shape[0]
    share = cols // pairs
    nk = rows // TW

    packed = pack(amplitudes[0], source[0]).reshape(pairs, share * 2 * nk, TW)
    held = lax.all_to_all(packed, "pair", split_axis=0, concat_axis=0, tiled=True)
    held = held.reshape(cols * 2 * nk, TW)

    parts = prep(diag_block, hole_coupling, share)
    row = lax.dynamic_slice_in_dim(virt_energy, lax.axis_index("virt") * rows, rows)[None, :]
    start = lax.axis_index("pair") * share
    tile = lax.dynamic_index_in_dim(column_tiles, start // TW, keepdims=False)
    kept = lax.dynamic_slice_in_dim(virt_energy, tile * TW + start % TW, share)
    col = jnp.broadcast_to(kept[None, :], (pairs, share)).reshape(-1, 1)
    own = jnp.broadcast_to(pair_energy[:, None], (pairs, share)).reshape(-1, 1)
    energies = (row, col, own)

    first, last = edges(held, nk, width)
    field = None
    for step in range(ITERS):
        before, after = exchange(first, last)
        total = inner(field, held, parts, nk)
        out = finish(total, before, after, edge_low, edge_high, energies, nk, step == ITERS - 1)
        if step < ITERS - 1:
            field, first, last = out
    back = lax.all_to_all(
        out[0].reshape(pairs, share * nk, TW), "pair", split_axis=0, concat_axis=0, tiled=True
    )
    return unpack(back.reshape(cols * nk, TW), rows, cols)[None]


def solution(mesh):
    in_specs = (
        P("pair", "virt", None),
        P("pair", "virt", None),
        P("virt", None),
        P("virt", None),
        P("virt", None),
        P(),
        P(),
        P(),
        P(),
    )
    out_specs = P("pair", "virt", None)
    return jax.shard_map(local, mesh=mesh, in_specs=in_specs, out_specs=out_specs, check_vma=False)
```

time: 166 us -> 137 us (0.83)
  blocking collectives: 76.9 us -> 102 us
  matrix products: 21.8 us -> 0 us
  waiting for transfers between devices: 21.6 us -> 5.37 us
  starting transfers between devices: 24.3 us -> 8.73 us
  Pallas kernels: 0 us -> 12 us
  local copies, waits for them, and re-layouts: 16.6 us -> 6.95 us
  other arithmetic: 4.27 us -> 0 us
    all_to_all x2, blocking collectives: 76.9 us -> 102 us  [the longest x1 65.2 us: local(): lax.all_to_all(packed, 'pair', split_axis=0, concat_axis=0, tiled=True)]
    dot_general x8 -> x0, matrix products: 21.8 us -> none  [the longest x2 14.4 us: couple_rows(): out = jnp.einsum('rc,pcn->prn', diag_block, field, precision=exact)]
    all_to_all x2 -> x0, waiting for transfers between devices: 21.5 us -> none  [local(): lax.all_to_all(mixed, 'pair', split_axis=0, concat_axis=1, tiled=True)]
    all_to_all x2 -> x0, starting transfers between devices: 12.7 us -> none  [local(): lax.all_to_all(mixed, 'pair', split_axis=0, concat_axis=1, tiled=True)]
    pallas_call x0 -> x8, Pallas kernels: none -> 12 us  [the longest x2 5.04 us: inner(): pl.pallas_call(functools.partial(inner_kernel, nk, packed), in_specs=[VME...]
    ppermute x4, waiting for transfers between devices: 0.01 us -> 5.37 us  [the longest x2 4.19 us: exchange(): after = lax.ppermute(first, 'virt', down)]
    div x2 -> x0, other arithmetic: 4.19 us -> none  [local(): field = (source + banded + hole) / denom]
    all_to_all x2 -> x0, local copies, waits for them, and re-layouts: 3.84 us -> none  [local(): lax.all_to_all(mixed, 'pair', split_axis=0, concat_axis=1, tiled=True)]
  transfers between devices with their start and end apart: 6 -> 4, of which waited for: 2 -> 2; matrix products, arithmetic and copies ran while one was open for 14% -> 2% of each run, Pallas kernels for 0% -> 5%
where the time goes in v1:
time: 137 us; the launch traced here: 136 us
  blocking collectives  102 us (74%)
  Pallas kernels  12 us (9%)
  starting transfers between devices  8.73 us (6%)
  local copies, waits for them, and re-layouts  6.95 us (5%)
  waiting for transfers between devices  5.37 us (4%)
    all_to_all x1, blocking collectives, local(): lax.all_to_all(packed, 'pair', split_axis=0, concat_axis=0, tiled=True)  65.2 us
    all_to_all x1, blocking collectives, local(): lax.all_to_all(out[0].reshape(pairs, share * nk, TW), 'pair', split_axis=...  36.5 us
    ppermute x2, starting transfers between devices, exchange(): before = lax.ppermute(last, 'virt', up)  6.15 us
    pallas_call x2, Pallas kernels, inner(): pl.pallas_call(functools.partial(inner_kernel, nk, packed), in_specs=[VME...  5.04 us
    unnamed x16, local copies, waits for them, and re-layouts  4.66 us
    ppermute x2, waiting for transfers between devices, exchange(): after = lax.ppermute(first, 'virt', down)  4.19 us
    pallas_call x1, Pallas kernels, unpack(): pl.pallas_call(unpack_kernel, grid=(nk,), in_specs=[pl.BlockSpec((cols *...  3.14 us
  transfers between devices with their start and end apart: 4, of which 2 were waited for; matrix products, arithmetic and copies ran while one was open for 2% of the time, Pallas kernels for 5%

profile of v1, /device:TPU:1, one launch (start us, length us, event | category | flops | bytes accessed | tf_op | source)
XLA Modules:
  0.0 135.6 jit_solution(12520227736846533280)
XLA Ops:
  0.0 0.0 copy-start.1
  0.0 1.2 copy-done.1
  1.2 0.0 copy-start.2
  1.2 1.2 copy-done.2
  2.5 1.2 pack.1
  3.7 65.2 %all_to_all.10 = f32[64,64,128]{2,1,0:T(8,128)S(1)} all-to-all(f32[64,64,128]{2,1,0:T(8,128)S(1)} %bitcast.12), channel_id=1, replica_groups=mesh['pair'=64,'virt'=12] {'pair'}, dimensions={0} | all-to-all | bytes 4194304 | tf_op jit(solution)/shard_map/all_to_all | solution.py:254
  68.8 0.0 copy-start.7
  68.8 0.0 copy-start.6
  68.8 0.0 copy-start.5
  68.8 0.2 edges.1
  69.1 1.5 %collective-permute-start = (f32[256,256]{1,0:T(8,128)S(1)}, f32[256,256]{1,0:T(8,128)S(1)}, u32[]{:S(2)}, u32[]{:S(2)}) collective-permute-start(f32[256,256]{1,0:T(8,128)S(1)} %get-tuple-element.18), channel_id=1, source_target_pairs={{0,1},{1,2},{2,3},{3,4},{4,5},{5,6},{6,7},{7,8},{8,9},{9,10},{10,1... | collective-permute-start | bytes 786440 | tf_op jit(solution)/shard_map/ppermute | solution.py:231
  70.6 1.3 collective-permute-start.1
  72.0 0.0 copy-done.7
  72.0 0.6 dynamic_slice.11
  73.2 0.8 dynamic_slice.12
  74.0 0.7 dynamic_slice.10
  74.7 0.0 copy-done.6
  74.7 0.1 broadcast_in_dim.20
  74.8 0.1 reshape.29.pair_ref
  74.9 0.1 reshape.28.col_ref
  74.9 0.0 copy-done.5
  75.0 0.0 copy-start
  75.0 2.2 %copy-done = f32[1024,1024]{1,0:T(8,128)S(1)} copy-done((f32[1024,1024]{1,0:T(8,128)S(1)}, f32[1024,1024]{1,0:T(8,128)}, u32[]{:S(2)}) %copy-start) | copy-done | bytes 4194328
  77.1 1.4 %prep.1 = (bf16[1024,1024]{1,0:T(8,128)(2,1)S(1)}, bf16[1024,1024]{1,0:T(8,128)(2,1)S(1)}, bf16[256,256]{1,0:T(8,128)(2,1)S(1)}, bf16[256,256]{1,0:T(8,128)(2,1)S(1)}) custom-call(f32[1024,1024]{1,0:T(8,128)S(1)} %copy-done, f32[64,64]{1,0:T(8,128)S(1)} %copy-done.5), custom_call_target="tpu_custom_call" | custom-call | flops 8388608 | bytes 8388608 | tf_op jit(solution)/shard_map/prep/pallas_call | solution.py:101
  78.6 0.0 copy-start.3
  78.6 0.0 copy-start.4
  78.6 2.6 %inner.2.sum_ref = f32[256,1024]{1,0:T(8,128)S(1)} custom-call(f32[4096,128]{1,0:T(8,128)S(1)} %bitcast.10, bf16[1024,1024]{1,0:T(8,128)(2,1)S(1)} %get-tuple-element.14.refs_1_.refs_2_, bf16[1024,1024]{1,0:T(8,128)(2,1)S(1)} %get-tuple-element.15.refs_2_.refs_3_, bf16[256,256]{1,0:T(8,128)(2,1)S(1)} %get-tuple-element.16.refs_3_.refs_4_, ...), custom_call_target="tpu_custom_call" | custom-call | flops 2013265920 | bytes 8388608 | tf_op jit(solution)/shard_map/inner/pallas_call | solution.py:165
  81.2 0.0 collective-permute-done.before_ref
  81.2 0.0 collective-permute-done.1.after_ref
  81.2 0.0 copy-done.3
  81.2 0.0 copy-done.4
  81.2 0.4 finish.2
  81.7 4.6 %collective-permute-start.2 = (f32[256,256]{1,0:T(8,128)S(1)}, f32[256,256]{1,0:T(8,128)S(1)}, u32[]{:S(2)}, u32[]{:S(2)}) collective-permute-start(f32[256,256]{1,0:T(8,128)S(1)} %get-tuple-element.21), channel_id=1, source_target_pairs={{0,1},{1,2},{2,3},{3,4},{4,5},{5,6},{6,7},{7,8},{8,9},{9,10},{10,1... | collective-permute-start | bytes 786440 | tf_op jit(solution)/shard_map/ppermute | solution.py:231
  86.3 1.3 collective-permute-start.3
  87.6 2.4 %inner.3.sum_ref = f32[256,1024]{1,0:T(8,128)S(1)} custom-call(f32[256,1024]{1,0:T(8,128)S(1)} %get-tuple-element.20.refs_0_, f32[4096,128]{1,0:T(8,128)S(1)} %bitcast.11, bf16[1024,1024]{1,0:T(8,128)(2,1)S(1)} %get-tuple-element.14.refs_1_.refs_2_, bf16[1024,1024]{1,0:T(8,128)(2,1)S(1)} %get-tuple-element.15.refs_2_.refs_3_, ...), custom_call_target="tpu_custom_call" | custom-call | flops 2013265920 | bytes 8388608 | tf_op jit(solution)/shard_map/inner/pallas_call | solution.py:165
  90.1 1.2 collective-permute-done.2.before_ref
  91.2 4.2 %collective-permute-done.3.after_ref = f32[256,256]{1,0:T(8,128)S(1)} collective-permute-done((f32[256,256]{1,0:T(8,128)S(1)}, f32[256,256]{1,0:T(8,128)S(1)}, u32[]{:S(2)}, u32[]{:S(2)}) %collective-permute-start.3) | collective-permute-done | bytes 262176 | tf_op jit(solution)/shard_map/ppermute | solution.py:232
  95.4 0.5 finish.3
  95.9 36.5 %all_to_all.11 = f32[64,32,128]{2,1,0:T(8,128)S(1)} all-to-all(f32[64,32,128]{2,1,0:T(8,128)S(1)} %bitcast.14), channel_id=1, replica_groups=mesh['pair'=64,'virt'=12] {'pair'}, dimensions={0} | all-to-all | bytes 2097152 | tf_op jit(solution)/shard_map/all_to_all | solution.py:274
  132.4 3.1 %unpack.1 = f32[1024,256]{1,0:T(8,128)} custom-call(f32[2048,128]{1,0:T(8,128)S(1)} %bitcast.13), custom_call_target="tpu_custom_call" | custom-call | tf_op jit(solution)/shard_map/unpack/pallas_call | solution.py:69
  (1 shorter events, 0.0 us)
Async XLA Ops:
  0.0 1.2 copy-start.1
  1.2 1.2 copy-start.2
  68.8 3.1 %copy-start.7 = (s32[2]{0:T(128)S(1)}, s32[2]{0:T(128)}, u32[]{:S(2)}) copy-start(s32[2]{0:T(128)} %param.17) | copy-start | bytes 28
  68.8 5.8 %copy-start.6 = (f32[64]{0:T(128)S(1)}, f32[64]{0:T(128)}, u32[]{:S(2)}) copy-start(f32[64]{0:T(128)} %param.15) | copy-start | bytes 772
  68.8 6.1 %copy-start.5 = (f32[64,64]{1,0:T(8,128)S(1)}, f32[64,64]{1,0:T(8,128)}, u32[]{:S(2)}) copy-start(f32[64,64]{1,0:T(8,128)} %l_ref.1) | copy-start | bytes 49156
  69.1 12.1 %collective-permute-start = (f32[256,256]{1,0:T(8,128)S(1)}, f32[256,256]{1,0:T(8,128)S(1)}, u32[]{:S(2)}, u32[]{:S(2)}) collective-permute-start(f32[256,256]{1,0:T(8,128)S(1)} %get-tuple-element.18), channel_id=1, source_target_pairs={{0,1},{1,2},{2,3},{3,4},{4,5},{5,6},{6,7},{7,8},{8,9},{9,10},{10,1... | collective-permute-start | bytes 786440 | tf_op jit(solution)/shard_map/ppermute | solution.py:231
  70.6 10.6 %collective-permute-start.1 = (f32[256,256]{1,0:T(8,128)S(1)}, f32[256,256]{1,0:T(8,128)S(1)}, u32[]{:S(2)}, u32[]{:S(2)}) collective-permute-start(f32[256,256]{1,0:T(8,128)S(1)} %get-tuple-element.19), channel_id=1, source_target_pairs={{1,0},{2,1},{3,2},{4,3},{5,4},{6,5},{7,6},{8,7},{9,8},{10,9},{11,1... | collective-permute-start | bytes 786440 | tf_op jit(solution)/shard_map/ppermute | solution.py:232
  75.0 2.2 %copy-start = (f32[1024,1024]{1,0:T(8,128)S(1)}, f32[1024,1024]{1,0:T(8,128)}, u32[]{:S(2)}) copy-start(f32[1024,1024]{1,0:T(8,128)} %d_ref.1) | copy-start | bytes 12582916
  78.6 2.7 %copy-start.3 = (f32[256,256]{1,0:T(8,128)S(1)}, f32[256,256]{1,0:T(8,128)}, u32[]{:S(2)}) copy-start(f32[256,256]{1,0:T(8,128)} %low_ref.3) | copy-start | bytes 786436
  78.6 2.7 %copy-start.4 = (f32[256,256]{1,0:T(8,128)S(1)}, f32[256,256]{1,0:T(8,128)}, u32[]{:S(2)}) copy-start(f32[256,256]{1,0:T(8,128)} %high_ref.3) | copy-start | bytes 786436
  81.7 9.6 %collective-permute-start.2 = (f32[256,256]{1,0:T(8,128)S(1)}, f32[256,256]{1,0:T(8,128)S(1)}, u32[]{:S(2)}, u32[]{:S(2)}) collective-permute-start(f32[256,256]{1,0:T(8,128)S(1)} %get-tuple-element.21), channel_id=1, source_target_pairs={{0,1},{1,2},{2,3},{3,4},{4,5},{5,6},{6,7},{7,8},{8,9},{9,10},{10,1... | collective-permute-start | bytes 786440 | tf_op jit(solution)/shard_map/ppermute | solution.py:231
  86.3 9.1 %collective-permute-start.3 = (f32[256,256]{1,0:T(8,128)S(1)}, f32[256,256]{1,0:T(8,128)S(1)}, u32[]{:S(2)}, u32[]{:S(2)}) collective-permute-start(f32[256,256]{1,0:T(8,128)S(1)} %get-tuple-element.22), channel_id=1, source_target_pairs={{1,0},{2,1},{3,2},{4,3},{5,4},{6,5},{7,6},{8,7},{9,8},{10,9},{11,1... | collective-permute-start | bytes 786440 | tf_op jit(solution)/shard_map/ppermute | solution.py:232

commit v2 on v1

v2 whole, which is shorter than its diff:
```python
import functools

import jax
import jax.numpy as jnp
from jax import lax
from jax.experimental import pallas as pl
from jax.experimental.pallas import tpu as pltpu
from jax.sharding import PartitionSpec as P

TW = 128
BF = jnp.bfloat16
F32 = jnp.float32
VMEM = pl.BlockSpec(memory_space=pltpu.VMEM)
HBM = pl.BlockSpec(memory_space=pltpu.HBM)
LIMIT = 16 * 1024 * 1024


def split(x):
    hi = x.astype(BF)
    return hi, (x - hi.astype(F32)).astype(BF)


def dot_nt(x, w):
    return lax.dot_general(x, w, (((1,), (1,)), ((), ())), preferred_element_type=F32)


def dot_nn(x, w):
    return jnp.dot(x, w, preferred_element_type=F32)


def three(dot, xh, xl, wh, wl):
    return dot(xh, wh) + (dot(xl, wh) + dot(xh, wl))


def pack_kernel(a_hbm, s_hbm, o_hbm, a_ref, s_ref, o_ref, in_sems, out_sems):
    rows, cols = a_ref.shape
    nk = rows // TW
    arrays = ((a_hbm, a_ref), (s_hbm, s_ref))
    piece = rows // 2
    copies = {}
    for t in range(cols // TW):
        for h in range(2):
            for i, (src, dst) in enumerate(arrays):
                here = (slice(h * piece, (h + 1) * piece), slice(t * TW, (t + 1) * TW))
                copies[t, h, i] = pltpu.make_async_copy(src.at[here], dst.at[here], in_sems.at[t, h, i])
                copies[t, h, i].start()
    length = TW * 2 * nk
    part = length // 4
    sent = []
    for t in range(cols // TW):
        for h in range(2):
            for i, (_, ref) in enumerate(arrays):
                copies[t, h, i].wait()
                for k in range(h * nk // 2, (h + 1) * nk // 2):
                    block = ref[k * TW : (k + 1) * TW, t * TW : (t + 1) * TW]
                    o_ref[pl.ds(t * length + i * nk + k, TW, stride=2 * nk), :] = block.T
        for j in range(4):
            here = slice(t * length + j * part, t * length + (j + 1) * part)
            copy = pltpu.make_async_copy(o_ref.at[here, :], o_hbm.at[here, :], out_sems.at[t, j])
            copy.start()
            sent.append(copy)
    for copy in sent:
        copy.wait()


def pack(a, s):
    rows, cols = a.shape
    nk = rows // TW
    size = (cols * 2 * nk, TW)
    return pl.pallas_call(
        pack_kernel,
        in_specs=[HBM] * 2,
        out_specs=HBM,
        out_shape=jax.ShapeDtypeStruct(size, F32),
        scratch_shapes=[pltpu.VMEM((rows, cols), F32)] * 2
        + [
            pltpu.VMEM(size, F32),
            pltpu.SemaphoreType.DMA((cols // TW, 2, 2)),
            pltpu.SemaphoreType.DMA((cols // TW, 4)),
        ],
        compiler_params=pltpu.CompilerParams(vmem_limit_bytes=60 * 1024 * 1024),
        name="pack",
    )(a, s)


def unpack_kernel(u_ref, o_hbm, o_ref, sems):
    rows, cols = o_ref.shape
    nk = rows // TW
    copies = []
    for k in range(nk):
        for t in range(cols // TW):
            block = u_ref[pl.ds(t * TW * nk + k, TW, stride=nk), :]
            o_ref[k * TW : (k + 1) * TW, t * TW : (t + 1) * TW] = block.T
        here = slice(k * TW, (k + 1) * TW)
        copy = pltpu.make_async_copy(o_ref.at[here, :], o_hbm.at[here, :], sems.at[k])
        copy.start()
        copies.append(copy)
    for copy in copies:
        copy.wait()


def unpack(u, rows, cols):
    nk = rows // TW
    return pl.pallas_call(
        unpack_kernel,
        in_specs=[VMEM],
        out_specs=HBM,
        out_shape=jax.ShapeDtypeStruct((rows, cols), F32),
        scratch_shapes=[pltpu.VMEM((rows, cols), F32), pltpu.SemaphoreType.DMA((nk,))],
        compiler_params=pltpu.CompilerParams(vmem_limit_bytes=LIMIT),
        name="unpack",
    )(u)


def prep_kernel(share, d_ref, l_ref, d2_ref, kh_ref, kl_ref):
    d2_ref[0], d2_ref[1] = split(d_ref[...])
    pairs = l_ref.shape[0]
    size = pairs * share
    spread = (
        lax.broadcasted_iota(jnp.int32, (size, pairs), 0) // share
        == lax.broadcasted_iota(jnp.int32, (size, pairs), 1)
    ).astype(F32).astype(BF)
    same = (
        lax.broadcasted_iota(jnp.int32, (size, size), 0) % share
        == lax.broadcasted_iota(jnp.int32, (size, size), 1) % share
    )
    for part, ref in zip(split(l_ref[...]), (kh_ref, kl_ref)):
        tall = dot_nn(spread, part).astype(BF)
        wide = dot_nt(tall, spread)
        ref[...] = jnp.where(same, wide, 0.0).astype(BF)


def prep(d, l, share):
    rows = d.shape[0]
    size = l.shape[0] * share
    return pl.pallas_call(
        functools.partial(prep_kernel, share),
        in_specs=[VMEM] * 2,
        out_specs=[VMEM] * 3,
        out_shape=[jax.ShapeDtypeStruct((2, rows, rows), BF)]
        + [jax.ShapeDtypeStruct((size, size), BF)] * 2,
        compiler_params=pltpu.CompilerParams(vmem_limit_bytes=LIMIT),
        cost_estimate=pl.CostEstimate(
            flops=8 * rows * rows, bytes_accessed=8 * rows * rows, transcendentals=0
        ),
        name="prep",
    )(d, l)


def edges_kernel(nk, p_ref, first_ref, last_ref):
    lines = first_ref.shape[0]
    tiles = first_ref.shape[1] // TW
    for j in range(tiles):
        cols = slice(j * TW, (j + 1) * TW)
        first_ref[:, cols] = p_ref[pl.ds(j, lines, stride=2 * nk), :]
        last_ref[:, cols] = p_ref[pl.ds(nk - tiles + j, lines, stride=2 * nk), :]


def edges(p, nk, width):
    lines = p.shape[0] // (2 * nk)
    return pl.pallas_call(
        functools.partial(edges_kernel, nk),
        in_specs=[VMEM],
        out_specs=[VMEM] * 2,
        out_shape=[jax.ShapeDtypeStruct((lines, width), F32)] * 2,
        compiler_params=pltpu.CompilerParams(vmem_limit_bytes=LIMIT),
        cost_estimate=pl.CostEstimate(flops=8 * 10**9, bytes_accessed=16 * lines * width, transcendentals=0),
        name="edges",
    )(p)


def energy(row, col_ref, pair_ref):
    return row + col_ref[...] - pair_ref[...]


def source_part(p_ref, nk, wide, c):
    lines = p_ref.shape[0] // (2 * nk)
    per = wide // TW
    return jnp.concatenate([p_ref[pl.ds(nk + c * per + j, lines, stride=2 * nk), :] for j in range(per)], 1)


def within(d2_ref, at, xh_ref, xl_ref, kh_ref, kl_ref, cols):
    out = three(dot_nt, xh_ref[...], xl_ref[...], d2_ref[(0, *at)], d2_ref[(1, *at)])
    return out + three(dot_nn, kh_ref[...], kl_ref[...], xh_ref[:, cols], xl_ref[:, cols])


def head_kernel(
    nk, p_ref, d2_ref, kh_ref, kl_ref, row_ref, col_ref, pair_ref, first_ref, last_ref, xh_ref, xl_ref
):
    lines, wide = first_ref.shape
    for k in range(nk):
        cols = slice(k * TW, (k + 1) * TW)
        xh_ref[:, cols], xl_ref[:, cols] = split(p_ref[pl.ds(k, lines, stride=2 * nk), :])
    for c, ref in ((0, first_ref), (nk * TW // wide - 1, last_ref)):
        cols = slice(c * wide, (c + 1) * wide)
        out = within(d2_ref, (cols,), xh_ref, xl_ref, kh_ref, kl_ref, cols) + source_part(p_ref, nk, wide, c)
        ref[...] = out / energy(row_ref[:, cols], col_ref, pair_ref)


def body_kernel(
    nk, p_ref, d2_ref, kh_ref, kl_ref, row_ref, col_ref, pair_ref, first_ref, last_ref, xh_ref, xl_ref,
    o_ref, gh_ref, gl_ref,
):
    lines, wide = first_ref.shape
    count = nk * TW // wide
    for c, ref in ((0, first_ref), (count - 1, last_ref)):
        cols = slice(c * wide, (c + 1) * wide)
        gh_ref[:, cols], gl_ref[:, cols] = split(ref[...])
    for c in range(1, count - 1):
        cols = slice(c * wide, (c + 1) * wide)
        out = within(d2_ref, (cols,), xh_ref, xl_ref, kh_ref, kl_ref, cols) + source_part(p_ref, nk, wide, c)
        gh_ref[:, cols], gl_ref[:, cols] = split(out / energy(row_ref[:, cols], col_ref, pair_ref))
    for c in range(count):
        cols = slice(c * wide, (c + 1) * wide)
        o_ref[:, cols] = within(d2_ref, (cols,), gh_ref, gl_ref, kh_ref, kl_ref, cols) + source_part(p_ref, nk, wide, c)


def mid_kernel(
    t_ref, first_ref, last_ref, before_ref, after_ref, low_ref, high_ref, low_next_ref, high_prev_ref,
    d2_ref, kh_ref, kl_ref, row_ref, row_prev_ref, row_next_ref, col_ref, pair_ref, o_ref,
):
    rows = t_ref.shape[1]
    wide = low_ref.shape[0]
    low = split(low_ref[...])
    high = split(high_ref[...])
    front = slice(0, wide)
    rear = slice(rows - wide, rows)
    own_front = three(dot_nt, *split(before_ref[...]), *low) / energy(row_ref[:, front], col_ref, pair_ref)
    own_rear = three(dot_nt, *split(after_ref[...]), *high) / energy(row_ref[:, rear], col_ref, pair_ref)
    prev = three(dot_nt, *split(first_ref[...]), *split(high_prev_ref[...]))
    prev = prev / energy(row_prev_ref[...], col_ref, pair_ref)
    after = three(dot_nt, *split(last_ref[...]), *split(low_next_ref[...]))
    after = after / energy(row_next_ref[...], col_ref, pair_ref)
    own_front = split(own_front)
    own_rear = split(own_rear)
    count = rows // wide
    for c in range(count):
        cols = slice(c * wide, (c + 1) * wide)
        out = t_ref[:, cols]
        out += three(dot_nt, *own_front, d2_ref[0, cols, front], d2_ref[1, cols, front])
        out += three(dot_nt, *own_rear, d2_ref[0, cols, rear], d2_ref[1, cols, rear])
        if c == 0:
            out += three(dot_nn, kh_ref[...], kl_ref[...], *own_front)
            out += three(dot_nt, *split(prev), *low)
        if c == count - 1:
            out += three(dot_nn, kh_ref[...], kl_ref[...], *own_rear)
            out += three(dot_nt, *split(after), *high)
        o_ref[:, cols] = out


def finish_kernel(nk, t_ref, before_ref, after_ref, low_ref, high_ref, row_ref, col_ref, pair_ref, o_ref):
    lines, rows = t_ref.shape
    wide = low_ref.shape[0]
    count = rows // wide
    per = wide // TW
    for c in [*range(1, count - 1), 0, count - 1]:
        cols = slice(c * wide, (c + 1) * wide)
        out = t_ref[:, cols]
        if c == 0:
            out += three(dot_nt, *split(before_ref[...]), *split(low_ref[...]))
        if c == count - 1:
            out += three(dot_nt, *split(after_ref[...]), *split(high_ref[...]))
        out = out / energy(row_ref[:, cols], col_ref, pair_ref)
        for j in range(per):
            o_ref[pl.ds(c * per + j, lines, stride=nk), :] = out[:, j * TW : (j + 1) * TW]


def call(name, kernel, args, shapes, flops, scratch=()):
    size = sum(a.size * a.dtype.itemsize for a in (*args, *shapes))
    return pl.pallas_call(
        kernel,
        in_specs=[VMEM] * len(args),
        out_specs=[VMEM] * len(shapes),
        out_shape=shapes,
        scratch_shapes=scratch,
        compiler_params=pltpu.CompilerParams(vmem_limit_bytes=LIMIT),
        cost_estimate=pl.CostEstimate(flops=flops, bytes_accessed=size, transcendentals=0),
        name=name,
    )(*args)


def exchange(first, last):
    count = lax.axis_size("virt")
    up = [(i, i + 1) for i in range(count - 1)]
    down = [(j, i) for i, j in up]
    before = lax.ppermute(last, "virt", up)
    after = lax.ppermute(first, "virt", down)
    return before, after


def local(
    amplitudes,
    source,
    diag_block,
    edge_low,
    edge_high,
    hole_coupling,
    pair_energy,
    virt_energy,
    column_tiles,
):
    rows, cols = amplitudes.shape[1:]
    width = edge_low.shape[0]
    pairs = pair_energy.shape[0]
    share = cols // pairs
    nk = rows // TW
    lines = pairs * share

    packed = pack(amplitudes[0], source[0]).reshape(pairs, share * 2 * nk, TW)
    held = lax.all_to_all(packed, "pair", split_axis=0, concat_axis=0, tiled=True)
    held = held.reshape(lines * 2 * nk, TW)

    parts = prep(diag_block, hole_coupling, share)
    high_prev, low_next = exchange(edge_low, edge_high)
    at = lax.axis_index("virt") * rows
    row = lax.dynamic_slice_in_dim(virt_energy, at, rows)[None, :]
    row_prev = lax.dynamic_slice_in_dim(virt_energy, jnp.maximum(at - width, 0), width)[None, :]
    row_next = lax.dynamic_slice_in_dim(
        virt_energy, jnp.minimum(at + rows, virt_energy.shape[0] - width), width
    )[None, :]
    start = lax.axis_index("pair") * share
    tile = lax.dynamic_index_in_dim(column_tiles, start // TW, keepdims=False)
    kept = lax.dynamic_slice_in_dim(virt_energy, tile * TW + start % TW, share)
    col = jnp.broadcast_to(kept[None, :], (pairs, share)).reshape(-1, 1)
    own = jnp.broadcast_to(pair_energy[:, None], (pairs, share)).reshape(-1, 1)
    small = (edge_low, edge_high, low_next, high_prev, row, row_prev, row_next, col, own)
    held, parts, small = lax.optimization_barrier((held, parts, small))
    low, high, low_next, high_prev, row, row_prev, row_next, col, own = small

    full = jax.ShapeDtypeStruct((lines, rows), F32)
    edge = jax.ShapeDtypeStruct((lines, width), F32)
    scratch = [pltpu.VMEM((lines, rows), BF)] * 2
    most = 6 * lines * rows * (rows + lines)
    first, last = edges(held, nk, width)
    before, after = exchange(first, last)
    d2, kh, kl = parts
    common = (held, d2, kh, kl, row, col, own)
    half = jax.ShapeDtypeStruct((lines, rows), BF)
    field_first, field_last, xh, xl = call(
        "head", functools.partial(head_kernel, nk), common, [edge, edge, half, half], most // 2
    )
    field_before, field_after = exchange(field_first, field_last)
    (total,) = call(
        "body",
        functools.partial(body_kernel, nk),
        (*common, field_first, field_last, xh, xl),
        [full],
        most + most // 2,
        scratch,
    )
    (total,) = call(
        "mid",
        mid_kernel,
        (total, first, last, before, after, low, high, low_next, high_prev, d2, kh, kl, row, row_prev, row_next, col, own),
        [full],
        most // 2,
    )
    (out,) = call(
        "finish",
        functools.partial(finish_kernel, nk),
        (total, field_before, field_after, low, high, row, col, own),
        [jax.ShapeDtypeStruct((lines * nk, TW), F32)],
        12 * lines * width * width,
    )
    back = lax.all_to_all(out.reshape(pairs, share * nk, TW), "pair", split_axis=0, concat_axis=0, tiled=True)
    return unpack(back.reshape(lines * nk, TW), rows, cols)[None]


def solution(mesh):
    in_specs = (
        P("pair", "virt", None),
        P("pair", "virt", None),
        P("virt", None),
        P("virt", None),
        P("virt", None),
        P(),
        P(),
        P(),
        P(),
    )
    out_specs = P("pair", "virt", None)
    return jax.shard_map(local, mesh=mesh, in_specs=in_specs, out_specs=out_specs, check_vma=False)
```

time: 137 us -> 128 us (0.934); the launches traced: 136 us -> 125 us
  blocking collectives: 102 us -> 35.2 us
  waiting for transfers between devices: 5.37 us -> 38.5 us
  starting transfers between devices: 8.73 us -> 28.3 us
  Pallas kernels: 12 us -> 13.9 us
    all_to_all x2 -> x1, blocking collectives: 102 us -> 35.2 us  [local(): lax.all_to_all(out.reshape(pairs, share * nk, TW), 'pair', split_axis=0,...]
    all_to_all x0 -> x1, waiting for transfers between devices: none -> 35.8 us  [local(): lax.all_to_all(packed, 'pair', split_axis=0, concat_axis=0, tiled=True)]
    all_to_all x0 -> x1, starting transfers between devices: none -> 14.6 us  [local(): lax.all_to_all(packed, 'pair', split_axis=0, concat_axis=0, tiled=True)]
    ppermute x2 -> x3, starting transfers between devices: 6.15 us -> 9.79 us  [exchange(): before = lax.ppermute(last, 'virt', up)]
    pallas_call x6, Pallas kernels: 10.3 us -> 12.2 us  [the longest x4 7.78 us: call(): pl.pallas_call(kernel, in_specs=[VMEM] * len(args), out_specs=[VMEM] * le...]
    ppermute x2 -> x3, waiting for transfers between devices: 4.19 us -> 2.65 us  [exchange(): after = lax.ppermute(first, 'virt', down)]
    ppermute x2 -> x3, starting transfers between devices: 2.58 us -> 3.88 us  [exchange(): after = lax.ppermute(first, 'virt', down)]
    unnamed x16 -> x20, local copies, waits for them, and re-layouts: 4.66 us -> 4.85 us
  transfers between devices with their start and end apart: 4 -> 7, of which waited for: 2 -> 2; matrix products, arithmetic and copies ran while one was open for 2% -> 3% of each run, Pallas kernels for 5% -> 7%
where the time goes in v2:
time: 128 us; the launch traced here: 125 us
  waiting for transfers between devices  38.5 us (30%)
  blocking collectives  35.2 us (28%)
  starting transfers between devices  28.3 us (22%)
  Pallas kernels  13.9 us (11%)
  local copies, waits for them, and re-layouts  8.31 us (6%)
    all_to_all x1, waiting for transfers between devices, local(): lax.all_to_all(packed, 'pair', split_axis=0, concat_axis=0, tiled=True)  35.8 us
    all_to_all x1, blocking collectives, local(): lax.all_to_all(out.reshape(pairs, share * nk, TW), 'pair', split_axis=0,...  35.2 us
    all_to_all x1, starting transfers between devices, local(): lax.all_to_all(packed, 'pair', split_axis=0, concat_axis=0, tiled=True)  14.6 us
    ppermute x3, starting transfers between devices, exchange(): before = lax.ppermute(last, 'virt', up)  9.79 us
    pallas_call x4, Pallas kernels, call(): pl.pallas_call(kernel, in_specs=[VMEM] * len(args), out_specs=[VMEM] * le...  7.78 us
    unnamed x20, local copies, waits for them, and re-layouts  4.85 us
    ppermute x3, starting transfers between devices, exchange(): after = lax.ppermute(first, 'virt', down)  3.88 us
    pallas_call x1, Pallas kernels, pack(): pl.pallas_call(pack_kernel, in_specs=[HBM] * 2, out_specs=HBM, out_shape=...  3.32 us
  transfers between devices with their start and end apart: 7, of which 2 were waited for; matrix products, arithmetic and copies ran while one was open for 3% of the time, Pallas kernels for 7%

profile of v2, /device:TPU:1, one launch (start us, length us, event | category | flops | bytes accessed | tf_op | source)
XLA Modules:
  0.0 125.1 jit_solution(17425239680697738162)
XLA Ops:
  0.0 0.0 copy-start.8
  0.0 0.0 copy-start.7
  0.0 3.3 %pack.1 = f32[4096,128]{1,0:T(8,128)} custom-call(f32[1024,256]{1,0:T(8,128)} %bitcast.23, f32[1024,256]{1,0:T(8,128)} %bitcast.24), custom_call_target="tpu_custom_call" | custom-call | tf_op jit(solution)/shard_map/pack/pallas_call | solution.py:70
  3.4 14.6 %all-to-all-start = ((f32[64,64,128]{2,1,0:T(8,128)}), f32[64,64,128]{2,1,0:T(8,128)S(1)}, u32[]{:S(2)}, u32[]{:S(2)}) async-start(f32[64,64,128]{2,1,0:T(8,128)} %bitcast.22), calls=%async_computation | async-start | bytes 4194304 | tf_op jit(solution)/shard_map/all_to_all | solution.py:310
  18.0 0.0 copy-done.3
  18.0 1.3 %collective-permute-start = (f32[256,256]{1,0:T(8,128)S(1)}, f32[256,256]{1,0:T(8,128)S(1)}, u32[]{:S(2)}, u32[]{:S(2)}) collective-permute-start(f32[256,256]{1,0:T(8,128)S(1)} %copy-done.3), channel_id=1, source_target_pairs={{1,0},{2,1},{3,2},{4,3},{5,4},{6,5},{7,6},{8,7},{9,8},{10,9},{11,1... | collective-permute-start | bytes 786440 | tf_op jit(solution)/shard_map/ppermute | solution.py:287
  19.3 0.0 copy-done.4
  19.3 4.0 %collective-permute-start.1 = (f32[256,256]{1,0:T(8,128)S(1)}, f32[256,256]{1,0:T(8,128)S(1)}, u32[]{:S(2)}, u32[]{:S(2)}) collective-permute-start(f32[256,256]{1,0:T(8,128)S(1)} %copy-done.4), channel_id=1, source_target_pairs={{0,1},{1,2},{2,3},{3,4},{4,5},{5,6},{6,7},{7,8},{8,9},{9,10},{10,1... | collective-permute-start | bytes 786440 | tf_op jit(solution)/shard_map/ppermute | solution.py:286
  23.4 0.0 copy-done.9
  23.4 0.6 dynamic_slice.19
  24.6 0.8 dynamic_slice.20
  25.4 0.1 reshape.24
  25.5 0.7 dynamic_slice.16
  26.2 0.0 copy-done.8
  26.2 0.1 broadcast_in_dim.28
  26.3 0.1 reshape.25
  26.4 0.0 copy-done.7
  26.4 0.0 copy-start.2
  26.5 2.2 %copy-done.2 = f32[1024,1024]{1,0:T(8,128)S(1)} copy-done((f32[1024,1024]{1,0:T(8,128)S(1)}, f32[1024,1024]{1,0:T(8,128)}, u32[]{:S(2)}) %copy-start.2) | copy-done | bytes 4194328
  28.6 1.4 %prep.1 = (bf16[2,1024,1024]{2,1,0:T(8,128)(2,1)S(1)}, bf16[256,256]{1,0:T(8,128)(2,1)S(1)}, bf16[256,256]{1,0:T(8,128)(2,1)S(1)}) custom-call(f32[1024,1024]{1,0:T(8,128)S(1)} %copy-done.2, f32[64,64]{1,0:T(8,128)S(1)} %copy-done.7), custom_call_target="tpu_custom_call" | custom-call | flops 8388608 | bytes 8388608 | tf_op jit(solution)/shard_map/prep/pallas_call | solution.py:136
  30.1 0.0 copy-start
  30.1 1.9 %copy-done = bf16[2,1024,1024]{2,1,0:T(8,128)(2,1)} copy-done((bf16[2,1024,1024]{2,1,0:T(8,128)(2,1)}, bf16[2,1024,1024]{2,1,0:T(8,128)(2,1)S(1)}, u32[]{:S(2)}) %copy-start) | copy-done | bytes 4194328
  32.0 0.8 fusion
  32.8 0.0 collective-permute-done.low_next_ref
  32.8 0.0 collective-permute-done.1.high_prev_ref
  32.9 0.7 copy-done.5
  33.6 35.8 %all-to-all-done = f32[64,64,128]{2,1,0:T(8,128)S(1)} async-done(((f32[64,64,128]{2,1,0:T(8,128)}), f32[64,64,128]{2,1,0:T(8,128)S(1)}, u32[]{:S(2)}, u32[]{:S(2)}) %all-to-all-start) | async-done | bytes 2097184 | tf_op jit(solution)/shard_map/all_to_all | solution.py:310
  69.4 0.1 copy.12.col_ref
  69.5 0.1 copy.13.pair_ref
  69.7 0.0 copy-start.1
  69.7 0.2 edges.1
  69.9 1.6 %collective-permute-start.2 = (f32[256,256]{1,0:T(8,128)S(1)}, f32[256,256]{1,0:T(8,128)S(1)}, u32[]{:S(2)}, u32[]{:S(2)}) collective-permute-start(f32[256,256]{1,0:T(8,128)S(1)} %get-tuple-element.42.last_ref), channel_id=1, source_target_pairs={{0,1},{1,2},{2,3},{3,4},{4,5},{5,6},{6,7},{7,8},{8,9},{9,10},{10,1... | collective-permute-start | bytes 786440 | tf_op jit(solution)/shard_map/ppermute | solution.py:286
  71.5 1.3 %collective-permute-start.3 = (f32[256,256]{1,0:T(8,128)S(1)}, f32[256,256]{1,0:T(8,128)S(1)}, u32[]{:S(2)}, u32[]{:S(2)}) collective-permute-start(f32[256,256]{1,0:T(8,128)S(1)} %get-tuple-element.41.first_ref), channel_id=1, source_target_pairs={{1,0},{2,1},{3,2},{4,3},{5,4},{6,5},{7,6},{8,7},{9,8},{10,9},{11,1... | collective-permute-start | bytes 786440 | tf_op jit(solution)/shard_map/ppermute | solution.py:287
  72.8 0.0 copy-done.1
  72.8 1.6 %head.1 = (f32[256,256]{1,0:T(8,128)S(1)}, f32[256,256]{1,0:T(8,128)S(1)}, bf16[256,1024]{1,0:T(8,128)(2,1)S(1)}, bf16[256,1024]{1,0:T(8,128)(2,1)S(1)}) custom-call(f32[4096,128]{1,0:T(8,128)S(1)} %bitcast.12, bf16[2,1024,1024]{2,1,0:T(8,128)(2,1)S(1)} %copy-done.1, bf16[256,256]{1,0:T(8,128)(2,1)S(1)} %get-tuple-element.32.kh_ref, ...), custom_call_target="tpu_custom_call" | custom-call | flops 1006632960 | bytes 8132608 | tf_op jit(solution)/shard_map/head/pallas_call | solution.py:270
  74.4 4.2 %collective-permute-start.4 = (f32[256,256]{1,0:T(8,128)S(1)}, f32[256,256]{1,0:T(8,128)S(1)}, u32[]{:S(2)}, u32[]{:S(2)}) collective-permute-start(f32[256,256]{1,0:T(8,128)S(1)} %get-tuple-element.38.last_ref), channel_id=1, source_target_pairs={{0,1},{1,2},{2,3},{3,4},{4,5},{5,6},{6,7},{7,8},{8,9},{9,10},{10,1... | collective-permute-start | bytes 786440 | tf_op jit(solution)/shard_map/ppermute | solution.py:286
  78.6 1.3 %collective-permute-start.5 = (f32[256,256]{1,0:T(8,128)S(1)}, f32[256,256]{1,0:T(8,128)S(1)}, u32[]{:S(2)}, u32[]{:S(2)}) collective-permute-start(f32[256,256]{1,0:T(8,128)S(1)} %get-tuple-element.37.first_ref), channel_id=1, source_target_pairs={{1,0},{2,1},{3,2},{4,3},{5,4},{6,5},{7,6},{8,7},{9,8},{10,9},{11,1... | collective-permute-start | bytes 786440 | tf_op jit(solution)/shard_map/ppermute | solution.py:287
  79.9 0.0 copy-start.6
  79.9 3.6 %body.1.t_ref = f32[256,1024]{1,0:T(8,128)S(1)} custom-call(f32[4096,128]{1,0:T(8,128)S(1)} %bitcast.13, bf16[2,1024,1024]{2,1,0:T(8,128)(2,1)S(1)} %copy-done.1, bf16[256,256]{1,0:T(8,128)(2,1)S(1)} %get-tuple-element.32.kh_ref, bf16[256,256]{1,0:T(8,128)(2,1)S(1)} %get-tuple-element.33.kl_ref, f32[1,1024]{1,0:T(1,128)S(1)} %bitcast.17, ...), custom_call_target="tpu_custom_call" | custom-call | flops 3019898880 | bytes 9181184 | tf_op jit(solution)/shard_map/body/pallas_call | solution.py:270
  83.5 0.0 collective-permute-done.2.before_ref
  83.5 0.0 collective-permute-done.3.after_ref
  83.5 0.0 copy-done.6
  83.5 2.1 %mid.1.t_ref = f32[256,1024]{1,0:T(8,128)S(1)} custom-call(f32[256,1024]{1,0:T(8,128)S(1)} %body.1.t_ref, f32[256,256]{1,0:T(8,128)S(1)} %get-tuple-element.41.first_ref, f32[256,256]{1,0:T(8,128)S(1)} %get-tuple-element.42.last_ref, f32[256,256]{1,0:T(8,128)S(1)} %collective-permute-done.2.before_ref, f32[256,256]{1,0:T(8,128)S(1)} %collective-permute-done.3.after_ref, ...), custom_call_target="tpu_custom_call" | custom-call | flops 1006632960 | bytes 8658944 | tf_op jit(solution)/shard_map/mid/pallas_call | solution.py:270
  85.6 0.0 collective-permute-done.4.before_ref
  85.6 2.6 %collective-permute-done.5.after_ref = f32[256,256]{1,0:T(8,128)S(1)} collective-permute-done((f32[256,256]{1,0:T(8,128)S(1)}, f32[256,256]{1,0:T(8,128)S(1)}, u32[]{:S(2)}, u32[]{:S(2)}) %collective-permute-start.5) | collective-permute-done | bytes 262176 | tf_op jit(solution)/shard_map/ppermute | solution.py:287
  88.3 0.5 finish.1
  88.8 35.2 %all_to_all.10 = f32[64,32,128]{2,1,0:T(8,128)S(1)} all-to-all(f32[64,32,128]{2,1,0:T(8,128)S(1)} %bitcast.15), channel_id=1, replica_groups=mesh['pair'=64,'virt'=12] {'pair'}, dimensions={0} | all-to-all | bytes 2097152 | tf_op jit(solution)/shard_map/all_to_all | solution.py:365
  124.0 1.1 unpack.1
  (5 shorter events, 0.0 us)
Async XLA Ops:
  0.0 18.0 %copy-start.3 = (f32[256,256]{1,0:T(8,128)S(1)}, f32[256,256]{1,0:T(8,128)}, u32[]{:S(2)}) copy-start(f32[256,256]{1,0:T(8,128)} %low_ref.1) | copy-start | bytes 786436
  0.0 19.3 %copy-start.4 = (f32[256,256]{1,0:T(8,128)S(1)}, f32[256,256]{1,0:T(8,128)}, u32[]{:S(2)}) copy-start(f32[256,256]{1,0:T(8,128)} %high_ref.1) | copy-start | bytes 786436
  0.0 23.4 %copy-start.9 = (s32[2]{0:T(128)S(1)}, s32[2]{0:T(128)}, u32[]{:S(2)}) copy-start(s32[2]{0:T(128)} %param.17) | copy-start | bytes 28
  0.0 26.2 %copy-start.8 = (f32[64]{0:T(128)S(1)}, f32[64]{0:T(128)}, u32[]{:S(2)}) copy-start(f32[64]{0:T(128)} %param.15) | copy-start | bytes 772
  0.0 26.4 %copy-start.7 = (f32[64,64]{1,0:T(8,128)S(1)}, f32[64,64]{1,0:T(8,128)}, u32[]{:S(2)}) copy-start(f32[64,64]{1,0:T(8,128)} %l_ref.1) | copy-start | bytes 49156
  3.4 66.0 %all-to-all-start = ((f32[64,64,128]{2,1,0:T(8,128)}), f32[64,64,128]{2,1,0:T(8,128)S(1)}, u32[]{:S(2)}, u32[]{:S(2)}) async-start(f32[64,64,128]{2,1,0:T(8,128)} %bitcast.22), calls=%async_computation | async-start | bytes 4194304 | tf_op jit(solution)/shard_map/all_to_all | solution.py:310
  18.0 14.8 %collective-permute-start = (f32[256,256]{1,0:T(8,128)S(1)}, f32[256,256]{1,0:T(8,128)S(1)}, u32[]{:S(2)}, u32[]{:S(2)}) collective-permute-start(f32[256,256]{1,0:T(8,128)S(1)} %copy-done.3), channel_id=1, source_target_pairs={{1,0},{2,1},{3,2},{4,3},{5,4},{6,5},{7,6},{8,7},{9,8},{10,9},{11,1... | collective-permute-start | bytes 786440 | tf_op jit(solution)/shard_map/ppermute | solution.py:287
  19.3 13.5 %collective-permute-start.1 = (f32[256,256]{1,0:T(8,128)S(1)}, f32[256,256]{1,0:T(8,128)S(1)}, u32[]{:S(2)}, u32[]{:S(2)}) collective-permute-start(f32[256,256]{1,0:T(8,128)S(1)} %copy-done.4), channel_id=1, source_target_pairs={{0,1},{1,2},{2,3},{3,4},{4,5},{5,6},{6,7},{7,8},{8,9},{9,10},{10,1... | collective-permute-start | bytes 786440 | tf_op jit(solution)/shard_map/ppermute | solution.py:286
  26.4 2.2 %copy-start.2 = (f32[1024,1024]{1,0:T(8,128)S(1)}, f32[1024,1024]{1,0:T(8,128)}, u32[]{:S(2)}) copy-start(f32[1024,1024]{1,0:T(8,128)} %d_ref.1) | copy-start | bytes 12582916
  30.1 1.9 %copy-start = (bf16[2,1024,1024]{2,1,0:T(8,128)(2,1)}, bf16[2,1024,1024]{2,1,0:T(8,128)(2,1)S(1)}, u32[]{:S(2)}) copy-start(bf16[2,1024,1024]{2,1,0:T(8,128)(2,1)S(1)} %get-tuple-element.31.d2_ref) | copy-start | bytes 12582916
  32.8 0.7 copy-start.5
  69.7 3.1 %copy-start.1 = (bf16[2,1024,1024]{2,1,0:T(8,128)(2,1)S(1)}, bf16[2,1024,1024]{2,1,0:T(8,128)(2,1)}, u32[]{:S(2)}) copy-start(bf16[2,1024,1024]{2,1,0:T(8,128)(2,1)} %copy-done) | copy-start | bytes 12582916
  69.9 13.6 %collective-permute-start.2 = (f32[256,256]{1,0:T(8,128)S(1)}, f32[256,256]{1,0:T(8,128)S(1)}, u32[]{:S(2)}, u32[]{:S(2)}) collective-permute-start(f32[256,256]{1,0:T(8,128)S(1)} %get-tuple-element.42.last_ref), channel_id=1, source_target_pairs={{0,1},{1,2},{2,3},{3,4},{4,5},{5,6},{6,7},{7,8},{8,9},{9,10},{10,1... | collective-permute-start | bytes 786440 | tf_op jit(solution)/shard_map/ppermute | solution.py:286
  71.5 12.0 %collective-permute-start.3 = (f32[256,256]{1,0:T(8,128)S(1)}, f32[256,256]{1,0:T(8,128)S(1)}, u32[]{:S(2)}, u32[]{:S(2)}) collective-permute-start(f32[256,256]{1,0:T(8,128)S(1)} %get-tuple-element.41.first_ref), channel_id=1, source_target_pairs={{1,0},{2,1},{3,2},{4,3},{5,4},{6,5},{7,6},{8,7},{9,8},{10,9},{11,1... | collective-permute-start | bytes 786440 | tf_op jit(solution)/shard_map/ppermute | solution.py:287
  74.4 11.3 %collective-permute-start.4 = (f32[256,256]{1,0:T(8,128)S(1)}, f32[256,256]{1,0:T(8,128)S(1)}, u32[]{:S(2)}, u32[]{:S(2)}) collective-permute-start(f32[256,256]{1,0:T(8,128)S(1)} %get-tuple-element.38.last_ref), channel_id=1, source_target_pairs={{0,1},{1,2},{2,3},{3,4},{4,5},{5,6},{6,7},{7,8},{8,9},{9,10},{10,1... | collective-permute-start | bytes 786440 | tf_op jit(solution)/shard_map/ppermute | solution.py:286
  78.6 9.7 %collective-permute-start.5 = (f32[256,256]{1,0:T(8,128)S(1)}, f32[256,256]{1,0:T(8,128)S(1)}, u32[]{:S(2)}, u32[]{:S(2)}) collective-permute-start(f32[256,256]{1,0:T(8,128)S(1)} %get-tuple-element.37.first_ref), channel_id=1, source_target_pairs={{1,0},{2,1},{3,2},{4,3},{5,4},{6,5},{7,6},{8,7},{9,8},{10,9},{11,1... | collective-permute-start | bytes 786440 | tf_op jit(solution)/shard_map/ppermute | solution.py:287
  79.9 3.6 %copy-start.6 = (f32[256,256]{1,0:T(8,128)S(1)}, f32[256,256]{1,0:T(8,128)}, u32[]{:S(2)}) copy-start(f32[256,256]{1,0:T(8,128)} %copy-done.5) | copy-start | bytes 786436

commit v3 on v0

v3 whole, which is shorter than its diff:
```python
import functools

import jax
import jax.numpy as jnp
from jax import lax
from jax.experimental import pallas as pl
from jax.experimental.pallas import tpu as pltpu
from jax.sharding import PartitionSpec as P

TW = 128
BF = jnp.bfloat16
F32 = jnp.float32
VMEM = pl.BlockSpec(memory_space=pltpu.VMEM)
HBM = pl.BlockSpec(memory_space=pltpu.HBM)
LIMIT = 16 * 1024 * 1024


def split(x):
    hi = x.astype(BF)
    return hi, (x - hi.astype(F32)).astype(BF)


def dot_nt(x, w):
    return lax.dot_general(x, w, (((1,), (1,)), ((), ())), preferred_element_type=F32)


def dot_nn(x, w):
    return jnp.dot(x, w, preferred_element_type=F32)


def three(dot, xh, xl, wh, wl):
    return dot(xh, wh) + (dot(xl, wh) + dot(xh, wl))


def pack_kernel(a_hbm, o_hbm, a_ref, o_ref, in_sems, out_sems):
    rows, cols = a_ref.shape
    nk = rows // TW
    tiles = cols // TW
    copies = []
    for t in range(tiles):
        here = (slice(None), slice(t * TW, (t + 1) * TW))
        copies.append(pltpu.make_async_copy(a_hbm.at[here], a_ref.at[here], in_sems.at[t]))
        copies[t].start()
    sent = []
    for t in range(tiles):
        copies[t].wait()
        turn(a_ref, o_ref, t, nk)
        here = slice(t * TW * nk, (t + 1) * TW * nk)
        sent.append(pltpu.make_async_copy(o_ref.at[here, :], o_hbm.at[here, :], out_sems.at[t]))
        sent[t].start()
    for copy in sent:
        copy.wait()


def turn(a_ref, o_ref, t, nk):
    for k in range(nk):
        block = a_ref[k * TW : (k + 1) * TW, t * TW : (t + 1) * TW]
        o_ref[pl.ds(t * TW * nk + k, TW, stride=nk), :] = block.T


def pack(a):
    rows, cols = a.shape
    size = (cols * rows // TW, TW)
    return pl.pallas_call(
        pack_kernel,
        in_specs=[HBM],
        out_specs=HBM,
        out_shape=jax.ShapeDtypeStruct(size, F32),
        scratch_shapes=[pltpu.VMEM((rows, cols), F32), pltpu.VMEM(size, F32)]
        + [pltpu.SemaphoreType.DMA((cols // TW,))] * 2,
        compiler_params=pltpu.CompilerParams(vmem_limit_bytes=60 * 1024 * 1024),
        name="pack",
    )(a)


def prep_kernel(share, d_ref, l_ref, d2_ref, kh_ref, kl_ref):
    d2_ref[0], d2_ref[1] = split(d_ref[...])
    pairs = l_ref.shape[0]
    size = pairs * share
    spread = (
        lax.broadcasted_iota(jnp.int32, (size, pairs), 0) // share
        == lax.broadcasted_iota(jnp.int32, (size, pairs), 1)
    ).astype(F32).astype(BF)
    same = (
        lax.broadcasted_iota(jnp.int32, (size, size), 0) % share
        == lax.broadcasted_iota(jnp.int32, (size, size), 1) % share
    )
    for part, ref in zip(split(l_ref[...]), (kh_ref, kl_ref)):
        tall = dot_nn(spread, part).astype(BF)
        wide = dot_nt(tall, spread)
        ref[...] = jnp.where(same, wide, 0.0).astype(BF)


def prep(d, l, share):
    rows = d.shape[0]
    size = l.shape[0] * share
    return pl.pallas_call(
        functools.partial(prep_kernel, share),
        in_specs=[VMEM] * 2,
        out_specs=[VMEM] * 3,
        out_shape=[jax.ShapeDtypeStruct((2, rows, rows), BF)]
        + [jax.ShapeDtypeStruct((size, size), BF)] * 2,
        compiler_params=pltpu.CompilerParams(vmem_limit_bytes=LIMIT),
        cost_estimate=pl.CostEstimate(
            flops=8 * rows * rows, bytes_accessed=8 * rows * rows, transcendentals=0
        ),
        name="prep",
    )(d, l)


def energy(row, col, pair):
    return row + col - pair


def coupled(d2_ref, xh_ref, xl_ref, rows):
    return three(dot_nn, d2_ref[0, rows, :], d2_ref[1, rows, :], xh_ref[...], xl_ref[...])


def with_edges(c, count, out, low_ref, high_ref, before_ref, after_ref):
    if c == 0:
        out += three(dot_nn, *split(low_ref[...]), *split(before_ref[...]))
    if c == count - 1:
        out += three(dot_nn, *split(high_ref[...]), *split(after_ref[...]))
    return out


def own_kernel(
    nk, x_ref, s_ref, before_ref, after_ref, low_ref, high_ref, d2_ref, virt_ref, kept_ref, pair_ref,
    u_ref, packed_ref, first_ref, last_ref, xh_ref, xl_ref,
):
    rows = x_ref.shape[0]
    wide = low_ref.shape[0]
    count = rows // wide
    xh_ref[...], xl_ref[...] = split(x_ref[...])
    for c in range(count):
        here = slice(c * wide, (c + 1) * wide)
        out = coupled(d2_ref, xh_ref, xl_ref, here) + s_ref[here, :]
        out = with_edges(c, count, out, low_ref, high_ref, before_ref, after_ref)
        out = out / energy(virt_ref[here, :], kept_ref[...], pair_ref[...])
        u_ref[here, :] = out
        if c == 0:
            first_ref[...] = out
        if c == count - 1:
            last_ref[...] = out
    for t in range(x_ref.shape[1] // TW):
        turn(u_ref, packed_ref, t, nk)


def again_kernel(u_ref, s_ref, before_ref, after_ref, low_ref, high_ref, d2_ref, o_ref, xh_ref, xl_ref):
    wide = low_ref.shape[0]
    count = u_ref.shape[0] // wide
    xh_ref[...], xl_ref[...] = split(u_ref[...])
    for c in range(count):
        here = slice(c * wide, (c + 1) * wide)
        out = coupled(d2_ref, xh_ref, xl_ref, here) + s_ref[here, :]
        o_ref[here, :] = with_edges(c, count, out, low_ref, high_ref, before_ref, after_ref)


def ladder_kernel(nk, p_ref, kh_ref, kl_ref, row_ref, col_ref, pair_ref, w_ref, first_ref, last_ref):
    lines = w_ref.shape[0]
    tiles = first_ref.shape[1] // TW
    for k in range(nk):
        cols = slice(k * TW, (k + 1) * TW)
        x = split(p_ref[pl.ds(k, lines, stride=nk), :])
        out = three(dot_nn, kh_ref[...], kl_ref[...], *x)
        out = out / energy(row_ref[:, cols], col_ref[...], pair_ref[...])
        w_ref[:, cols] = out
        if k < tiles:
            first_ref[:, cols] = out
        if k >= nk - tiles:
            j = k - nk + tiles
            last_ref[:, j * TW : (j + 1) * TW] = out


def inner_kernel(wide, w_ref, d2_ref, kh_ref, kl_ref, o_ref, xh_ref, xl_ref):
    xh_ref[...], xl_ref[...] = split(w_ref[...])
    for c in range(w_ref.shape[1] // wide):
        cols = slice(c * wide, (c + 1) * wide)
        out = three(dot_nt, xh_ref[...], xl_ref[...], d2_ref[0, cols, :], d2_ref[1, cols, :])
        o_ref[:, cols] = out + three(dot_nn, kh_ref[...], kl_ref[...], xh_ref[:, cols], xl_ref[:, cols])


def outer_kernel(t_ref, before_ref, after_ref, low_ref, high_ref, o_ref):
    rows = t_ref.shape[1]
    wide = low_ref.shape[0]
    front = slice(0, wide)
    rear = slice(rows - wide, rows)
    o_ref[:, wide : rows - wide] = t_ref[:, wide : rows - wide]
    o_ref[:, front] = t_ref[:, front] + three(dot_nt, *split(before_ref[...]), *split(low_ref[...]))
    o_ref[:, rear] = t_ref[:, rear] + three(dot_nt, *split(after_ref[...]), *split(high_ref[...]))


def join_kernel(nk, p_ref, t_ref, kh_ref, kl_ref, o_ref):
    lines = t_ref.shape[0]
    for k in range(nk):
        here = pl.ds(k, lines, stride=nk)
        x = split(p_ref[here, :])
        o_ref[here, :] = three(dot_nn, kh_ref[...], kl_ref[...], *x) + t_ref[:, k * TW : (k + 1) * TW]


def last_kernel(p_ref, t_ref, virt_ref, kept_ref, pair_ref, o_hbm, o_ref, sems):
    rows, cols = t_ref.shape
    nk = rows // TW
    per = 2
    copies = []
    for k in range(nk):
        here = slice(k * TW, (k + 1) * TW)
        for t in range(cols // TW):
            lanes = slice(t * TW, (t + 1) * TW)
            out = t_ref[here, lanes] + p_ref[pl.ds(t * TW * nk + k, TW, stride=nk), :].T
            o_ref[here, lanes] = out / energy(virt_ref[here, :], kept_ref[:, lanes], pair_ref[...])
        if k % per == per - 1:
            done = slice((k + 1 - per) * TW, (k + 1) * TW)
            copies.append(pltpu.make_async_copy(o_ref.at[done, :], o_hbm.at[done, :], sems.at[k // per]))
            copies[-1].start()
    for copy in copies:
        copy.wait()


def call(name, kernel, args, shapes, flops, scratch=(), out_specs=None):
    size = sum(a.size * a.dtype.itemsize for a in (*args, *shapes))
    return pl.pallas_call(
        kernel,
        in_specs=[VMEM] * len(args),
        out_specs=out_specs or [VMEM] * len(shapes),
        out_shape=shapes,
        scratch_shapes=scratch,
        compiler_params=pltpu.CompilerParams(vmem_limit_bytes=LIMIT),
        cost_estimate=pl.CostEstimate(flops=flops, bytes_accessed=size, transcendentals=0),
        name=name,
    )(*args)


def exchange(first, last):
    count = lax.axis_size("virt")
    up = [(i, i + 1) for i in range(count - 1)]
    down = [(j, i) for i, j in up]
    before = lax.ppermute(last, "virt", up)
    after = lax.ppermute(first, "virt", down)
    return before, after


def local(
    amplitudes,
    source,
    diag_block,
    edge_low,
    edge_high,
    hole_coupling,
    pair_energy,
    virt_energy,
    column_tiles,
):
    rows, cols = amplitudes.shape[1:]
    width = edge_low.shape[0]
    pairs = pair_energy.shape[0]
    share = cols // pairs
    nk = rows // TW
    lines = pairs * share

    def shape(*dims, kind=F32):
        return jax.ShapeDtypeStruct(dims, kind)

    def spread(packed):
        out = lax.all_to_all(packed.reshape(pairs, share * nk, TW), "pair", split_axis=0, concat_axis=0, tiled=True)
        return out.reshape(lines * nk, TW)

    field = amplitudes[0]
    held = spread(pack(field))

    at = lax.axis_index("virt") * rows
    row = lax.dynamic_slice_in_dim(virt_energy, at, rows)
    mine = lax.dynamic_slice_in_dim(pair_energy, lax.axis_index("pair"), 1)
    kept = jnp.concatenate(
        [lax.dynamic_slice_in_dim(virt_energy, column_tiles[t] * TW, TW) for t in range(cols // TW)]
    )
    own_energy = (row[:, None], kept[None, :], mine[None, :])
    start = lax.axis_index("pair") * share
    col = jnp.broadcast_to(lax.dynamic_slice_in_dim(kept, start, share)[None, :], (pairs, share)).reshape(-1, 1)
    all_pairs = jnp.broadcast_to(pair_energy[:, None], (pairs, share)).reshape(-1, 1)
    energies = (row[None, :], col, all_pairs)

    d2, kh, kl = prep(diag_block, hole_coupling, share)
    most = 6 * lines * rows * rows
    pair_scratch = [pltpu.VMEM((rows, cols), BF)] * 2
    before, after = exchange(field[:width], field[rows - width :])
    u, packed, first, last = call(
        "own",
        functools.partial(own_kernel, nk),
        (field, source[0], before, after, edge_low, edge_high, d2, *own_energy),
        [shape(rows, cols), shape(cols * nk, TW), shape(width, cols), shape(width, cols)],
        most,
        pair_scratch,
    )
    held_u = spread(packed)
    u_before, u_after = exchange(first, last)

    w, first, last = call(
        "ladder",
        functools.partial(ladder_kernel, nk),
        (held, kh, kl, *energies),
        [shape(lines, rows), shape(lines, width), shape(lines, width)],
        most // 4,
    )
    before, after = exchange(first, last)
    (total,) = call(
        "inner",
        functools.partial(inner_kernel, width),
        (w, d2, kh, kl),
        [shape(lines, rows)],
        most + most // 4,
        [pltpu.VMEM((lines, rows), BF)] * 2,
    )
    (total,) = call("outer", outer_kernel, (total, before, after, edge_low, edge_high), [shape(lines, rows)], most // 8)
    (out,) = call(
        "join", functools.partial(join_kernel, nk), (held_u, total, kh, kl), [shape(lines * nk, TW)], most // 4
    )
    back = spread(out)
    (own,) = call(
        "again",
        again_kernel,
        (u, source[0], u_before, u_after, edge_low, edge_high, d2),
        [shape(rows, cols)],
        most,
        pair_scratch,
    )
    (out,) = call(
        "last",
        last_kernel,
        (back, own, *own_energy),
        [shape(rows, cols)],
        10 * rows * cols,
        [pltpu.VMEM((rows, cols), F32), pltpu.SemaphoreType.DMA((nk // 2,))],
        [HBM],
    )
    return out[None]


def solution(mesh):
    in_specs = (
        P("pair", "virt", None),
        P("pair", "virt", None),
        P("virt", None),
        P("virt", None),
        P("virt", None),
        P(),
        P(),
        P(),
        P(),
    )
    out_specs = P("pair", "virt", None)
    return jax.shard_map(local, mesh=mesh, in_specs=in_specs, out_specs=out_specs, check_vma=False)
```

time: 166 us -> 124 us (0.75)
  blocking collectives: 76.9 us -> 0 us
  matrix products: 21.8 us -> 0 us
  waiting for transfers between devices: 21.6 us -> 40.6 us
  Pallas kernels: 0 us -> 18.6 us
  starting transfers between devices: 24.3 us -> 40 us
  local copies, waits for them, and re-layouts: 16.6 us -> 22.7 us
  other arithmetic: 4.27 us -> 0.01 us
    all_to_all x2 -> x0, blocking collectives: 76.9 us -> none  [local(): lax.all_to_all(field, 'pair', split_axis=1, concat_axis=0, tiled=True)]
    dot_general x8 -> x0, matrix products: 21.8 us -> none  [the longest x2 14.4 us: couple_rows(): out = jnp.einsum('rc,pcn->prn', diag_block, field, precision=exact)]
    pallas_call x0 -> x9, Pallas kernels: none -> 18.6 us  [the longest x7 14.8 us: call(): pl.pallas_call(kernel, in_specs=[VMEM] * len(args), out_specs=out_specs o...]
    all_to_all x2 -> x3, starting transfers between devices: 12.7 us -> 28.8 us  [spread(): lax.all_to_all(packed.reshape(pairs, share * nk, TW), 'pair', split_axis=...]
    unnamed x20 -> x46, local copies, waits for them, and re-layouts: 4.26 us -> 18.6 us
    ppermute x4 -> x6, waiting for transfers between devices: 0.01 us -> 10.9 us  [the longest x3 6.39 us: exchange(): after = lax.ppermute(first, 'virt', down)]
    all_to_all x2 -> x3, waiting for transfers between devices: 21.5 us -> 29.7 us  [spread(): lax.all_to_all(packed.reshape(pairs, share * nk, TW), 'pair', split_axis=...]
    div x2 -> x0, other arithmetic: 4.19 us -> none  [local(): field = (source + banded + hole) / denom]
  transfers between devices with their start and end apart: 6 -> 9, of which waited for: 2 -> 6; matrix products, arithmetic and copies ran while one was open for 14% -> 3% of each run, Pallas kernels for 0% -> 9%
where the time goes in v3:
time: 124 us; the launch traced here: 123 us
  waiting for transfers between devices  40.6 us (33%)
  starting transfers between devices  40 us (32%)
  local copies, waits for them, and re-layouts  22.7 us (18%)
  Pallas kernels  18.6 us (15%)
  between operations  1.53 us (1%)
    all_to_all x3, waiting for transfers between devices, spread(): lax.all_to_all(packed.reshape(pairs, share * nk, TW), 'pair', split_axis=...  29.7 us
    all_to_all x3, starting transfers between devices, spread(): lax.all_to_all(packed.reshape(pairs, share * nk, TW), 'pair', split_axis=...  28.8 us
    unnamed x46, local copies, waits for them, and re-layouts  18.6 us
    pallas_call x7, Pallas kernels, call(): pl.pallas_call(kernel, in_specs=[VMEM] * len(args), out_specs=out_specs o...  14.8 us
    ppermute x3, starting transfers between devices, exchange(): before = lax.ppermute(last, 'virt', up)  7.31 us
    ppermute x3, waiting for transfers between devices, exchange(): after = lax.ppermute(first, 'virt', down)  6.39 us
    ppermute x3, waiting for transfers between devices, exchange(): before = lax.ppermute(last, 'virt', up)  4.53 us
    ppermute x3, starting transfers between devices, exchange(): after = lax.ppermute(first, 'virt', down)  3.86 us
  transfers between devices with their start and end apart: 9, of which 6 were waited for; matrix products, arithmetic and copies ran while one was open for 3% of the time, Pallas kernels for 9%

profile of v3, /device:TPU:1, one launch (start us, length us, event | category | flops | bytes accessed | tf_op | source)
XLA Modules:
  0.0 123.4 jit_solution(16775966249774738861)
XLA Ops:
  0.0 2.4 %pack.1 = f32[2048,128]{1,0:T(8,128)} custom-call(f32[1024,256]{1,0:T(8,128)} %bitcast.19), custom_call_target="tpu_custom_call" | custom-call | tf_op jit(solution)/shard_map/pack/pallas_call | solution.py:64
  2.4 14.7 %all-to-all-start.1 = ((f32[64,32,128]{2,1,0:T(8,128)}), f32[64,32,128]{2,1,0:T(8,128)S(1)}, u32[]{:S(2)}, u32[]{:S(2)}) async-start(f32[64,32,128]{2,1,0:T(8,128)} %bitcast.30), calls=%async_computation.1 | async-start | bytes 2097152 | tf_op jit(solution)/shard_map/all_to_all | solution.py:265
  17.2 0.8 slice_bitcast_fusion
  18.0 1.3 %collective-permute-start.1 = (f32[256,256]{1,0:T(8,128)}, f32[256,256]{1,0:T(8,128)S(1)}, u32[]{:S(2)}, u32[]{:S(2)}) collective-permute-start(f32[256,256]{1,0:T(8,128)} %get-tuple-element.25), channel_id=1, source_target_pairs={{1,0},{2,1},{3,2},{4,3},{5,4},{6,5},{7,6},{8,7},{9,8},{10,9},{11,1... | collective-permute-start | bytes 786440 | tf_op jit(solution)/shard_map/ppermute | solution.py:239
  19.3 4.7 %collective-permute-start = (f32[256,256]{1,0:T(8,128)}, f32[256,256]{1,0:T(8,128)}, u32[]{:S(2)}, u32[]{:S(2)}) collective-permute-start(f32[256,256]{1,0:T(8,128)} %get-tuple-element.26), channel_id=1, source_target_pairs={{0,1},{1,2},{2,3},{3,4},{4,5},{5,6},{6,7},{7,8},{8,9},{9,10},{10,1... | collective-permute-start | bytes 786440 | tf_op jit(solution)/shard_map/ppermute | solution.py:238
  24.0 0.6 fusion.1
  25.9 0.7 dynamic_slice.15
  26.6 0.2 copy.10.virt_ref
  26.8 0.6 dynamic_slice.18
  27.4 2.2 %copy-done.4 = f32[1024,1024]{1,0:T(8,128)S(1)} copy-done((f32[1024,1024]{1,0:T(8,128)S(1)}, f32[1024,1024]{1,0:T(8,128)}, u32[]{:S(2)}) %copy-start.4) | copy-done | bytes 4194328
  29.6 0.8 copy-done.18
  30.4 1.4 %prep.1 = (bf16[2,1024,1024]{2,1,0:T(8,128)(2,1)S(1)}, bf16[256,256]{1,0:T(8,128)(2,1)S(1)}, bf16[256,256]{1,0:T(8,128)(2,1)S(1)}) custom-call(f32[1024,1024]{1,0:T(8,128)S(1)} %copy-done.4, f32[64,64]{1,0:T(8,128)S(1)} %copy-done.18), custom_call_target="tpu_custom_call" | custom-call | flops 8388608 | bytes 8388608 | tf_op jit(solution)/shard_map/prep/pallas_call | solution.py:97
  31.8 0.6 copy-done.14
  32.5 0.8 fusion
  33.3 3.8 %own.1 = (f32[1024,256]{1,0:T(8,128)S(1)}, f32[2048,128]{1,0:T(8,128)S(1)}, f32[256,256]{1,0:T(8,128)S(1)}, f32[256,256]{1,0:T(8,128)S(1)}) custom-call(f32[1024,256]{1,0:T(8,128)S(1)} %bitcast.20, f32[1024,256]{1,0:T(8,128)S(1)} %bitcast.23, f32[256,256]{1,0:T(8,128)} %collective-permute-done.before_ref, f32[256,256]{1,0:T(8,128)S(1)} %collective-permute-done.1.after_ref, ...), custom_call_target="tpu_custom_call" | custom-call | flops 1610612736 | bytes 9966596 | tf_op jit(solution)/shard_map/own/pallas_call | solution.py:222
  37.1 2.0 %copy-done = bf16[2,1024,1024]{2,1,0:T(8,128)(2,1)} copy-done((bf16[2,1024,1024]{2,1,0:T(8,128)(2,1)}, bf16[2,1024,1024]{2,1,0:T(8,128)(2,1)S(1)}, u32[]{:S(2)}) %copy-start) | copy-done | bytes 4194328
  39.1 1.0 copy-done.11
  40.0 1.0 copy-done.12
  41.0 0.7 copy-done.19
  41.7 0.7 copy-done.20
  42.5 3.3 %all-to-all-done.1 = f32[64,32,128]{2,1,0:T(8,128)S(1)} async-done(((f32[64,32,128]{2,1,0:T(8,128)}), f32[64,32,128]{2,1,0:T(8,128)S(1)}, u32[]{:S(2)}, u32[]{:S(2)}) %all-to-all-start.1) | async-done | bytes 1048608 | tf_op jit(solution)/shard_map/all_to_all | solution.py:265
  45.8 7.9 %all-to-all-start = ((f32[64,32,128]{2,1,0:T(8,128)}), f32[64,32,128]{2,1,0:T(8,128)}, u32[]{:S(2)}, u32[]{:S(2)}) async-start(f32[64,32,128]{2,1,0:T(8,128)} %bitcast.25), calls=%async_computation | async-start | bytes 2097152 | tf_op jit(solution)/shard_map/all_to_all | solution.py:265
  53.7 0.1 dynamic_slice.19
  53.8 0.1 reshape.41.pair_ref
  53.9 0.1 reshape.40.col_ref
  54.0 0.9 copy-done.15
  54.9 1.1 ladder.1
  56.0 1.3 %collective-permute-start.2 = (f32[256,256]{1,0:T(8,128)S(1)}, f32[256,256]{1,0:T(8,128)S(1)}, u32[]{:S(2)}, u32[]{:S(2)}) collective-permute-start(f32[256,256]{1,0:T(8,128)S(1)} %get-tuple-element.20), channel_id=1, source_target_pairs={{0,1},{1,2},{2,3},{3,4},{4,5},{5,6},{6,7},{7,8},{8,9},{9,10},{10,1... | collective-permute-start | bytes 786440 | tf_op jit(solution)/shard_map/ppermute | solution.py:238
  57.3 1.3 %collective-permute-start.3 = (f32[256,256]{1,0:T(8,128)S(1)}, f32[256,256]{1,0:T(8,128)S(1)}, u32[]{:S(2)}, u32[]{:S(2)}) collective-permute-start(f32[256,256]{1,0:T(8,128)S(1)} %get-tuple-element.21), channel_id=1, source_target_pairs={{1,0},{2,1},{3,2},{4,3},{5,4},{6,5},{7,6},{8,7},{9,8},{10,9},{11,1... | collective-permute-start | bytes 786440 | tf_op jit(solution)/shard_map/ppermute | solution.py:239
  58.6 2.2 %copy-done.1 = bf16[2,1024,1024]{2,1,0:T(8,128)(2,1)S(1)} copy-done((bf16[2,1024,1024]{2,1,0:T(8,128)(2,1)S(1)}, bf16[2,1024,1024]{2,1,0:T(8,128)(2,1)}, u32[]{:S(2)}) %copy-start.1) | copy-done | bytes 4194328
  60.8 0.9 copy-done.16
  61.7 2.2 %inner.1.t_ref = f32[256,1024]{1,0:T(8,128)S(1)} custom-call(f32[256,1024]{1,0:T(8,128)S(1)} %get-tuple-element.19.w_ref, bf16[2,1024,1024]{2,1,0:T(8,128)(2,1)S(1)} %copy-done.1, bf16[256,256]{1,0:T(8,128)(2,1)S(1)} %get-tuple-element.17.kh_ref, bf16[256,256]{1,0:T(8,128)(2,1)S(1)} %copy-done.16), custom_call_target="tpu_custom_call" | custom-call | flops 2013265920 | bytes 6553600 | tf_op jit(solution)/shard_map/inner/pallas_call | solution.py:222
  63.9 2.7 %collective-permute-done.3.after_ref = f32[256,256]{1,0:T(8,128)S(1)} collective-permute-done((f32[256,256]{1,0:T(8,128)S(1)}, f32[256,256]{1,0:T(8,128)S(1)}, u32[]{:S(2)}, u32[]{:S(2)}) %collective-permute-start.3) | collective-permute-done | bytes 262176 | tf_op jit(solution)/shard_map/ppermute | solution.py:239
  66.6 0.4 outer.1.t_ref
  67.1 15.1 %all-to-all-done = f32[64,32,128]{2,1,0:T(8,128)} async-done(((f32[64,32,128]{2,1,0:T(8,128)}), f32[64,32,128]{2,1,0:T(8,128)}, u32[]{:S(2)}, u32[]{:S(2)}) %all-to-all-start) | async-done | bytes 1048608 | tf_op jit(solution)/shard_map/all_to_all | solution.py:265
  82.1 3.2 %join.1 = f32[2048,128]{1,0:T(8,128)} custom-call(f32[2048,128]{1,0:T(8,128)} %bitcast.10.p_ref, f32[256,1024]{1,0:T(8,128)S(1)} %outer.1.t_ref, bf16[256,256]{1,0:T(8,128)(2,1)S(1)} %get-tuple-element.17.kh_ref, bf16[256,256]{1,0:T(8,128)(2,1)S(1)} %copy-done.17), custom_call_target="tpu_custom_call" | custom-call | flops 402653184 | bytes 3407872 | tf_op jit(solution)/shard_map/join/pallas_call | solution.py:222
  85.3 6.2 %all-to-all-start.2 = ((f32[64,32,128]{2,1,0:T(8,128)}), f32[64,32,128]{2,1,0:T(8,128)S(1)}, u32[]{:S(2)}, u32[]{:S(2)}) async-start(f32[64,32,128]{2,1,0:T(8,128)} %bitcast.14), calls=%async_computation.2 | async-start | bytes 2097152 | tf_op jit(solution)/shard_map/all_to_all | solution.py:265
  91.5 1.3 %collective-permute-start.4 = (f32[256,256]{1,0:T(8,128)}, f32[256,256]{1,0:T(8,128)S(1)}, u32[]{:S(2)}, u32[]{:S(2)}) collective-permute-start(f32[256,256]{1,0:T(8,128)} %copy-done.20), channel_id=1, source_target_pairs={{0,1},{1,2},{2,3},{3,4},{4,5},{5,6},{6,7},{7,8},{8,9},{9,10},{10,1... | collective-permute-start | bytes 786440 | tf_op jit(solution)/shard_map/ppermute | solution.py:238
  92.9 1.3 %collective-permute-start.5 = (f32[256,256]{1,0:T(8,128)}, f32[256,256]{1,0:T(8,128)S(1)}, u32[]{:S(2)}, u32[]{:S(2)}) collective-permute-start(f32[256,256]{1,0:T(8,128)} %copy-done.19), channel_id=1, source_target_pairs={{1,0},{2,1},{3,2},{4,3},{5,4},{6,5},{7,6},{8,7},{9,8},{10,9},{11,1... | collective-permute-start | bytes 786440 | tf_op jit(solution)/shard_map/ppermute | solution.py:239
  94.2 4.5 %collective-permute-done.4.before_ref = f32[256,256]{1,0:T(8,128)S(1)} collective-permute-done((f32[256,256]{1,0:T(8,128)}, f32[256,256]{1,0:T(8,128)S(1)}, u32[]{:S(2)}, u32[]{:S(2)}) %collective-permute-start.4) | collective-permute-done | bytes 262176 | tf_op jit(solution)/shard_map/ppermute | solution.py:238
  98.7 3.7 %collective-permute-done.5.after_ref = f32[256,256]{1,0:T(8,128)S(1)} collective-permute-done((f32[256,256]{1,0:T(8,128)}, f32[256,256]{1,0:T(8,128)S(1)}, u32[]{:S(2)}, u32[]{:S(2)}) %collective-permute-start.5) | collective-permute-done | bytes 262176 | tf_op jit(solution)/shard_map/ppermute | solution.py:239
  102.4 2.2 %copy-done.2 = bf16[2,1024,1024]{2,1,0:T(8,128)(2,1)S(1)} copy-done((bf16[2,1024,1024]{2,1,0:T(8,128)(2,1)S(1)}, bf16[2,1024,1024]{2,1,0:T(8,128)(2,1)}, u32[]{:S(2)}) %copy-start.2) | copy-done | bytes 4194328
  104.6 1.2 copy-done.13
  105.8 2.0 %again.1.t_ref = f32[1024,256]{1,0:T(8,128)S(1)} custom-call(f32[1024,256]{1,0:T(8,128)S(1)} %copy-done.13, f32[1024,256]{1,0:T(8,128)S(1)} %bitcast.24, f32[256,256]{1,0:T(8,128)S(1)} %collective-permute-done.4.before_ref, f32[256,256]{1,0:T(8,128)S(1)} %collective-permute-done.5.after_ref, f32[256,256]{1,0:T(8,128)S(1)} %copy-done.9, ...), custom_call_target="tpu_custom_call" | custom-call | flops 1610612736 | bytes 8388608 | tf_op jit(solution)/shard_map/again/pallas_call | solution.py:222
  107.8 1.0 copy-done.7
  108.8 11.3 %all-to-all-done.2 = f32[64,32,128]{2,1,0:T(8,128)S(1)} async-done(((f32[64,32,128]{2,1,0:T(8,128)}), f32[64,32,128]{2,1,0:T(8,128)S(1)}, u32[]{:S(2)}, u32[]{:S(2)}) %all-to-all-start.2) | async-done | bytes 1048608 | tf_op jit(solution)/shard_map/all_to_all | solution.py:265
  120.1 1.2 copy-done.8
  121.3 2.1 %last.1 = f32[1024,256]{1,0:T(8,128)} custom-call(f32[2048,128]{1,0:T(8,128)S(1)} %bitcast.21, f32[1024,256]{1,0:T(8,128)S(1)} %copy-done.8, f32[1024,1]{1,0:T(8,128)S(1)} %copy.10.virt_ref, f32[1,256]{1,0:T(1,128)S(1)} %bitcast.29, f32[1,1]{1,0:T(1,128)} %bitcast.8.pair_ref), custom_call_target="tpu_custom_call" | custom-call | flops 2621440 | bytes 3150852 | tf_op jit(solution)/shard_map/last/pallas_call | solution.py:222
  (37 shorter events, 0.2 us)
Async XLA Ops:
  0.0 17.2 %copy-start.3 = (f32[1,1024,256]{2,1,0:T(8,128)S(1)}, f32[1,1024,256]{2,1,0:T(8,128)}, u32[]{:S(2)}) copy-start(f32[1,1024,256]{2,1,0:T(8,128)} %param.9) | copy-start | bytes 3145732
  0.0 24.0 %copy-start.21 = (s32[2]{0:T(128)S(1)}, s32[2]{0:T(128)}, u32[]{:S(2)}) copy-start(s32[2]{0:T(128)} %param.17) | copy-start | bytes 28
  0.0 26.8 %copy-start.22 = (f32[64]{0:T(128)S(1)}, f32[64]{0:T(128)}, u32[]{:S(2)}) copy-start(f32[64]{0:T(128)} %param.15) | copy-start | bytes 772
  2.4 30.9 %copy-start.9 = (f32[256,256]{1,0:T(8,128)S(1)}, f32[256,256]{1,0:T(8,128)}, u32[]{:S(2)}) copy-start(f32[256,256]{1,0:T(8,128)} %low_ref.5) | copy-start | bytes 786436
  2.4 30.9 %copy-start.10 = (f32[256,256]{1,0:T(8,128)S(1)}, f32[256,256]{1,0:T(8,128)}, u32[]{:S(2)}) copy-start(f32[256,256]{1,0:T(8,128)} %high_ref.5) | copy-start | bytes 786436
  2.4 43.3 %all-to-all-start.1 = ((f32[64,32,128]{2,1,0:T(8,128)}), f32[64,32,128]{2,1,0:T(8,128)S(1)}, u32[]{:S(2)}, u32[]{:S(2)}) async-start(f32[64,32,128]{2,1,0:T(8,128)} %bitcast.30), calls=%async_computation.1 | async-start | bytes 2097152 | tf_op jit(solution)/shard_map/all_to_all | solution.py:265
  18.0 15.2 %collective-permute-start.1 = (f32[256,256]{1,0:T(8,128)}, f32[256,256]{1,0:T(8,128)S(1)}, u32[]{:S(2)}, u32[]{:S(2)}) collective-permute-start(f32[256,256]{1,0:T(8,128)} %get-tuple-element.25), channel_id=1, source_target_pairs={{1,0},{2,1},{3,2},{4,3},{5,4},{6,5},{7,6},{8,7},{9,8},{10,9},{11,1... | collective-permute-start | bytes 786440 | tf_op jit(solution)/shard_map/ppermute | solution.py:239
  19.3 13.9 %collective-permute-start = (f32[256,256]{1,0:T(8,128)}, f32[256,256]{1,0:T(8,128)}, u32[]{:S(2)}, u32[]{:S(2)}) collective-permute-start(f32[256,256]{1,0:T(8,128)} %get-tuple-element.26), channel_id=1, source_target_pairs={{0,1},{1,2},{2,3},{3,4},{4,5},{5,6},{6,7},{7,8},{8,9},{9,10},{10,1... | collective-permute-start | bytes 786440 | tf_op jit(solution)/shard_map/ppermute | solution.py:238
  27.4 2.2 %copy-start.4 = (f32[1024,1024]{1,0:T(8,128)S(1)}, f32[1024,1024]{1,0:T(8,128)}, u32[]{:S(2)}) copy-start(f32[1024,1024]{1,0:T(8,128)} %d_ref.1) | copy-start | bytes 12582916
  29.6 0.8 copy-start.18
  30.4 2.9 %copy-start.5 = (f32[1,1024,256]{2,1,0:T(8,128)S(1)}, f32[1,1024,256]{2,1,0:T(8,128)}, u32[]{:S(2)}) copy-start(f32[1,1024,256]{2,1,0:T(8,128)} %param.10) | copy-start | bytes 3145732
  31.8 0.7 copy-start.14
  37.1 2.0 %copy-start = (bf16[2,1024,1024]{2,1,0:T(8,128)(2,1)}, bf16[2,1024,1024]{2,1,0:T(8,128)(2,1)S(1)}, u32[]{:S(2)}) copy-start(bf16[2,1024,1024]{2,1,0:T(8,128)(2,1)S(1)} %get-tuple-element.15.d2_ref) | copy-start | bytes 12582916
  39.1 1.0 copy-start.11
  40.0 1.0 copy-start.12
  41.0 0.7 copy-start.19
  41.7 0.7 copy-start.20
  45.8 36.4 %all-to-all-start = ((f32[64,32,128]{2,1,0:T(8,128)}), f32[64,32,128]{2,1,0:T(8,128)}, u32[]{:S(2)}, u32[]{:S(2)}) async-start(f32[64,32,128]{2,1,0:T(8,128)} %bitcast.25), calls=%async_computation | async-start | bytes 2097152 | tf_op jit(solution)/shard_map/all_to_all | solution.py:265
  54.0 0.9 copy-start.15
  56.0 8.0 %collective-permute-start.2 = (f32[256,256]{1,0:T(8,128)S(1)}, f32[256,256]{1,0:T(8,128)S(1)}, u32[]{:S(2)}, u32[]{:S(2)}) collective-permute-start(f32[256,256]{1,0:T(8,128)S(1)} %get-tuple-element.20), channel_id=1, source_target_pairs={{0,1},{1,2},{2,3},{3,4},{4,5},{5,6},{6,7},{7,8},{8,9},{9,10},{10,1... | collective-permute-start | bytes 786440 | tf_op jit(solution)/shard_map/ppermute | solution.py:238
  57.3 9.3 %collective-permute-start.3 = (f32[256,256]{1,0:T(8,128)S(1)}, f32[256,256]{1,0:T(8,128)S(1)}, u32[]{:S(2)}, u32[]{:S(2)}) collective-permute-start(f32[256,256]{1,0:T(8,128)S(1)} %get-tuple-element.21), channel_id=1, source_target_pairs={{1,0},{2,1},{3,2},{4,3},{5,4},{6,5},{7,6},{8,7},{9,8},{10,9},{11,1... | collective-permute-start | bytes 786440 | tf_op jit(solution)/shard_map/ppermute | solution.py:239
  58.6 2.2 %copy-start.1 = (bf16[2,1024,1024]{2,1,0:T(8,128)(2,1)S(1)}, bf16[2,1024,1024]{2,1,0:T(8,128)(2,1)}, u32[]{:S(2)}) copy-start(bf16[2,1024,1024]{2,1,0:T(8,128)(2,1)} %copy-done) | copy-start | bytes 12582916
  60.8 0.9 copy-start.16
  61.7 20.4 %copy-start.17 = (bf16[256,256]{1,0:T(8,128)(2,1)S(1)}, bf16[256,256]{1,0:T(8,128)(2,1)}, u32[]{:S(2)}) copy-start(bf16[256,256]{1,0:T(8,128)(2,1)} %copy-done.14) | copy-start | bytes 393220
  63.9 38.5 %copy-start.6 = (f32[1,1024,256]{2,1,0:T(8,128)S(1)}, f32[1,1024,256]{2,1,0:T(8,128)}, u32[]{:S(2)}) copy-start(f32[1,1024,256]{2,1,0:T(8,128)} %param.10) | copy-start | bytes 3145732
  85.3 34.8 %all-to-all-start.2 = ((f32[64,32,128]{2,1,0:T(8,128)}), f32[64,32,128]{2,1,0:T(8,128)S(1)}, u32[]{:S(2)}, u32[]{:S(2)}) async-start(f32[64,32,128]{2,1,0:T(8,128)} %bitcast.14), calls=%async_computation.2 | async-start | bytes 2097152 | tf_op jit(solution)/shard_map/all_to_all | solution.py:265
  91.5 7.1 %collective-permute-start.4 = (f32[256,256]{1,0:T(8,128)}, f32[256,256]{1,0:T(8,128)S(1)}, u32[]{:S(2)}, u32[]{:S(2)}) collective-permute-start(f32[256,256]{1,0:T(8,128)} %copy-done.20), channel_id=1, source_target_pairs={{0,1},{1,2},{2,3},{3,4},{4,5},{5,6},{6,7},{7,8},{8,9},{9,10},{10,1... | collective-permute-start | bytes 786440 | tf_op jit(solution)/shard_map/ppermute | solution.py:238
  92.9 9.5 %collective-permute-start.5 = (f32[256,256]{1,0:T(8,128)}, f32[256,256]{1,0:T(8,128)S(1)}, u32[]{:S(2)}, u32[]{:S(2)}) collective-permute-start(f32[256,256]{1,0:T(8,128)} %copy-done.19), channel_id=1, source_target_pairs={{1,0},{2,1},{3,2},{4,3},{5,4},{6,5},{7,6},{8,7},{9,8},{10,9},{11,1... | collective-permute-start | bytes 786440 | tf_op jit(solution)/shard_map/ppermute | solution.py:239
  102.4 2.2 %copy-start.2 = (bf16[2,1024,1024]{2,1,0:T(8,128)(2,1)S(1)}, bf16[2,1024,1024]{2,1,0:T(8,128)(2,1)}, u32[]{:S(2)}) copy-start(bf16[2,1024,1024]{2,1,0:T(8,128)(2,1)} %copy-done) | copy-start | bytes 12582916
  104.6 1.2 copy-start.13
  107.8 1.0 copy-start.7
  120.1 1.2 copy-start.8

commit v4 on v3

--- a/solution.py
+++ b/solution.py
@@ -73,8 +73,7 @@
     )(a)
 
 
-def prep_kernel(share, d_ref, l_ref, d2_ref, kh_ref, kl_ref):
-    d2_ref[0], d2_ref[1] = split(d_ref[...])
+def prep_kernel(share, l_ref, kh_ref, kl_ref):
     pairs = l_ref.shape[0]
     size = pairs * share
     spread = (
@@ -91,29 +90,8 @@
         ref[...] = jnp.where(same, wide, 0.0).astype(BF)
 
 
-def prep(d, l, share):
-    rows = d.shape[0]
-    size = l.shape[0] * share
-    return pl.pallas_call(
-        functools.partial(prep_kernel, share),
-        in_specs=[VMEM] * 2,
-        out_specs=[VMEM] * 3,
-        out_shape=[jax.ShapeDtypeStruct((2, rows, rows), BF)]
-        + [jax.ShapeDtypeStruct((size, size), BF)] * 2,
-        compiler_params=pltpu.CompilerParams(vmem_limit_bytes=LIMIT),
-        cost_estimate=pl.CostEstimate(
-            flops=8 * rows * rows, bytes_accessed=8 * rows * rows, transcendentals=0
-        ),
-        name="prep",
-    )(d, l)
-
-
 def energy(row, col, pair):
     return row + col - pair
-
-
-def coupled(d2_ref, xh_ref, xl_ref, rows):
-    return three(dot_nn, d2_ref[0, rows, :], d2_ref[1, rows, :], xh_ref[...], xl_ref[...])
 
 
 def with_edges(c, count, out, low_ref, high_ref, before_ref, after_ref):
@@ -125,25 +103,72 @@
 
 
 def own_kernel(
-    nk, x_ref, s_ref, before_ref, after_ref, low_ref, high_ref, d2_ref, virt_ref, kept_ref, pair_ref,
-    u_ref, packed_ref, first_ref, last_ref, xh_ref, xl_ref,
+    x_hbm, s_hbm, d_hbm, y_hbm, d2_hbm, x_ref, s_ref, d_ref, xh_ref, xl_ref, d2_ref, y_ref, in_sems, out_sems
 ):
     rows = x_ref.shape[0]
-    wide = low_ref.shape[0]
-    count = rows // wide
+    count = in_sems.shape[0] - 2
+    wide = rows // count
+    arrays = [pltpu.make_async_copy(x_hbm, x_ref, in_sems.at[0]), pltpu.make_async_copy(s_hbm, s_ref, in_sems.at[1])]
+    arrays[0].start()
+    parts = []
+    for c in range(count):
+        here = slice(c * wide, (c + 1) * wide)
+        parts.append(pltpu.make_async_copy(d_hbm.at[here, :], d_ref.at[here, :], in_sems.at[2 + c]))
+        parts[c].start()
+        if c == 0:
+            arrays[1].start()
+    sent = []
+    arrays[0].wait()
     xh_ref[...], xl_ref[...] = split(x_ref[...])
     for c in range(count):
         here = slice(c * wide, (c + 1) * wide)
-        out = coupled(d2_ref, xh_ref, xl_ref, here) + s_ref[here, :]
-        out = with_edges(c, count, out, low_ref, high_ref, before_ref, after_ref)
-        out = out / energy(virt_ref[here, :], kept_ref[...], pair_ref[...])
-        u_ref[here, :] = out
+        parts[c].wait()
+        d2_ref[0, here, :], d2_ref[1, here, :] = split(d_ref[here, :])
+        sent.append(pltpu.make_async_copy(d2_ref.at[:, here, :], d2_hbm.at[:, here, :], out_sems.at[0, c]))
+        sent[-1].start()
         if c == 0:
-            first_ref[...] = out
-        if c == count - 1:
-            last_ref[...] = out
-    for t in range(x_ref.shape[1] // TW):
+            arrays[1].wait()
+        out = three(dot_nn, d2_ref[0, here, :], d2_ref[1, here, :], xh_ref[...], xl_ref[...])
+        y_ref[here, :] = out + s_ref[here, :]
+        sent.append(pltpu.make_async_copy(y_ref.at[here, :], y_hbm.at[here, :], out_sems.at[1, c]))
+        sent[-1].start()
+    for copy in sent:
+        copy.wait()
+
+
+def ready_kernel(
+    nk, y_hbm, before_ref, after_ref, low_ref, high_ref, virt_ref, kept_ref, pair_ref,
+    u_hbm, packed_hbm, first_hbm, last_hbm, y_ref, u_ref, packed_ref, in_sems, out_sems,
+):
+    rows, cols = u_ref.shape
+    wide = low_ref.shape[0]
+    count = rows // wide
+    got = []
+    for c in range(count):
+        here = slice(c * wide, (c + 1) * wide)
+        got.append(pltpu.make_async_copy(y_hbm.at[here, :], y_ref.at[here, :], in_sems.at[c]))
+        got[c].start()
+    sent = []
+
+    def send(source, target):
+        copy = pltpu.make_async_copy(source, target, out_sems.at[len(sent)])
+        copy.start()
+        sent.append(copy)
+
+    for c in range(count):
+        here = slice(c * wide, (c + 1) * wide)
+        got[c].wait()
+        out = with_edges(c, count, y_ref[here, :], low_ref, high_ref, before_ref, after_ref)
+        u_ref[here, :] = out / energy(virt_ref[here, :], kept_ref[...], pair_ref[...])
+    for t in range(cols // TW):
         turn(u_ref, packed_ref, t, nk)
+        here = slice(t * TW * nk, (t + 1) * TW * nk)
+        send(packed_ref.at[here, :], packed_hbm.at[here, :])
+    send(u_ref, u_hbm)
+    send(u_ref.at[:wide, :], first_hbm)
+    send(u_ref.at[rows - wide :, :], last_hbm)
+    for copy in sent:
+        copy.wait()
 
 
 def again_kernel(u_ref, s_ref, before_ref, after_ref, low_ref, high_ref, d2_ref, o_ref, xh_ref, xl_ref):
@@ -152,7 +177,8 @@
     xh_ref[...], xl_ref[...] = split(u_ref[...])
     for c in range(count):
         here = slice(c * wide, (c + 1) * wide)
-        out = coupled(d2_ref, xh_ref, xl_ref, here) + s_ref[here, :]
+        out = three(dot_nn, d2_ref[0, here, :], d2_ref[1, here, :], xh_ref[...], xl_ref[...])
+        out += s_ref[here, :]
         o_ref[here, :] = with_edges(c, count, out, low_ref, high_ref, before_ref, after_ref)
 
 
@@ -190,7 +216,8 @@
     o_ref[:, rear] = t_ref[:, rear] + three(dot_nt, *split(after_ref[...]), *split(high_ref[...]))
 
 
-def join_kernel(nk, p_ref, t_ref, kh_ref, kl_ref, o_ref):
+def join_kernel(nk, share, p_ref, t_ref, l_ref, o_ref, kh_ref, kl_ref):
+    prep_kernel(share, l_ref, kh_ref, kl_ref)
     lines = t_ref.shape[0]
     for k in range(nk):
         here = pl.ds(k, lines, stride=nk)
@@ -217,15 +244,15 @@
         copy.wait()
 
 
-def call(name, kernel, args, shapes, flops, scratch=(), out_specs=None):
+def call(name, kernel, args, shapes, flops, scratch=(), out_specs=None, hbm=(), limit=LIMIT):
     size = sum(a.size * a.dtype.itemsize for a in (*args, *shapes))
     return pl.pallas_call(
         kernel,
-        in_specs=[VMEM] * len(args),
+        in_specs=[HBM if i in hbm else VMEM for i in range(len(args))],
         out_specs=out_specs or [VMEM] * len(shapes),
         out_shape=shapes,
         scratch_shapes=scratch,
-        compiler_params=pltpu.CompilerParams(vmem_limit_bytes=LIMIT),
+        compiler_params=pltpu.CompilerParams(vmem_limit_bytes=limit),
         cost_estimate=pl.CostEstimate(flops=flops, bytes_accessed=size, transcendentals=0),
         name=name,
     )(*args)
@@ -280,17 +307,50 @@
     all_pairs = jnp.broadcast_to(pair_energy[:, None], (pairs, share)).reshape(-1, 1)
     energies = (row[None, :], col, all_pairs)
 
-    d2, kh, kl = prep(diag_block, hole_coupling, share)
+    kh, kl = call(
+        "prep", functools.partial(prep_kernel, share), (hole_coupling,), [shape(lines, lines, kind=BF)] * 2, lines**3
+    )
     most = 6 * lines * rows * rows
     pair_scratch = [pltpu.VMEM((rows, cols), BF)] * 2
     before, after = exchange(field[:width], field[rows - width :])
+    matrix = pltpu.VMEM((rows, cols), F32)
+    parts = rows // width
+    y, d2 = call(
+        "own",
+        own_kernel,
+        (field, source[0], diag_block),
+        [shape(rows, cols), shape(2, rows, rows, kind=BF)],
+        most,
+        [
+            matrix,
+            matrix,
+            pltpu.VMEM((rows, rows), F32),
+            *pair_scratch,
+            pltpu.VMEM((2, rows, rows), BF),
+            matrix,
+            pltpu.SemaphoreType.DMA((2 + parts,)),
+            pltpu.SemaphoreType.DMA((2, parts)),
+        ],
+        [HBM] * 2,
+        (0, 1, 2),
+        60 * 1024 * 1024,
+    )
     u, packed, first, last = call(
-        "own",
-        functools.partial(own_kernel, nk),
-        (field, source[0], before, after, edge_low, edge_high, d2, *own_energy),
+        "ready",
+        functools.partial(ready_kernel, nk),
+        (y, before, after, edge_low, edge_high, *own_energy),
         [shape(rows, cols), shape(cols * nk, TW), shape(width, cols), shape(width, cols)],
-        most,
-        pair_scratch,
+        most // 8,
+        [
+            matrix,
+            matrix,
+            pltpu.VMEM((cols * nk, TW), F32),
+            pltpu.SemaphoreType.DMA((parts,)),
+            pltpu.SemaphoreType.DMA((3 + cols // TW,)),
+        ],
+        [HBM] * 4,
+        (0,),
+        60 * 1024 * 1024,
     )
     held_u = spread(packed)
     u_before, u_after = exchange(first, last)
@@ -313,7 +373,12 @@
     )
     (total,) = call("outer", outer_kernel, (total, before, after, edge_low, edge_high), [shape(lines, rows)], most // 8)
     (out,) = call(
-        "join", functools.partial(join_kernel, nk), (held_u, total, kh, kl), [shape(lines * nk, TW)], most // 4
+        "join",
+        functools.partial(join_kernel, nk, share),
+        (held_u, total, hole_coupling),
+        [shape(lines * nk, TW)],
+        most // 4,
+        [pltpu.VMEM((lines, lines), BF)] * 2,
     )
     back = spread(out)
     (own,) = call(

time: 124 us -> 121 us (0.976)
  local copies, waits for them, and re-layouts: 22.7 us -> 11.9 us
  Pallas kernels: 18.6 us -> 25 us
  waiting for transfers between devices: 40.6 us -> 42.2 us
    unnamed x46 -> x30, local copies, waits for them, and re-layouts: 18.6 us -> 7.68 us
    pallas_call x8 -> x9, Pallas kernels: 16.2 us -> 22.6 us  [call(): pl.pallas_call(kernel, in_specs=[HBM if i in hbm else VMEM for i in range...]
    ppermute x3, waiting for transfers between devices: 6.39 us -> 7.85 us  [exchange(): after = lax.ppermute(first, 'virt', down)]
  transfers between devices with their start and end apart: 9 -> 9, of which waited for: 6 -> 6; matrix products, arithmetic and copies ran while one was open for 3% -> 4% of each run, Pallas kernels for 9% -> 15%
where the time goes in v4:
time: 121 us; the launch traced here: 120 us
  waiting for transfers between devices  42.2 us (35%)
  starting transfers between devices  38.8 us (32%)
  Pallas kernels  25 us (21%)
  local copies, waits for them, and re-layouts  11.9 us (10%)
  between operations  1.76 us (1%)
    all_to_all x3, waiting for transfers between devices, spread(): lax.all_to_all(packed.reshape(pairs, share * nk, TW), 'pair', split_axis=...  30.2 us
    all_to_all x3, starting transfers between devices, spread(): lax.all_to_all(packed.reshape(pairs, share * nk, TW), 'pair', split_axis=...  27.6 us
    pallas_call x9, Pallas kernels, call(): pl.pallas_call(kernel, in_specs=[HBM if i in hbm else VMEM for i in range...  22.6 us
    ppermute x3, waiting for transfers between devices, exchange(): after = lax.ppermute(first, 'virt', down)  7.85 us
    unnamed x30, local copies, waits for them, and re-layouts  7.68 us
    ppermute x3, starting transfers between devices, exchange(): before = lax.ppermute(last, 'virt', up)  7.29 us
    ppermute x3, waiting for transfers between devices, exchange(): before = lax.ppermute(last, 'virt', up)  4.2 us
    ppermute x3, starting transfers between devices, exchange(): after = lax.ppermute(first, 'virt', down)  3.88 us
  transfers between devices with their start and end apart: 9, of which 6 were waited for; matrix products, arithmetic and copies ran while one was open for 4% of the time, Pallas kernels for 15%

profile of v4, /device:TPU:1, one launch (start us, length us, event | category | flops | bytes accessed | tf_op | source)
XLA Modules:
  0.0 120.3 jit_solution(11386855297140113135)
XLA Ops:
  0.0 2.4 %pack.1 = f32[2048,128]{1,0:T(8,128)} custom-call(f32[1024,256]{1,0:T(8,128)} %bitcast.28), custom_call_target="tpu_custom_call" | custom-call | tf_op jit(solution)/shard_map/pack/pallas_call | solution.py:64
  2.4 14.6 %all-to-all-start.1 = ((f32[64,32,128]{2,1,0:T(8,128)}), f32[64,32,128]{2,1,0:T(8,128)S(1)}, u32[]{:S(2)}, u32[]{:S(2)}) async-start(f32[64,32,128]{2,1,0:T(8,128)} %bitcast.30), calls=%async_computation.1 | async-start | bytes 2097152 | tf_op jit(solution)/shard_map/all_to_all | solution.py:292
  17.1 1.3 %collective-permute-start.1 = (f32[256,256]{1,0:T(8,128)S(1)}, f32[256,256]{1,0:T(8,128)S(1)}, u32[]{:S(2)}, u32[]{:S(2)}) collective-permute-start(f32[256,256]{1,0:T(8,128)S(1)} %get-tuple-element.27), channel_id=1, source_target_pairs={{1,0},{2,1},{3,2},{4,3},{5,4},{6,5},{7,6},{8,7},{9,8},{10,9},{11,1... | collective-permute-start | bytes 786440 | tf_op jit(solution)/shard_map/ppermute | solution.py:266
  18.4 4.0 %collective-permute-start = (f32[256,256]{1,0:T(8,128)S(1)}, f32[256,256]{1,0:T(8,128)S(1)}, u32[]{:S(2)}, u32[]{:S(2)}) collective-permute-start(f32[256,256]{1,0:T(8,128)S(1)} %get-tuple-element.28), channel_id=1, source_target_pairs={{0,1},{1,2},{2,3},{3,4},{4,5},{5,6},{6,7},{7,8},{8,9},{9,10},{10,1... | collective-permute-start | bytes 786440 | tf_op jit(solution)/shard_map/ppermute | solution.py:265
  22.4 0.6 fusion.1
  24.3 0.7 dynamic_slice.15
  25.0 1.1 copy.10.virt_ref
  26.1 0.7 dynamic_slice.18
  26.7 0.8 fusion
  27.5 0.6 pad_maximum_fusion
  28.1 6.5 %own.1 = (f32[1024,256]{1,0:T(8,128)}, bf16[2,1024,1024]{2,1,0:T(8,128)(2,1)}) custom-call(f32[1024,256]{1,0:T(8,128)} %bitcast.29, f32[1024,256]{1,0:T(8,128)} %bitcast.22, f32[1024,1024]{1,0:T(8,128)} %d_hbm.1), custom_call_target="tpu_custom_call" | custom-call | flops 1610612736 | bytes 11534336 | tf_op jit(solution)/shard_map/own/pallas_call | solution.py:249
  34.7 0.0 collective-permute-done.1.after_ref
  34.7 0.0 copy-start.10
  34.7 0.0 collective-permute-done.before_ref
  34.7 0.7 copy-done.10
  35.4 0.1 copy-done.11
  35.6 5.7 %ready.1 = (f32[1024,256]{1,0:T(8,128)}, f32[2048,128]{1,0:T(8,128)}, f32[256,256]{1,0:T(8,128)}, f32[256,256]{1,0:T(8,128)}) custom-call(f32[1024,256]{1,0:T(8,128)} %get-tuple-element.16.y_hbm, f32[256,256]{1,0:T(8,128)} %copy-done.11, f32[256,256]{1,0:T(8,128)} %copy-done.10, f32[256,256]{1,0:T(8,128)} %low_ref.5, f32[256,256]{1,0:T(8,128)} %high_ref.5, ...), custom_call_target="tpu_custom_call" | custom-call | flops 201326592 | bytes 4723716 | tf_op jit(solution)/shard_map/ready/pallas_call | solution.py:249
  41.2 4.4 %all-to-all-done.1 = f32[64,32,128]{2,1,0:T(8,128)S(1)} async-done(((f32[64,32,128]{2,1,0:T(8,128)}), f32[64,32,128]{2,1,0:T(8,128)S(1)}, u32[]{:S(2)}, u32[]{:S(2)}) %all-to-all-start.1) | async-done | bytes 1048608 | tf_op jit(solution)/shard_map/all_to_all | solution.py:292
  45.6 6.7 %all-to-all-start = ((f32[64,32,128]{2,1,0:T(8,128)}), f32[64,32,128]{2,1,0:T(8,128)S(1)}, u32[]{:S(2)}, u32[]{:S(2)}) async-start(f32[64,32,128]{2,1,0:T(8,128)} %bitcast.31), calls=%async_computation | async-start | bytes 2097152 | tf_op jit(solution)/shard_map/all_to_all | solution.py:292
  52.3 0.1 dynamic_slice.19
  52.4 0.1 broadcast_in_dim.32
  52.4 0.1 reshape.41.pair_ref
  52.5 0.1 reshape.40.col_ref
  52.6 0.0 copy-done.7
  52.6 0.3 prep.1
  53.0 0.0 copy-start.4
  53.0 0.0 copy-start.5
  53.0 1.1 ladder.1
  54.1 1.6 %collective-permute-start.2 = (f32[256,256]{1,0:T(8,128)S(1)}, f32[256,256]{1,0:T(8,128)S(1)}, u32[]{:S(2)}, u32[]{:S(2)}) collective-permute-start(f32[256,256]{1,0:T(8,128)S(1)} %get-tuple-element.22), channel_id=1, source_target_pairs={{0,1},{1,2},{2,3},{3,4},{4,5},{5,6},{6,7},{7,8},{8,9},{9,10},{10,1... | collective-permute-start | bytes 786440 | tf_op jit(solution)/shard_map/ppermute | solution.py:265
  55.7 1.3 %collective-permute-start.3 = (f32[256,256]{1,0:T(8,128)S(1)}, f32[256,256]{1,0:T(8,128)S(1)}, u32[]{:S(2)}, u32[]{:S(2)}) collective-permute-start(f32[256,256]{1,0:T(8,128)S(1)} %get-tuple-element.23), channel_id=1, source_target_pairs={{1,0},{2,1},{3,2},{4,3},{5,4},{6,5},{7,6},{8,7},{9,8},{10,9},{11,1... | collective-permute-start | bytes 786440 | tf_op jit(solution)/shard_map/ppermute | solution.py:266
  57.0 2.2 %copy-done.1 = bf16[2,1024,1024]{2,1,0:T(8,128)(2,1)S(1)} copy-done((bf16[2,1024,1024]{2,1,0:T(8,128)(2,1)S(1)}, bf16[2,1024,1024]{2,1,0:T(8,128)(2,1)}, u32[]{:S(2)}) %copy-start.1) | copy-done | bytes 4194328
  59.2 2.2 %inner.1.t_ref = f32[256,1024]{1,0:T(8,128)S(1)} custom-call(f32[256,1024]{1,0:T(8,128)S(1)} %get-tuple-element.20.w_ref, bf16[2,1024,1024]{2,1,0:T(8,128)(2,1)S(1)} %copy-done.1, bf16[256,256]{1,0:T(8,128)(2,1)S(1)} %get-tuple-element.18.kh_ref, bf16[256,256]{1,0:T(8,128)(2,1)S(1)} %get-tuple-element.19.kl_ref), custom_call_target="tpu_custom_call" | custom-call | flops 2013265920 | bytes 6553600 | tf_op jit(solution)/shard_map/inner/pallas_call | solution.py:249
  61.4 0.0 collective-permute-done.2.before_ref
  61.5 3.8 %collective-permute-done.3.after_ref = f32[256,256]{1,0:T(8,128)S(1)} collective-permute-done((f32[256,256]{1,0:T(8,128)S(1)}, f32[256,256]{1,0:T(8,128)S(1)}, u32[]{:S(2)}, u32[]{:S(2)}) %collective-permute-start.3) | collective-permute-done | bytes 262176 | tf_op jit(solution)/shard_map/ppermute | solution.py:266
  65.3 0.4 outer.1.t_ref
  65.7 15.1 %all-to-all-done = f32[64,32,128]{2,1,0:T(8,128)S(1)} async-done(((f32[64,32,128]{2,1,0:T(8,128)}), f32[64,32,128]{2,1,0:T(8,128)S(1)}, u32[]{:S(2)}, u32[]{:S(2)}) %all-to-all-start) | async-done | bytes 1048608 | tf_op jit(solution)/shard_map/all_to_all | solution.py:292
  80.8 2.3 %join.1 = f32[2048,128]{1,0:T(8,128)} custom-call(f32[2048,128]{1,0:T(8,128)S(1)} %bitcast.19, f32[256,1024]{1,0:T(8,128)S(1)} %outer.1.t_ref, f32[64,64]{1,0:T(8,128)S(1)} %copy-done.7), custom_call_target="tpu_custom_call" | custom-call | flops 402653184 | bytes 3162112 | tf_op jit(solution)/shard_map/join/pallas_call | solution.py:249
  83.1 6.4 %all-to-all-start.2 = ((f32[64,32,128]{2,1,0:T(8,128)}), f32[64,32,128]{2,1,0:T(8,128)S(1)}, u32[]{:S(2)}, u32[]{:S(2)}) async-start(f32[64,32,128]{2,1,0:T(8,128)} %bitcast.14), calls=%async_computation.2 | async-start | bytes 2097152 | tf_op jit(solution)/shard_map/all_to_all | solution.py:292
  89.5 1.7 %collective-permute-start.4 = (f32[256,256]{1,0:T(8,128)}, f32[256,256]{1,0:T(8,128)S(1)}, u32[]{:S(2)}, u32[]{:S(2)}) collective-permute-start(f32[256,256]{1,0:T(8,128)} %get-tuple-element.25), channel_id=1, source_target_pairs={{0,1},{1,2},{2,3},{3,4},{4,5},{5,6},{6,7},{7,8},{8,9},{9,10},{10,1... | collective-permute-start | bytes 786440 | tf_op jit(solution)/shard_map/ppermute | solution.py:265
  91.1 1.3 %collective-permute-start.5 = (f32[256,256]{1,0:T(8,128)S(1)}, f32[256,256]{1,0:T(8,128)S(1)}, u32[]{:S(2)}, u32[]{:S(2)}) collective-permute-start(f32[256,256]{1,0:T(8,128)S(1)} %copy-done.14), channel_id=1, source_target_pairs={{1,0},{2,1},{3,2},{4,3},{5,4},{6,5},{7,6},{8,7},{9,8},{10,9},{11,1... | collective-permute-start | bytes 786440 | tf_op jit(solution)/shard_map/ppermute | solution.py:266
  92.4 4.2 %collective-permute-done.4.before_ref = f32[256,256]{1,0:T(8,128)S(1)} collective-permute-done((f32[256,256]{1,0:T(8,128)}, f32[256,256]{1,0:T(8,128)S(1)}, u32[]{:S(2)}, u32[]{:S(2)}) %collective-permute-start.4) | collective-permute-done | bytes 262176 | tf_op jit(solution)/shard_map/ppermute | solution.py:265
  96.6 4.0 %collective-permute-done.5.after_ref = f32[256,256]{1,0:T(8,128)S(1)} collective-permute-done((f32[256,256]{1,0:T(8,128)S(1)}, f32[256,256]{1,0:T(8,128)S(1)}, u32[]{:S(2)}, u32[]{:S(2)}) %collective-permute-start.5) | collective-permute-done | bytes 262176 | tf_op jit(solution)/shard_map/ppermute | solution.py:266
  100.7 2.2 %copy-done.2 = bf16[2,1024,1024]{2,1,0:T(8,128)(2,1)S(1)} copy-done((bf16[2,1024,1024]{2,1,0:T(8,128)(2,1)S(1)}, bf16[2,1024,1024]{2,1,0:T(8,128)(2,1)}, u32[]{:S(2)}) %copy-start.2) | copy-done | bytes 4194328
  102.9 1.2 %copy-done.3 = f32[1,1024,256]{2,1,0:T(8,128)S(1)} copy-done((f32[1,1024,256]{2,1,0:T(8,128)S(1)}, f32[1,1024,256]{2,1,0:T(8,128)}, u32[]{:S(2)}) %copy-start.3) | copy-done | bytes 1048600
  104.1 1.2 %copy-done.6 = f32[1024,256]{1,0:T(8,128)S(1)} copy-done((f32[1024,256]{1,0:T(8,128)S(1)}, f32[1024,256]{1,0:T(8,128)}, u32[]{:S(2)}) %copy-start.6) | copy-done | bytes 1048600
  105.3 2.0 %again.1.t_ref = f32[1024,256]{1,0:T(8,128)S(1)} custom-call(f32[1024,256]{1,0:T(8,128)S(1)} %copy-done.6, f32[1024,256]{1,0:T(8,128)S(1)} %bitcast.23, f32[256,256]{1,0:T(8,128)S(1)} %collective-permute-done.4.before_ref, f32[256,256]{1,0:T(8,128)S(1)} %collective-permute-done.5.after_ref, f32[256,256]{1,0:T(8,128)S(1)} %copy-done.4, ...), custom_call_target="tpu_custom_call" | custom-call | flops 1610612736 | bytes 8388608 | tf_op jit(solution)/shard_map/again/pallas_call | solution.py:249
  107.3 10.7 %all-to-all-done.2 = f32[64,32,128]{2,1,0:T(8,128)S(1)} async-done(((f32[64,32,128]{2,1,0:T(8,128)}), f32[64,32,128]{2,1,0:T(8,128)S(1)}, u32[]{:S(2)}, u32[]{:S(2)}) %all-to-all-start.2) | async-done | bytes 1048608 | tf_op jit(solution)/shard_map/all_to_all | solution.py:292
  118.0 2.1 %last.1 = f32[1024,256]{1,0:T(8,128)} custom-call(f32[2048,128]{1,0:T(8,128)S(1)} %bitcast.20, f32[1024,256]{1,0:T(8,128)S(1)} %again.1.t_ref, f32[1024,1]{1,0:T(8,128)S(1)} %copy-done, f32[1,256]{1,0:T(1,128)S(1)} %bitcast.27, f32[1,1]{1,0:T(1,128)} %bitcast.8.pair_ref), custom_call_target="tpu_custom_call" | custom-call | flops 2621440 | bytes 3150852 | tf_op jit(solution)/shard_map/last/pallas_call | solution.py:249
  (22 shorter events, 0.1 us)
Async XLA Ops:
  0.0 17.0 %copy-start.9 = (f32[1,1024,256]{2,1,0:T(8,128)S(1)}, f32[1,1024,256]{2,1,0:T(8,128)}, u32[]{:S(2)}) copy-start(f32[1,1024,256]{2,1,0:T(8,128)} %param.9) | copy-start | bytes 3145732
  0.0 22.4 %copy-start.12 = (s32[2]{0:T(128)S(1)}, s32[2]{0:T(128)}, u32[]{:S(2)}) copy-start(s32[2]{0:T(128)} %param.17) | copy-start | bytes 28
  0.0 26.1 %copy-start.13 = (f32[64]{0:T(128)S(1)}, f32[64]{0:T(128)}, u32[]{:S(2)}) copy-start(f32[64]{0:T(128)} %param.15) | copy-start | bytes 772
  2.4 43.2 %all-to-all-start.1 = ((f32[64,32,128]{2,1,0:T(8,128)}), f32[64,32,128]{2,1,0:T(8,128)S(1)}, u32[]{:S(2)}, u32[]{:S(2)}) async-start(f32[64,32,128]{2,1,0:T(8,128)} %bitcast.30), calls=%async_computation.1 | async-start | bytes 2097152 | tf_op jit(solution)/shard_map/all_to_all | solution.py:292
  17.1 17.6 %collective-permute-start.1 = (f32[256,256]{1,0:T(8,128)S(1)}, f32[256,256]{1,0:T(8,128)S(1)}, u32[]{:S(2)}, u32[]{:S(2)}) collective-permute-start(f32[256,256]{1,0:T(8,128)S(1)} %get-tuple-element.27), channel_id=1, source_target_pairs={{1,0},{2,1},{3,2},{4,3},{5,4},{6,5},{7,6},{8,7},{9,8},{10,9},{11,1... | collective-permute-start | bytes 786440 | tf_op jit(solution)/shard_map/ppermute | solution.py:266
  18.4 16.3 %collective-permute-start = (f32[256,256]{1,0:T(8,128)S(1)}, f32[256,256]{1,0:T(8,128)S(1)}, u32[]{:S(2)}, u32[]{:S(2)}) collective-permute-start(f32[256,256]{1,0:T(8,128)S(1)} %get-tuple-element.28), channel_id=1, source_target_pairs={{0,1},{1,2},{2,3},{3,4},{4,5},{5,6},{6,7},{7,8},{8,9},{9,10},{10,1... | collective-permute-start | bytes 786440 | tf_op jit(solution)/shard_map/ppermute | solution.py:265
  28.1 24.1 %copy-start.8 = (f32[256]{0:T(256)S(1)}, f32[256]{0:T(256)}, u32[]{:S(2)}) copy-start(f32[256]{0:T(256)} %pad_maximum_fusion) | copy-start | bytes 3076
  28.1 24.5 %copy-start.7 = (f32[64,64]{1,0:T(8,128)S(1)}, f32[64,64]{1,0:T(8,128)}, u32[]{:S(2)}) copy-start(f32[64,64]{1,0:T(8,128)} %l_ref.3) | copy-start | bytes 49156
  34.7 0.7 copy-start.10
  34.7 0.8 copy-start.11
  45.6 35.2 %all-to-all-start = ((f32[64,32,128]{2,1,0:T(8,128)}), f32[64,32,128]{2,1,0:T(8,128)S(1)}, u32[]{:S(2)}, u32[]{:S(2)}) async-start(f32[64,32,128]{2,1,0:T(8,128)} %bitcast.31), calls=%async_computation | async-start | bytes 2097152 | tf_op jit(solution)/shard_map/all_to_all | solution.py:292
  53.0 12.3 %copy-start.4 = (f32[256,256]{1,0:T(8,128)S(1)}, f32[256,256]{1,0:T(8,128)}, u32[]{:S(2)}) copy-start(f32[256,256]{1,0:T(8,128)} %low_ref.5) | copy-start | bytes 786436
  53.0 12.3 %copy-start.5 = (f32[256,256]{1,0:T(8,128)S(1)}, f32[256,256]{1,0:T(8,128)}, u32[]{:S(2)}) copy-start(f32[256,256]{1,0:T(8,128)} %high_ref.5) | copy-start | bytes 786436
  54.1 7.4 %collective-permute-start.2 = (f32[256,256]{1,0:T(8,128)S(1)}, f32[256,256]{1,0:T(8,128)S(1)}, u32[]{:S(2)}, u32[]{:S(2)}) collective-permute-start(f32[256,256]{1,0:T(8,128)S(1)} %get-tuple-element.22), channel_id=1, source_target_pairs={{0,1},{1,2},{2,3},{3,4},{4,5},{5,6},{6,7},{7,8},{8,9},{9,10},{10,1... | collective-permute-start | bytes 786440 | tf_op jit(solution)/shard_map/ppermute | solution.py:265
  55.7 9.5 %collective-permute-start.3 = (f32[256,256]{1,0:T(8,128)S(1)}, f32[256,256]{1,0:T(8,128)S(1)}, u32[]{:S(2)}, u32[]{:S(2)}) collective-permute-start(f32[256,256]{1,0:T(8,128)S(1)} %get-tuple-element.23), channel_id=1, source_target_pairs={{1,0},{2,1},{3,2},{4,3},{5,4},{6,5},{7,6},{8,7},{9,8},{10,9},{11,1... | collective-permute-start | bytes 786440 | tf_op jit(solution)/shard_map/ppermute | solution.py:266
  57.0 2.2 %copy-start.1 = (bf16[2,1024,1024]{2,1,0:T(8,128)(2,1)S(1)}, bf16[2,1024,1024]{2,1,0:T(8,128)(2,1)}, u32[]{:S(2)}) copy-start(bf16[2,1024,1024]{2,1,0:T(8,128)(2,1)} %get-tuple-element.21.d2_ref) | copy-start | bytes 12582916
  61.4 29.7 %copy-start.14 = (f32[256,256]{1,0:T(8,128)S(1)}, f32[256,256]{1,0:T(8,128)}, u32[]{:S(2)}) copy-start(f32[256,256]{1,0:T(8,128)} %get-tuple-element.26) | copy-start | bytes 786436
  83.1 34.9 %all-to-all-start.2 = ((f32[64,32,128]{2,1,0:T(8,128)}), f32[64,32,128]{2,1,0:T(8,128)S(1)}, u32[]{:S(2)}, u32[]{:S(2)}) async-start(f32[64,32,128]{2,1,0:T(8,128)} %bitcast.14), calls=%async_computation.2 | async-start | bytes 2097152 | tf_op jit(solution)/shard_map/all_to_all | solution.py:292
  89.5 7.2 %collective-permute-start.4 = (f32[256,256]{1,0:T(8,128)}, f32[256,256]{1,0:T(8,128)S(1)}, u32[]{:S(2)}, u32[]{:S(2)}) collective-permute-start(f32[256,256]{1,0:T(8,128)} %get-tuple-element.25), channel_id=1, source_target_pairs={{0,1},{1,2},{2,3},{3,4},{4,5},{5,6},{6,7},{7,8},{8,9},{9,10},{10,1... | collective-permute-start | bytes 786440 | tf_op jit(solution)/shard_map/ppermute | solution.py:265
  91.1 9.5 %collective-permute-start.5 = (f32[256,256]{1,0:T(8,128)S(1)}, f32[256,256]{1,0:T(8,128)S(1)}, u32[]{:S(2)}, u32[]{:S(2)}) collective-permute-start(f32[256,256]{1,0:T(8,128)S(1)} %copy-done.14), channel_id=1, source_target_pairs={{1,0},{2,1},{3,2},{4,3},{5,4},{6,5},{7,6},{8,7},{9,8},{10,9},{11,1... | collective-permute-start | bytes 786440 | tf_op jit(solution)/shard_map/ppermute | solution.py:266
  100.7 2.2 %copy-start.2 = (bf16[2,1024,1024]{2,1,0:T(8,128)(2,1)S(1)}, bf16[2,1024,1024]{2,1,0:T(8,128)(2,1)}, u32[]{:S(2)}) copy-start(bf16[2,1024,1024]{2,1,0:T(8,128)(2,1)} %get-tuple-element.21.d2_ref) | copy-start | bytes 12582916
  102.9 1.2 %copy-start.3 = (f32[1,1024,256]{2,1,0:T(8,128)S(1)}, f32[1,1024,256]{2,1,0:T(8,128)}, u32[]{:S(2)}) copy-start(f32[1,1024,256]{2,1,0:T(8,128)} %param.10) | copy-start | bytes 3145732
  104.1 1.2 %copy-start.6 = (f32[1024,256]{1,0:T(8,128)S(1)}, f32[1024,256]{1,0:T(8,128)}, u32[]{:S(2)}) copy-start(f32[1024,256]{1,0:T(8,128)} %get-tuple-element.24.u_ref) | copy-start | bytes 3145732
  105.3 12.7 %copy-start = (f32[1024,1]{1,0:T(8,128)S(1)}, f32[1024,1]{1,0:T(8,128)}, u32[]{:S(2)}) copy-start(f32[1024,1]{1,0:T(8,128)} %copy.10.virt_ref) | copy-start | bytes 12292

commit v5 on v4

--- a/solution.py
+++ b/solution.py
@@ -92,6 +92,14 @@
 
 def energy(row, col, pair):
     return row + col - pair
+
+
+def own_energy_of(virt_ref, kept_ref, pair_ref, start, stop):
+    rows = [virt_ref[:, k * TW : (k + 1) * TW] for k in range(start, stop)]
+    tall = jnp.concatenate([jnp.broadcast_to(row, (TW, TW)).T for row in rows], 0)
+    tiles = kept_ref.shape[1] // TW
+    kept = [kept_ref[:, t * TW : (t + 1) * TW] for t in range(tiles)]
+    return jnp.concatenate([energy(tall, part, pair_ref[...]) for part in kept], 1)
 
 
 def with_edges(c, count, out, low_ref, high_ref, before_ref, after_ref):
@@ -159,7 +167,7 @@
         here = slice(c * wide, (c + 1) * wide)
         got[c].wait()
         out = with_edges(c, count, y_ref[here, :], low_ref, high_ref, before_ref, after_ref)
-        u_ref[here, :] = out / energy(virt_ref[here, :], kept_ref[...], pair_ref[...])
+        u_ref[here, :] = out / own_energy_of(virt_ref, kept_ref, pair_ref, c * wide // TW, (c + 1) * wide // TW)
     for t in range(cols // TW):
         turn(u_ref, packed_ref, t, nk)
         here = slice(t * TW * nk, (t + 1) * TW * nk)
@@ -232,10 +240,11 @@
     copies = []
     for k in range(nk):
         here = slice(k * TW, (k + 1) * TW)
+        denom = own_energy_of(virt_ref, kept_ref, pair_ref, k, k + 1)
         for t in range(cols // TW):
             lanes = slice(t * TW, (t + 1) * TW)
             out = t_ref[here, lanes] + p_ref[pl.ds(t * TW * nk + k, TW, stride=nk), :].T
-            o_ref[here, lanes] = out / energy(virt_ref[here, :], kept_ref[:, lanes], pair_ref[...])
+            o_ref[here, lanes] = out / denom[:, lanes]
         if k % per == per - 1:
             done = slice((k + 1 - per) * TW, (k + 1) * TW)
             copies.append(pltpu.make_async_copy(o_ref.at[done, :], o_hbm.at[done, :], sems.at[k // per]))
@@ -301,7 +310,7 @@
     kept = jnp.concatenate(
         [lax.dynamic_slice_in_dim(virt_energy, column_tiles[t] * TW, TW) for t in range(cols // TW)]
     )
-    own_energy = (row[:, None], kept[None, :], mine[None, :])
+    own_energy = (row[None, :], kept[None, :], mine[None, :])
     start = lax.axis_index("pair") * share
     col = jnp.broadcast_to(lax.dynamic_slice_in_dim(kept, start, share)[None, :], (pairs, share)).reshape(-1, 1)
     all_pairs = jnp.broadcast_to(pair_energy[:, None], (pairs, share)).reshape(-1, 1)

time: 121 us -> 120 us (level)
  waiting for transfers between devices: 42.2 us -> 43.7 us
    all_to_all x3, waiting for transfers between devices: 30.2 us -> 31.4 us  [spread(): lax.all_to_all(packed.reshape(pairs, share * nk, TW), 'pair', split_axis=...]
where the time goes in v5:
time: 120 us
  waiting for transfers between devices  43.7 us (36%)
  starting transfers between devices  37.6 us (31%)
  Pallas kernels  24.9 us (21%)
  local copies, waits for them, and re-layouts  11.1 us (9%)
  between operations  1.79 us (1%)
    all_to_all x3, waiting for transfers between devices, spread(): lax.all_to_all(packed.reshape(pairs, share * nk, TW), 'pair', split_axis=...  31.4 us
    all_to_all x3, starting transfers between devices, spread(): lax.all_to_all(packed.reshape(pairs, share * nk, TW), 'pair', split_axis=...  27.1 us
    pallas_call x9, Pallas kernels, call(): pl.pallas_call(kernel, in_specs=[HBM if i in hbm else VMEM for i in range...  22.5 us
    ppermute x3, waiting for transfers between devices, exchange(): after = lax.ppermute(first, 'virt', down)  8.02 us
    unnamed x30, local copies, waits for them, and re-layouts  7.41 us
    ppermute x3, starting transfers between devices, exchange(): before = lax.ppermute(last, 'virt', up)  6.65 us
    ppermute x3, waiting for transfers between devices, exchange(): before = lax.ppermute(last, 'virt', up)  4.21 us
    ppermute x3, starting transfers between devices, exchange(): after = lax.ppermute(first, 'virt', down)  3.88 us
  transfers between devices with their start and end apart: 9, of which 6 were waited for; matrix products, arithmetic and copies ran while one was open for 4% of the time, Pallas kernels for 15%

profile of v5, /device:TPU:1, one launch (start us, length us, event | category | flops | bytes accessed | tf_op | source)
XLA Modules:
  0.0 119.6 jit_solution(7920290311174884628)
XLA Ops:
  0.0 2.4 %pack.1 = f32[2048,128]{1,0:T(8,128)} custom-call(f32[1024,256]{1,0:T(8,128)} %bitcast.28), custom_call_target="tpu_custom_call" | custom-call | tf_op jit(solution)/shard_map/pack/pallas_call | solution.py:64
  2.4 14.6 %all-to-all-start.1 = ((f32[64,32,128]{2,1,0:T(8,128)}), f32[64,32,128]{2,1,0:T(8,128)S(1)}, u32[]{:S(2)}, u32[]{:S(2)}) async-start(f32[64,32,128]{2,1,0:T(8,128)} %bitcast.30), calls=%async_computation.1 | async-start | bytes 2097152 | tf_op jit(solution)/shard_map/all_to_all | solution.py:301
  17.1 1.3 %collective-permute-start.1 = (f32[256,256]{1,0:T(8,128)S(1)}, f32[256,256]{1,0:T(8,128)S(1)}, u32[]{:S(2)}, u32[]{:S(2)}) collective-permute-start(f32[256,256]{1,0:T(8,128)S(1)} %get-tuple-element.27), channel_id=1, source_target_pairs={{1,0},{2,1},{3,2},{4,3},{5,4},{6,5},{7,6},{8,7},{9,8},{10,9},{11,1... | collective-permute-start | bytes 786440 | tf_op jit(solution)/shard_map/ppermute | solution.py:275
  18.4 4.0 %collective-permute-start = (f32[256,256]{1,0:T(8,128)S(1)}, f32[256,256]{1,0:T(8,128)S(1)}, u32[]{:S(2)}, u32[]{:S(2)}) collective-permute-start(f32[256,256]{1,0:T(8,128)S(1)} %get-tuple-element.28), channel_id=1, source_target_pairs={{0,1},{1,2},{2,3},{3,4},{4,5},{5,6},{6,7},{7,8},{8,9},{9,10},{10,1... | collective-permute-start | bytes 786440 | tf_op jit(solution)/shard_map/ppermute | solution.py:274
  22.4 0.7 fusion.1
  24.4 0.0 copy-done.14
  24.4 0.6 dynamic_slice.18
  25.0 1.3 %dynamic_slice.15 = f32[1024]{0:T(1024)} dynamic-slice(f32[12288]{0:T(1024)} %param.16, s32[]{:T(128)S(6)} %select_n.15), dynamic_slice_sizes={1024} | dynamic-slice | bytes 8196 | tf_op jit(solution)/shard_map/dynamic_slice | solution.py:308
  26.3 0.8 fusion
  27.0 0.6 pad_maximum_fusion
  27.6 6.5 %own.1 = (f32[1024,256]{1,0:T(8,128)}, bf16[2,1024,1024]{2,1,0:T(8,128)(2,1)}) custom-call(f32[1024,256]{1,0:T(8,128)} %bitcast.29, f32[1024,256]{1,0:T(8,128)} %bitcast.21, f32[1024,1024]{1,0:T(8,128)} %d_hbm.1), custom_call_target="tpu_custom_call" | custom-call | flops 1610612736 | bytes 11534336 | tf_op jit(solution)/shard_map/own/pallas_call | solution.py:258
  34.2 0.0 collective-permute-done.1.after_ref
  34.2 0.0 collective-permute-done.before_ref
  34.2 0.7 copy-done.11
  34.9 0.2 copy-done.12
  35.1 5.5 %ready.1 = (f32[1024,256]{1,0:T(8,128)}, f32[2048,128]{1,0:T(8,128)}, f32[256,256]{1,0:T(8,128)}, f32[256,256]{1,0:T(8,128)}) custom-call(f32[1024,256]{1,0:T(8,128)} %get-tuple-element.16.y_hbm, f32[256,256]{1,0:T(8,128)} %copy-done.12, f32[256,256]{1,0:T(8,128)} %copy-done.11, f32[256,256]{1,0:T(8,128)} %low_ref.5, f32[256,256]{1,0:T(8,128)} %high_ref.5, ...), custom_call_target="tpu_custom_call" | custom-call | flops 201326592 | bytes 4723716 | tf_op jit(solution)/shard_map/ready/pallas_call | solution.py:258
  40.6 5.0 %all-to-all-done.1 = f32[64,32,128]{2,1,0:T(8,128)S(1)} async-done(((f32[64,32,128]{2,1,0:T(8,128)}), f32[64,32,128]{2,1,0:T(8,128)S(1)}, u32[]{:S(2)}, u32[]{:S(2)}) %all-to-all-start.1) | async-done | bytes 1048608 | tf_op jit(solution)/shard_map/all_to_all | solution.py:301
  45.6 6.3 %all-to-all-start = ((f32[64,32,128]{2,1,0:T(8,128)}), f32[64,32,128]{2,1,0:T(8,128)S(1)}, u32[]{:S(2)}, u32[]{:S(2)}) async-start(f32[64,32,128]{2,1,0:T(8,128)} %bitcast.31), calls=%async_computation | async-start | bytes 2097152 | tf_op jit(solution)/shard_map/all_to_all | solution.py:301
  51.9 0.1 dynamic_slice.19
  52.0 0.1 broadcast_in_dim.29
  52.1 0.1 reshape.41.pair_ref
  52.2 0.1 reshape.40.col_ref
  52.3 0.3 prep.1
  52.6 0.0 copy-done.7
  52.6 0.0 copy-start.3
  52.6 0.0 copy-start.4
  52.6 1.2 ladder.1
  53.8 1.3 %collective-permute-start.2 = (f32[256,256]{1,0:T(8,128)S(1)}, f32[256,256]{1,0:T(8,128)S(1)}, u32[]{:S(2)}, u32[]{:S(2)}) collective-permute-start(f32[256,256]{1,0:T(8,128)S(1)} %get-tuple-element.22), channel_id=1, source_target_pairs={{0,1},{1,2},{2,3},{3,4},{4,5},{5,6},{6,7},{7,8},{8,9},{9,10},{10,1... | collective-permute-start | bytes 786440 | tf_op jit(solution)/shard_map/ppermute | solution.py:274
  55.1 1.3 %collective-permute-start.3 = (f32[256,256]{1,0:T(8,128)S(1)}, f32[256,256]{1,0:T(8,128)S(1)}, u32[]{:S(2)}, u32[]{:S(2)}) collective-permute-start(f32[256,256]{1,0:T(8,128)S(1)} %get-tuple-element.23), channel_id=1, source_target_pairs={{1,0},{2,1},{3,2},{4,3},{5,4},{6,5},{7,6},{8,7},{9,8},{10,9},{11,1... | collective-permute-start | bytes 786440 | tf_op jit(solution)/shard_map/ppermute | solution.py:275
  56.4 2.2 %copy-done = bf16[2,1024,1024]{2,1,0:T(8,128)(2,1)S(1)} copy-done((bf16[2,1024,1024]{2,1,0:T(8,128)(2,1)S(1)}, bf16[2,1024,1024]{2,1,0:T(8,128)(2,1)}, u32[]{:S(2)}) %copy-start) | copy-done | bytes 4194328
  58.6 2.2 %inner.1.t_ref = f32[256,1024]{1,0:T(8,128)S(1)} custom-call(f32[256,1024]{1,0:T(8,128)S(1)} %get-tuple-element.20.w_ref, bf16[2,1024,1024]{2,1,0:T(8,128)(2,1)S(1)} %copy-done, bf16[256,256]{1,0:T(8,128)(2,1)S(1)} %get-tuple-element.18.kh_ref, bf16[256,256]{1,0:T(8,128)(2,1)S(1)} %get-tuple-element.19.kl_ref), custom_call_target="tpu_custom_call" | custom-call | flops 2013265920 | bytes 6553600 | tf_op jit(solution)/shard_map/inner/pallas_call | solution.py:258
  60.9 0.0 copy-start.2
  60.9 0.0 collective-permute-done.2.before_ref
  60.9 3.8 %collective-permute-done.3.after_ref = f32[256,256]{1,0:T(8,128)S(1)} collective-permute-done((f32[256,256]{1,0:T(8,128)S(1)}, f32[256,256]{1,0:T(8,128)S(1)}, u32[]{:S(2)}, u32[]{:S(2)}) %collective-permute-start.3) | collective-permute-done | bytes 262176 | tf_op jit(solution)/shard_map/ppermute | solution.py:275
  64.7 0.4 outer.1.t_ref
  65.1 15.3 %all-to-all-done = f32[64,32,128]{2,1,0:T(8,128)S(1)} async-done(((f32[64,32,128]{2,1,0:T(8,128)}), f32[64,32,128]{2,1,0:T(8,128)S(1)}, u32[]{:S(2)}, u32[]{:S(2)}) %all-to-all-start) | async-done | bytes 1048608 | tf_op jit(solution)/shard_map/all_to_all | solution.py:301
  80.5 2.3 %join.1 = f32[2048,128]{1,0:T(8,128)} custom-call(f32[2048,128]{1,0:T(8,128)S(1)} %bitcast.18, f32[256,1024]{1,0:T(8,128)S(1)} %outer.1.t_ref, f32[64,64]{1,0:T(8,128)S(1)} %copy-done.8), custom_call_target="tpu_custom_call" | custom-call | flops 402653184 | bytes 3162112 | tf_op jit(solution)/shard_map/join/pallas_call | solution.py:258
  82.7 6.2 %all-to-all-start.2 = ((f32[64,32,128]{2,1,0:T(8,128)}), f32[64,32,128]{2,1,0:T(8,128)S(1)}, u32[]{:S(2)}, u32[]{:S(2)}) async-start(f32[64,32,128]{2,1,0:T(8,128)} %bitcast.13), calls=%async_computation.2 | async-start | bytes 2097152 | tf_op jit(solution)/shard_map/all_to_all | solution.py:301
  88.9 1.3 %collective-permute-start.4 = (f32[256,256]{1,0:T(8,128)}, f32[256,256]{1,0:T(8,128)S(1)}, u32[]{:S(2)}, u32[]{:S(2)}) collective-permute-start(f32[256,256]{1,0:T(8,128)} %get-tuple-element.25), channel_id=1, source_target_pairs={{0,1},{1,2},{2,3},{3,4},{4,5},{5,6},{6,7},{7,8},{8,9},{9,10},{10,1... | collective-permute-start | bytes 786440 | tf_op jit(solution)/shard_map/ppermute | solution.py:274
  90.3 1.3 %collective-permute-start.5 = (f32[256,256]{1,0:T(8,128)}, f32[256,256]{1,0:T(8,128)S(1)}, u32[]{:S(2)}, u32[]{:S(2)}) collective-permute-start(f32[256,256]{1,0:T(8,128)} %get-tuple-element.26), channel_id=1, source_target_pairs={{1,0},{2,1},{3,2},{4,3},{5,4},{6,5},{7,6},{8,7},{9,8},{10,9},{11,1... | collective-permute-start | bytes 786440 | tf_op jit(solution)/shard_map/ppermute | solution.py:275
  91.6 4.2 %collective-permute-done.4.before_ref = f32[256,256]{1,0:T(8,128)S(1)} collective-permute-done((f32[256,256]{1,0:T(8,128)}, f32[256,256]{1,0:T(8,128)S(1)}, u32[]{:S(2)}, u32[]{:S(2)}) %collective-permute-start.4) | collective-permute-done | bytes 262176 | tf_op jit(solution)/shard_map/ppermute | solution.py:274
  95.8 4.2 %collective-permute-done.5.after_ref = f32[256,256]{1,0:T(8,128)S(1)} collective-permute-done((f32[256,256]{1,0:T(8,128)}, f32[256,256]{1,0:T(8,128)S(1)}, u32[]{:S(2)}, u32[]{:S(2)}) %collective-permute-start.5) | collective-permute-done | bytes 262176 | tf_op jit(solution)/shard_map/ppermute | solution.py:275
  100.0 2.2 %copy-done.1 = bf16[2,1024,1024]{2,1,0:T(8,128)(2,1)S(1)} copy-done((bf16[2,1024,1024]{2,1,0:T(8,128)(2,1)S(1)}, bf16[2,1024,1024]{2,1,0:T(8,128)(2,1)}, u32[]{:S(2)}) %copy-start.1) | copy-done | bytes 4194328
  102.2 0.9 copy-done.5
  103.1 1.2 %copy-done.6 = f32[1024,256]{1,0:T(8,128)S(1)} copy-done((f32[1024,256]{1,0:T(8,128)S(1)}, f32[1024,256]{1,0:T(8,128)}, u32[]{:S(2)}) %copy-start.6) | copy-done | bytes 1048600
  104.4 2.1 %again.1.t_ref = f32[1024,256]{1,0:T(8,128)S(1)} custom-call(f32[1024,256]{1,0:T(8,128)S(1)} %copy-done.6, f32[1024,256]{1,0:T(8,128)S(1)} %bitcast.22, f32[256,256]{1,0:T(8,128)S(1)} %collective-permute-done.4.before_ref, f32[256,256]{1,0:T(8,128)S(1)} %collective-permute-done.5.after_ref, f32[256,256]{1,0:T(8,128)S(1)} %copy-done.3, ...), custom_call_target="tpu_custom_call" | custom-call | flops 1610612736 | bytes 8388608 | tf_op jit(solution)/shard_map/again/pallas_call | solution.py:258
  106.5 11.0 %all-to-all-done.2 = f32[64,32,128]{2,1,0:T(8,128)S(1)} async-done(((f32[64,32,128]{2,1,0:T(8,128)}), f32[64,32,128]{2,1,0:T(8,128)S(1)}, u32[]{:S(2)}, u32[]{:S(2)}) %all-to-all-start.2) | async-done | bytes 1048608 | tf_op jit(solution)/shard_map/all_to_all | solution.py:301
  117.5 2.0 %last.1 = f32[1024,256]{1,0:T(8,128)} custom-call(f32[2048,128]{1,0:T(8,128)S(1)} %bitcast.19, f32[1024,256]{1,0:T(8,128)S(1)} %again.1.t_ref, f32[1,1024]{1,0:T(1,128)S(1)} %bitcast.25, f32[1,256]{1,0:T(1,128)S(1)} %bitcast.27, f32[1,1]{1,0:T(1,128)} %bitcast.8.pair_ref), custom_call_target="tpu_custom_call" | custom-call | flops 2621440 | bytes 3150852 | tf_op jit(solution)/shard_map/last/pallas_call | solution.py:258
  (21 shorter events, 0.1 us)
Async XLA Ops:
  0.0 17.0 %copy-start.10 = (f32[1,1024,256]{2,1,0:T(8,128)S(1)}, f32[1,1024,256]{2,1,0:T(8,128)}, u32[]{:S(2)}) copy-start(f32[1,1024,256]{2,1,0:T(8,128)} %param.9) | copy-start | bytes 3145732
  0.0 22.4 %copy-start.13 = (s32[2]{0:T(128)S(1)}, s32[2]{0:T(128)}, u32[]{:S(2)}) copy-start(s32[2]{0:T(128)} %param.17) | copy-start | bytes 28
  0.0 24.4 %copy-start.14 = (f32[64]{0:T(128)S(1)}, f32[64]{0:T(128)}, u32[]{:S(2)}) copy-start(f32[64]{0:T(128)} %param.15) | copy-start | bytes 772
  2.4 43.2 %all-to-all-start.1 = ((f32[64,32,128]{2,1,0:T(8,128)}), f32[64,32,128]{2,1,0:T(8,128)S(1)}, u32[]{:S(2)}, u32[]{:S(2)}) async-start(f32[64,32,128]{2,1,0:T(8,128)} %bitcast.30), calls=%async_computation.1 | async-start | bytes 2097152 | tf_op jit(solution)/shard_map/all_to_all | solution.py:301
  17.1 17.1 %collective-permute-start.1 = (f32[256,256]{1,0:T(8,128)S(1)}, f32[256,256]{1,0:T(8,128)S(1)}, u32[]{:S(2)}, u32[]{:S(2)}) collective-permute-start(f32[256,256]{1,0:T(8,128)S(1)} %get-tuple-element.27), channel_id=1, source_target_pairs={{1,0},{2,1},{3,2},{4,3},{5,4},{6,5},{7,6},{8,7},{9,8},{10,9},{11,1... | collective-permute-start | bytes 786440 | tf_op jit(solution)/shard_map/ppermute | solution.py:275
  18.4 15.8 %collective-permute-start = (f32[256,256]{1,0:T(8,128)S(1)}, f32[256,256]{1,0:T(8,128)S(1)}, u32[]{:S(2)}, u32[]{:S(2)}) collective-permute-start(f32[256,256]{1,0:T(8,128)S(1)} %get-tuple-element.28), channel_id=1, source_target_pairs={{0,1},{1,2},{2,3},{3,4},{4,5},{5,6},{6,7},{7,8},{8,9},{9,10},{10,1... | collective-permute-start | bytes 786440 | tf_op jit(solution)/shard_map/ppermute | solution.py:274
  27.6 24.3 %copy-start.9 = (f32[256]{0:T(256)S(1)}, f32[256]{0:T(256)}, u32[]{:S(2)}) copy-start(f32[256]{0:T(256)} %pad_maximum_fusion) | copy-start | bytes 3076
  27.6 24.6 %copy-start.8 = (f32[64,64]{1,0:T(8,128)S(1)}, f32[64,64]{1,0:T(8,128)}, u32[]{:S(2)}) copy-start(f32[64,64]{1,0:T(8,128)} %l_ref.3) | copy-start | bytes 49156
  27.6 25.0 %copy-start.7 = (f32[1024]{0:T(1024)S(1)}, f32[1024]{0:T(1024)}, u32[]{:S(2)}) copy-start(f32[1024]{0:T(1024)} %dynamic_slice.15) | copy-start | bytes 12292
  34.2 0.7 copy-start.11
  34.2 0.8 copy-start.12
  45.6 34.9 %all-to-all-start = ((f32[64,32,128]{2,1,0:T(8,128)}), f32[64,32,128]{2,1,0:T(8,128)S(1)}, u32[]{:S(2)}, u32[]{:S(2)}) async-start(f32[64,32,128]{2,1,0:T(8,128)} %bitcast.31), calls=%async_computation | async-start | bytes 2097152 | tf_op jit(solution)/shard_map/all_to_all | solution.py:301
  52.6 12.1 %copy-start.3 = (f32[256,256]{1,0:T(8,128)S(1)}, f32[256,256]{1,0:T(8,128)}, u32[]{:S(2)}) copy-start(f32[256,256]{1,0:T(8,128)} %low_ref.5) | copy-start | bytes 786436
  52.6 12.1 %copy-start.4 = (f32[256,256]{1,0:T(8,128)S(1)}, f32[256,256]{1,0:T(8,128)}, u32[]{:S(2)}) copy-start(f32[256,256]{1,0:T(8,128)} %high_ref.5) | copy-start | bytes 786436
  53.8 7.1 %collective-permute-start.2 = (f32[256,256]{1,0:T(8,128)S(1)}, f32[256,256]{1,0:T(8,128)S(1)}, u32[]{:S(2)}, u32[]{:S(2)}) collective-permute-start(f32[256,256]{1,0:T(8,128)S(1)} %get-tuple-element.22), channel_id=1, source_target_pairs={{0,1},{1,2},{2,3},{3,4},{4,5},{5,6},{6,7},{7,8},{8,9},{9,10},{10,1... | collective-permute-start | bytes 786440 | tf_op jit(solution)/shard_map/ppermute | solution.py:274
  55.1 9.5 %collective-permute-start.3 = (f32[256,256]{1,0:T(8,128)S(1)}, f32[256,256]{1,0:T(8,128)S(1)}, u32[]{:S(2)}, u32[]{:S(2)}) collective-permute-start(f32[256,256]{1,0:T(8,128)S(1)} %get-tuple-element.23), channel_id=1, source_target_pairs={{1,0},{2,1},{3,2},{4,3},{5,4},{6,5},{7,6},{8,7},{9,8},{10,9},{11,1... | collective-permute-start | bytes 786440 | tf_op jit(solution)/shard_map/ppermute | solution.py:275
  56.4 2.2 %copy-start = (bf16[2,1024,1024]{2,1,0:T(8,128)(2,1)S(1)}, bf16[2,1024,1024]{2,1,0:T(8,128)(2,1)}, u32[]{:S(2)}) copy-start(bf16[2,1024,1024]{2,1,0:T(8,128)(2,1)} %get-tuple-element.21.d2_ref) | copy-start | bytes 12582916
  60.9 39.1 %copy-start.2 = (f32[1,1024,256]{2,1,0:T(8,128)S(1)}, f32[1,1024,256]{2,1,0:T(8,128)}, u32[]{:S(2)}) copy-start(f32[1,1024,256]{2,1,0:T(8,128)} %param.10) | copy-start | bytes 3145732
  82.7 34.8 %all-to-all-start.2 = ((f32[64,32,128]{2,1,0:T(8,128)}), f32[64,32,128]{2,1,0:T(8,128)S(1)}, u32[]{:S(2)}, u32[]{:S(2)}) async-start(f32[64,32,128]{2,1,0:T(8,128)} %bitcast.13), calls=%async_computation.2 | async-start | bytes 2097152 | tf_op jit(solution)/shard_map/all_to_all | solution.py:301
  88.9 6.8 %collective-permute-start.4 = (f32[256,256]{1,0:T(8,128)}, f32[256,256]{1,0:T(8,128)S(1)}, u32[]{:S(2)}, u32[]{:S(2)}) collective-permute-start(f32[256,256]{1,0:T(8,128)} %get-tuple-element.25), channel_id=1, source_target_pairs={{0,1},{1,2},{2,3},{3,4},{4,5},{5,6},{6,7},{7,8},{8,9},{9,10},{10,1... | collective-permute-start | bytes 786440 | tf_op jit(solution)/shard_map/ppermute | solution.py:274
  90.3 9.7 %collective-permute-start.5 = (f32[256,256]{1,0:T(8,128)}, f32[256,256]{1,0:T(8,128)S(1)}, u32[]{:S(2)}, u32[]{:S(2)}) collective-permute-start(f32[256,256]{1,0:T(8,128)} %get-tuple-element.26), channel_id=1, source_target_pairs={{1,0},{2,1},{3,2},{4,3},{5,4},{6,5},{7,6},{8,7},{9,8},{10,9},{11,1... | collective-permute-start | bytes 786440 | tf_op jit(solution)/shard_map/ppermute | solution.py:275
  100.0 2.2 %copy-start.1 = (bf16[2,1024,1024]{2,1,0:T(8,128)(2,1)S(1)}, bf16[2,1024,1024]{2,1,0:T(8,128)(2,1)}, u32[]{:S(2)}) copy-start(bf16[2,1024,1024]{2,1,0:T(8,128)(2,1)} %get-tuple-element.21.d2_ref) | copy-start | bytes 12582916
  102.2 0.9 copy-start.5
  103.1 1.2 %copy-start.6 = (f32[1024,256]{1,0:T(8,128)S(1)}, f32[1024,256]{1,0:T(8,128)}, u32[]{:S(2)}) copy-start(f32[1024,256]{1,0:T(8,128)} %get-tuple-element.24.u_ref) | copy-start | bytes 3145732

commit v6 on v5

--- a/solution.py
+++ b/solution.py
@@ -359,7 +359,7 @@
         ],
         [HBM] * 4,
         (0,),
-        60 * 1024 * 1024,
+        52 * 1024 * 1024,
     )
     held_u = spread(packed)
     u_before, u_after = exchange(first, last)

time: 120 us -> 120 us (level)
  Pallas kernels: 24.9 us -> 23.3 us
  waiting for transfers between devices: 43.7 us -> 45.3 us
    pallas_call x9, Pallas kernels: 22.5 us -> 20.9 us  [call(): pl.pallas_call(kernel, in_specs=[HBM if i in hbm else VMEM for i in range...]
    all_to_all x3, waiting for transfers between devices: 31.4 us -> 33 us  [spread(): lax.all_to_all(packed.reshape(pairs, share * nk, TW), 'pair', split_axis=...]
    unnamed x30 -> x28, local copies, waits for them, and re-layouts: 7.41 us -> 8 us
  transfers between devices with their start and end apart: 9 -> 9, of which waited for: 6 -> 6; matrix products, arithmetic and copies ran while one was open for 4% -> 3% of each run, Pallas kernels for 15% -> 14%
where the time goes in v6:
time: 120 us
  waiting for transfers between devices  45.3 us (38%)
  starting transfers between devices  37.6 us (31%)
  Pallas kernels  23.3 us (19%)
  local copies, waits for them, and re-layouts  11.7 us (10%)
  between operations  1.71 us (1%)
    all_to_all x3, waiting for transfers between devices, spread(): lax.all_to_all(packed.reshape(pairs, share * nk, TW), 'pair', split_axis=...  33 us
    all_to_all x3, starting transfers between devices, spread(): lax.all_to_all(packed.reshape(pairs, share * nk, TW), 'pair', split_axis=...  27.1 us
    pallas_call x9, Pallas kernels, call(): pl.pallas_call(kernel, in_specs=[HBM if i in hbm else VMEM for i in range...  20.9 us
    unnamed x28, local copies, waits for them, and re-layouts  8 us
    ppermute x3, waiting for transfers between devices, exchange(): after = lax.ppermute(first, 'virt', down)  7.77 us
    ppermute x3, starting transfers between devices, exchange(): before = lax.ppermute(last, 'virt', up)  6.61 us
    ppermute x3, waiting for transfers between devices, exchange(): before = lax.ppermute(last, 'virt', up)  4.53 us
    ppermute x3, starting transfers between devices, exchange(): after = lax.ppermute(first, 'virt', down)  3.86 us
  transfers between devices with their start and end apart: 9, of which 6 were waited for; matrix products, arithmetic and copies ran while one was open for 3% of the time, Pallas kernels for 14%

profile of v6, /device:TPU:1, one launch (start us, length us, event | category | flops | bytes accessed | tf_op | source)
XLA Modules:
  0.0 119.6 jit_solution(12380015327102330807)
XLA Ops:
  0.0 2.4 %pack.1 = f32[2048,128]{1,0:T(8,128)} custom-call(f32[1024,256]{1,0:T(8,128)} %bitcast.28), custom_call_target="tpu_custom_call" | custom-call | tf_op jit(solution)/shard_map/pack/pallas_call | solution.py:64
  2.4 14.6 %all-to-all-start.1 = ((f32[64,32,128]{2,1,0:T(8,128)}), f32[64,32,128]{2,1,0:T(8,128)S(1)}, u32[]{:S(2)}, u32[]{:S(2)}) async-start(f32[64,32,128]{2,1,0:T(8,128)} %bitcast.30), calls=%async_computation.1 | async-start | bytes 2097152 | tf_op jit(solution)/shard_map/all_to_all | solution.py:301
  17.0 0.0 copy-start.3
  17.0 0.0 copy-start.4
  17.0 0.8 slice_bitcast_fusion
  17.8 1.3 %collective-permute-start.1 = (f32[256,256]{1,0:T(8,128)}, f32[256,256]{1,0:T(8,128)S(1)}, u32[]{:S(2)}, u32[]{:S(2)}) collective-permute-start(f32[256,256]{1,0:T(8,128)} %get-tuple-element.27), channel_id=1, source_target_pairs={{1,0},{2,1},{3,2},{4,3},{5,4},{6,5},{7,6},{8,7},{9,8},{10,9},{11,1... | collective-permute-start | bytes 786440 | tf_op jit(solution)/shard_map/ppermute | solution.py:275
  19.1 4.0 %collective-permute-start = (f32[256,256]{1,0:T(8,128)S(1)}, f32[256,256]{1,0:T(8,128)S(1)}, u32[]{:S(2)}, u32[]{:S(2)}) collective-permute-start(f32[256,256]{1,0:T(8,128)S(1)} %get-tuple-element.28), channel_id=1, source_target_pairs={{0,1},{1,2},{2,3},{3,4},{4,5},{5,6},{6,7},{7,8},{8,9},{9,10},{10,1... | collective-permute-start | bytes 786440 | tf_op jit(solution)/shard_map/ppermute | solution.py:274
  23.1 0.0 copy-done.12
  23.1 0.6 fusion.1
  25.0 0.6 dynamic_slice.18
  25.6 0.7 dynamic_slice.15
  26.2 0.8 fusion
  27.0 6.6 %own.1 = (f32[1024,256]{1,0:T(8,128)}, bf16[2,1024,1024]{2,1,0:T(8,128)(2,1)}) custom-call(f32[1024,256]{1,0:T(8,128)} %bitcast.29, f32[1024,256]{1,0:T(8,128)} %bitcast.21, f32[1024,1024]{1,0:T(8,128)} %d_hbm.1), custom_call_target="tpu_custom_call" | custom-call | flops 1610612736 | bytes 11534336 | tf_op jit(solution)/shard_map/own/pallas_call | solution.py:258
  33.6 0.0 collective-permute-done.1.after_ref
  33.6 0.0 collective-permute-done.before_ref
  33.6 4.1 %ready.1 = (f32[1024,256]{1,0:T(8,128)}, f32[2048,128]{1,0:T(8,128)}, f32[256,256]{1,0:T(8,128)S(1)}, f32[256,256]{1,0:T(8,128)S(1)}) custom-call(f32[1024,256]{1,0:T(8,128)} %get-tuple-element.16.y_hbm, f32[256,256]{1,0:T(8,128)S(1)} %collective-permute-done.before_ref, f32[256,256]{1,0:T(8,128)S(1)} %collective-permute-done.1.after_ref, ...), custom_call_target="tpu_custom_call" | custom-call | flops 201326592 | bytes 4723716 | tf_op jit(solution)/shard_map/ready/pallas_call | solution.py:258
  37.8 0.7 copy-done.9
  38.5 0.7 copy-done.10
  39.2 6.4 %all-to-all-done.1 = f32[64,32,128]{2,1,0:T(8,128)S(1)} async-done(((f32[64,32,128]{2,1,0:T(8,128)}), f32[64,32,128]{2,1,0:T(8,128)S(1)}, u32[]{:S(2)}, u32[]{:S(2)}) %all-to-all-start.1) | async-done | bytes 1048608 | tf_op jit(solution)/shard_map/all_to_all | solution.py:301
  45.6 6.3 %all-to-all-start = ((f32[64,32,128]{2,1,0:T(8,128)}), f32[64,32,128]{2,1,0:T(8,128)S(1)}, u32[]{:S(2)}, u32[]{:S(2)}) async-start(f32[64,32,128]{2,1,0:T(8,128)} %bitcast.31), calls=%async_computation | async-start | bytes 2097152 | tf_op jit(solution)/shard_map/all_to_all | solution.py:301
  51.9 0.1 dynamic_slice.19
  52.0 0.1 broadcast_in_dim.29
  52.0 0.1 reshape.41.pair_ref
  52.1 0.1 reshape.40.col_ref
  52.2 0.3 prep.1
  52.6 0.0 copy-start.5
  52.6 1.1 ladder.1
  53.7 1.3 %collective-permute-start.2 = (f32[256,256]{1,0:T(8,128)S(1)}, f32[256,256]{1,0:T(8,128)S(1)}, u32[]{:S(2)}, u32[]{:S(2)}) collective-permute-start(f32[256,256]{1,0:T(8,128)S(1)} %get-tuple-element.22), channel_id=1, source_target_pairs={{0,1},{1,2},{2,3},{3,4},{4,5},{5,6},{6,7},{7,8},{8,9},{9,10},{10,1... | collective-permute-start | bytes 786440 | tf_op jit(solution)/shard_map/ppermute | solution.py:274
  55.0 1.3 %collective-permute-start.3 = (f32[256,256]{1,0:T(8,128)S(1)}, f32[256,256]{1,0:T(8,128)S(1)}, u32[]{:S(2)}, u32[]{:S(2)}) collective-permute-start(f32[256,256]{1,0:T(8,128)S(1)} %get-tuple-element.23), channel_id=1, source_target_pairs={{1,0},{2,1},{3,2},{4,3},{5,4},{6,5},{7,6},{8,7},{9,8},{10,9},{11,1... | collective-permute-start | bytes 786440 | tf_op jit(solution)/shard_map/ppermute | solution.py:275
  56.3 2.2 %copy-done = bf16[2,1024,1024]{2,1,0:T(8,128)(2,1)S(1)} copy-done((bf16[2,1024,1024]{2,1,0:T(8,128)(2,1)S(1)}, bf16[2,1024,1024]{2,1,0:T(8,128)(2,1)}, u32[]{:S(2)}) %copy-start) | copy-done | bytes 4194328
  58.5 2.2 %inner.1.t_ref = f32[256,1024]{1,0:T(8,128)S(1)} custom-call(f32[256,1024]{1,0:T(8,128)S(1)} %get-tuple-element.20.w_ref, bf16[2,1024,1024]{2,1,0:T(8,128)(2,1)S(1)} %copy-done, bf16[256,256]{1,0:T(8,128)(2,1)S(1)} %get-tuple-element.18.kh_ref, bf16[256,256]{1,0:T(8,128)(2,1)S(1)} %get-tuple-element.19.kl_ref), custom_call_target="tpu_custom_call" | custom-call | flops 2013265920 | bytes 6553600 | tf_op jit(solution)/shard_map/inner/pallas_call | solution.py:258
  60.7 0.0 copy-start.2
  60.7 0.0 collective-permute-done.2.before_ref
  60.7 3.8 %collective-permute-done.3.after_ref = f32[256,256]{1,0:T(8,128)S(1)} collective-permute-done((f32[256,256]{1,0:T(8,128)S(1)}, f32[256,256]{1,0:T(8,128)S(1)}, u32[]{:S(2)}, u32[]{:S(2)}) %collective-permute-start.3) | collective-permute-done | bytes 262176 | tf_op jit(solution)/shard_map/ppermute | solution.py:275
  64.5 0.4 outer.1.t_ref
  65.0 15.5 %all-to-all-done = f32[64,32,128]{2,1,0:T(8,128)S(1)} async-done(((f32[64,32,128]{2,1,0:T(8,128)}), f32[64,32,128]{2,1,0:T(8,128)S(1)}, u32[]{:S(2)}, u32[]{:S(2)}) %all-to-all-start) | async-done | bytes 1048608 | tf_op jit(solution)/shard_map/all_to_all | solution.py:301
  80.4 2.3 %join.1 = f32[2048,128]{1,0:T(8,128)} custom-call(f32[2048,128]{1,0:T(8,128)S(1)} %bitcast.18, f32[256,1024]{1,0:T(8,128)S(1)} %outer.1.t_ref, f32[64,64]{1,0:T(8,128)S(1)} %copy-done.8), custom_call_target="tpu_custom_call" | custom-call | flops 402653184 | bytes 3162112 | tf_op jit(solution)/shard_map/join/pallas_call | solution.py:258
  82.7 6.2 %all-to-all-start.2 = ((f32[64,32,128]{2,1,0:T(8,128)}), f32[64,32,128]{2,1,0:T(8,128)S(1)}, u32[]{:S(2)}, u32[]{:S(2)}) async-start(f32[64,32,128]{2,1,0:T(8,128)} %bitcast.13), calls=%async_computation.2 | async-start | bytes 2097152 | tf_op jit(solution)/shard_map/all_to_all | solution.py:301
  88.9 1.3 %collective-permute-start.4 = (f32[256,256]{1,0:T(8,128)}, f32[256,256]{1,0:T(8,128)S(1)}, u32[]{:S(2)}, u32[]{:S(2)}) collective-permute-start(f32[256,256]{1,0:T(8,128)} %copy-done.10), channel_id=1, source_target_pairs={{0,1},{1,2},{2,3},{3,4},{4,5},{5,6},{6,7},{7,8},{8,9},{9,10},{10,1... | collective-permute-start | bytes 786440 | tf_op jit(solution)/shard_map/ppermute | solution.py:274
  90.2 1.3 %collective-permute-start.5 = (f32[256,256]{1,0:T(8,128)}, f32[256,256]{1,0:T(8,128)S(1)}, u32[]{:S(2)}, u32[]{:S(2)}) collective-permute-start(f32[256,256]{1,0:T(8,128)} %copy-done.9), channel_id=1, source_target_pairs={{1,0},{2,1},{3,2},{4,3},{5,4},{6,5},{7,6},{8,7},{9,8},{10,9},{11,1... | collective-permute-start | bytes 786440 | tf_op jit(solution)/shard_map/ppermute | solution.py:275
  91.5 4.5 %collective-permute-done.4.before_ref = f32[256,256]{1,0:T(8,128)S(1)} collective-permute-done((f32[256,256]{1,0:T(8,128)}, f32[256,256]{1,0:T(8,128)S(1)}, u32[]{:S(2)}, u32[]{:S(2)}) %collective-permute-start.4) | collective-permute-done | bytes 262176 | tf_op jit(solution)/shard_map/ppermute | solution.py:274
  96.0 3.9 %collective-permute-done.5.after_ref = f32[256,256]{1,0:T(8,128)S(1)} collective-permute-done((f32[256,256]{1,0:T(8,128)}, f32[256,256]{1,0:T(8,128)S(1)}, u32[]{:S(2)}, u32[]{:S(2)}) %collective-permute-start.5) | collective-permute-done | bytes 262176 | tf_op jit(solution)/shard_map/ppermute | solution.py:275
  100.0 2.2 %copy-done.1 = bf16[2,1024,1024]{2,1,0:T(8,128)(2,1)S(1)} copy-done((bf16[2,1024,1024]{2,1,0:T(8,128)(2,1)S(1)}, bf16[2,1024,1024]{2,1,0:T(8,128)(2,1)}, u32[]{:S(2)}) %copy-start.1) | copy-done | bytes 4194328
  102.2 0.9 copy-done.6
  103.1 1.2 %copy-done.7 = f32[1024,256]{1,0:T(8,128)S(1)} copy-done((f32[1024,256]{1,0:T(8,128)S(1)}, f32[1024,256]{1,0:T(8,128)}, u32[]{:S(2)}) %copy-start.7) | copy-done | bytes 1048600
  104.4 2.0 %again.1.t_ref = f32[1024,256]{1,0:T(8,128)S(1)} custom-call(f32[1024,256]{1,0:T(8,128)S(1)} %copy-done.7, f32[1024,256]{1,0:T(8,128)S(1)} %bitcast.22, f32[256,256]{1,0:T(8,128)S(1)} %collective-permute-done.4.before_ref, f32[256,256]{1,0:T(8,128)S(1)} %collective-permute-done.5.after_ref, f32[256,256]{1,0:T(8,128)S(1)} %copy-done.3, ...), custom_call_target="tpu_custom_call" | custom-call | flops 1610612736 | bytes 8388608 | tf_op jit(solution)/shard_map/again/pallas_call | solution.py:258
  106.4 11.1 %all-to-all-done.2 = f32[64,32,128]{2,1,0:T(8,128)S(1)} async-done(((f32[64,32,128]{2,1,0:T(8,128)}), f32[64,32,128]{2,1,0:T(8,128)S(1)}, u32[]{:S(2)}, u32[]{:S(2)}) %all-to-all-start.2) | async-done | bytes 1048608 | tf_op jit(solution)/shard_map/all_to_all | solution.py:301
  117.5 2.0 %last.1 = f32[1024,256]{1,0:T(8,128)} custom-call(f32[2048,128]{1,0:T(8,128)S(1)} %bitcast.19, f32[1024,256]{1,0:T(8,128)S(1)} %again.1.t_ref, f32[1,1024]{1,0:T(1,128)S(1)} %bitcast.25, f32[1,256]{1,0:T(1,128)S(1)} %bitcast.27, f32[1,1]{1,0:T(1,128)} %bitcast.8.pair_ref), custom_call_target="tpu_custom_call" | custom-call | flops 2621440 | bytes 3150852 | tf_op jit(solution)/shard_map/last/pallas_call | solution.py:258
  (19 shorter events, 0.0 us)
Async XLA Ops:
  0.0 17.0 %copy-start.11 = (f32[1,1024,256]{2,1,0:T(8,128)S(1)}, f32[1,1024,256]{2,1,0:T(8,128)}, u32[]{:S(2)}) copy-start(f32[1,1024,256]{2,1,0:T(8,128)} %param.9) | copy-start | bytes 3145732
  0.0 23.1 %copy-start.12 = (s32[2]{0:T(128)S(1)}, s32[2]{0:T(128)}, u32[]{:S(2)}) copy-start(s32[2]{0:T(128)} %param.17) | copy-start | bytes 28
  0.0 24.9 %copy-start.13 = (f32[64]{0:T(128)S(1)}, f32[64]{0:T(128)}, u32[]{:S(2)}) copy-start(f32[64]{0:T(128)} %param.15) | copy-start | bytes 772
  2.4 43.2 %all-to-all-start.1 = ((f32[64,32,128]{2,1,0:T(8,128)}), f32[64,32,128]{2,1,0:T(8,128)S(1)}, u32[]{:S(2)}, u32[]{:S(2)}) async-start(f32[64,32,128]{2,1,0:T(8,128)} %bitcast.30), calls=%async_computation.1 | async-start | bytes 2097152 | tf_op jit(solution)/shard_map/all_to_all | solution.py:301
  17.0 16.6 %copy-start.3 = (f32[256,256]{1,0:T(8,128)S(1)}, f32[256,256]{1,0:T(8,128)}, u32[]{:S(2)}) copy-start(f32[256,256]{1,0:T(8,128)} %low_ref.5) | copy-start | bytes 786436
  17.0 16.6 %copy-start.4 = (f32[256,256]{1,0:T(8,128)S(1)}, f32[256,256]{1,0:T(8,128)}, u32[]{:S(2)}) copy-start(f32[256,256]{1,0:T(8,128)} %high_ref.5) | copy-start | bytes 786436
  17.8 15.8 %collective-permute-start.1 = (f32[256,256]{1,0:T(8,128)}, f32[256,256]{1,0:T(8,128)S(1)}, u32[]{:S(2)}, u32[]{:S(2)}) collective-permute-start(f32[256,256]{1,0:T(8,128)} %get-tuple-element.27), channel_id=1, source_target_pairs={{1,0},{2,1},{3,2},{4,3},{5,4},{6,5},{7,6},{8,7},{9,8},{10,9},{11,1... | collective-permute-start | bytes 786440 | tf_op jit(solution)/shard_map/ppermute | solution.py:275
  19.1 14.5 %collective-permute-start = (f32[256,256]{1,0:T(8,128)S(1)}, f32[256,256]{1,0:T(8,128)S(1)}, u32[]{:S(2)}, u32[]{:S(2)}) collective-permute-start(f32[256,256]{1,0:T(8,128)S(1)} %get-tuple-element.28), channel_id=1, source_target_pairs={{0,1},{1,2},{2,3},{3,4},{4,5},{5,6},{6,7},{7,8},{8,9},{9,10},{10,1... | collective-permute-start | bytes 786440 | tf_op jit(solution)/shard_map/ppermute | solution.py:274
  27.0 25.2 %copy-start.8 = (f32[64,64]{1,0:T(8,128)S(1)}, f32[64,64]{1,0:T(8,128)}, u32[]{:S(2)}) copy-start(f32[64,64]{1,0:T(8,128)} %l_ref.3) | copy-start | bytes 49156
  37.8 0.7 copy-start.9
  38.5 0.7 copy-start.10
  45.6 34.9 %all-to-all-start = ((f32[64,32,128]{2,1,0:T(8,128)}), f32[64,32,128]{2,1,0:T(8,128)S(1)}, u32[]{:S(2)}, u32[]{:S(2)}) async-start(f32[64,32,128]{2,1,0:T(8,128)} %bitcast.31), calls=%async_computation | async-start | bytes 2097152 | tf_op jit(solution)/shard_map/all_to_all | solution.py:301
  52.6 11.9 %copy-start.5 = (f32[256,256]{1,0:T(8,128)S(1)}, f32[256,256]{1,0:T(8,128)}, u32[]{:S(2)}) copy-start(f32[256,256]{1,0:T(8,128)} %high_ref.5) | copy-start | bytes 786436
  53.7 7.0 %collective-permute-start.2 = (f32[256,256]{1,0:T(8,128)S(1)}, f32[256,256]{1,0:T(8,128)S(1)}, u32[]{:S(2)}, u32[]{:S(2)}) collective-permute-start(f32[256,256]{1,0:T(8,128)S(1)} %get-tuple-element.22), channel_id=1, source_target_pairs={{0,1},{1,2},{2,3},{3,4},{4,5},{5,6},{6,7},{7,8},{8,9},{9,10},{10,1... | collective-permute-start | bytes 786440 | tf_op jit(solution)/shard_map/ppermute | solution.py:274
  55.0 9.6 %collective-permute-start.3 = (f32[256,256]{1,0:T(8,128)S(1)}, f32[256,256]{1,0:T(8,128)S(1)}, u32[]{:S(2)}, u32[]{:S(2)}) collective-permute-start(f32[256,256]{1,0:T(8,128)S(1)} %get-tuple-element.23), channel_id=1, source_target_pairs={{1,0},{2,1},{3,2},{4,3},{5,4},{6,5},{7,6},{8,7},{9,8},{10,9},{11,1... | collective-permute-start | bytes 786440 | tf_op jit(solution)/shard_map/ppermute | solution.py:275
  56.3 2.2 %copy-start = (bf16[2,1024,1024]{2,1,0:T(8,128)(2,1)S(1)}, bf16[2,1024,1024]{2,1,0:T(8,128)(2,1)}, u32[]{:S(2)}) copy-start(bf16[2,1024,1024]{2,1,0:T(8,128)(2,1)} %get-tuple-element.21.d2_ref) | copy-start | bytes 12582916
  60.7 39.3 %copy-start.2 = (f32[1,1024,256]{2,1,0:T(8,128)S(1)}, f32[1,1024,256]{2,1,0:T(8,128)}, u32[]{:S(2)}) copy-start(f32[1,1024,256]{2,1,0:T(8,128)} %param.10) | copy-start | bytes 3145732
  82.7 34.8 %all-to-all-start.2 = ((f32[64,32,128]{2,1,0:T(8,128)}), f32[64,32,128]{2,1,0:T(8,128)S(1)}, u32[]{:S(2)}, u32[]{:S(2)}) async-start(f32[64,32,128]{2,1,0:T(8,128)} %bitcast.13), calls=%async_computation.2 | async-start | bytes 2097152 | tf_op jit(solution)/shard_map/all_to_all | solution.py:301
  88.9 7.1 %collective-permute-start.4 = (f32[256,256]{1,0:T(8,128)}, f32[256,256]{1,0:T(8,128)S(1)}, u32[]{:S(2)}, u32[]{:S(2)}) collective-permute-start(f32[256,256]{1,0:T(8,128)} %copy-done.10), channel_id=1, source_target_pairs={{0,1},{1,2},{2,3},{3,4},{4,5},{5,6},{6,7},{7,8},{8,9},{9,10},{10,1... | collective-permute-start | bytes 786440 | tf_op jit(solution)/shard_map/ppermute | solution.py:274
  90.2 9.8 %collective-permute-start.5 = (f32[256,256]{1,0:T(8,128)}, f32[256,256]{1,0:T(8,128)S(1)}, u32[]{:S(2)}, u32[]{:S(2)}) collective-permute-start(f32[256,256]{1,0:T(8,128)} %copy-done.9), channel_id=1, source_target_pairs={{1,0},{2,1},{3,2},{4,3},{5,4},{6,5},{7,6},{8,7},{9,8},{10,9},{11,1... | collective-permute-start | bytes 786440 | tf_op jit(solution)/shard_map/ppermute | solution.py:275
  100.0 2.2 %copy-start.1 = (bf16[2,1024,1024]{2,1,0:T(8,128)(2,1)S(1)}, bf16[2,1024,1024]{2,1,0:T(8,128)(2,1)}, u32[]{:S(2)}) copy-start(bf16[2,1024,1024]{2,1,0:T(8,128)(2,1)} %get-tuple-element.21.d2_ref) | copy-start | bytes 12582916
  102.2 0.9 copy-start.6
  103.1 1.2 %copy-start.7 = (f32[1024,256]{1,0:T(8,128)S(1)}, f32[1024,256]{1,0:T(8,128)}, u32[]{:S(2)}) copy-start(f32[1024,256]{1,0:T(8,128)} %get-tuple-element.24.u_ref) | copy-start | bytes 3145732
